TPU v7x, 32 devices: a whole 2x2x4 slice. The times are simulated.
32 devices in a mesh: seq: 16 (over z, y, core), head: 2 (over x).
Axes of the slice: x: 2, y: 2, z: 4, core: 2. Of those that a mesh axis runs over, the one named last changes fastest.
Arguments:
- queries: bfloat16 [2048, 8192], P('seq', 'head'), may hold values from -48 to 48
- keyval: bfloat16 [2048, 2048], P('seq', 'head'), may hold values from -48 to 48
- grad_out: bfloat16 [2048, 8192], P('seq', 'head'), may hold values from -6 to 6
- doc_ids: int32 [2048], P('seq'), may hold values from 0 to 3, never falling along the last dimension, each value on 1 to 1024 neighbouring positions
- deltas: bfloat16 [2, 2048, 8192], P('head', 'seq'), may hold values from -6 to 6
- node_weights: bfloat16 [8192, 2048], P('head', 'seq'), may hold values from -0.0625 to 0.0625
- layer_slot: int32 [2], replicated, may hold values from 0 to 1, each once
Outputs:
- grad_query: bfloat16 [2048, 8192], P('seq', 'head')
- grad_keyval: bfloat16 [2048, 2048], P('seq', 'head')
- scores: float32 [2, 16], replicated
Inputs may be any that keep to these rules, and one draw needn't show every extreme that they name: `layer_slot`: each of the 2 layers stands in exactly one slot. `doc_ids`: never falling along the sequence.
All inputs are finite; a program needn't handle non-finite values.
Results may differ from a plain program's by a relative error of at most 0.013.
Values may be sent and summed in bfloat16 or wider, within the bound.
No kernel may reach another device: no remote copies, remote signals or barrier semaphores. Data moves between devices by JAX's collectives and lax.ppermute only.
A program may use at most 128 MiB of HBM per device.

v0:
```python
import math

import jax
import jax.numpy as jnp
from jax import lax
from jax.sharding import PartitionSpec as P

H = 64
KVH = 8
HD = 128


def over_blocks(step, carry, pieces):
    total_rows = pieces[0].shape[0]
    block_rows = 512

    def one_turn(turn_index, running):
        offset = turn_index * block_rows
        blocks = tuple((lax.dynamic_slice_in_dim(piece, offset, block_rows, 0) for piece in pieces))
        return step(running, *blocks, offset)

    return lax.fori_loop(0, total_rows // block_rows, one_turn, carry)


def on_device(queries, keyval, grad_out, doc_ids, deltas, node_weights, layer_slot):
    tok_rows = queries.shape[0]
    kv_local = keyval.shape[1] // (2 * HD)
    group_size = H // KVH
    score_scale = 1.0 / math.sqrt(HD)
    seq_total = tok_rows * lax.axis_size("seq")
    query_grid = queries.reshape(tok_rows, kv_local, group_size, HD)
    out_grid = grad_out.reshape(tok_rows, kv_local, group_size, HD)
    row_positions = lax.axis_index("seq") * tok_rows + jnp.arange(tok_rows, dtype=jnp.int32)

    def block_logits(kv_rows, key_ids, key_start):
        width = kv_rows.shape[0]
        kv_grid = kv_rows.reshape(width, kv_local, 2, HD)
        logits = (
            jnp.einsum(
                "tgie,rge->gitr", query_grid, kv_grid[:, :, 0], preferred_element_type=jnp.float32
            )
            * score_scale
        )
        key_positions = key_start + jnp.arange(width, dtype=jnp.int32)
        allowed = (key_ids[None, :] == doc_ids[:, None]) & (
            key_positions[None, :] <= row_positions[:, None]
        )
        return (logits, allowed, kv_grid)

    def forward_step(carry, kv_rows, key_ids, key_start):
        run_max, run_sum, accum = carry
        logits, allowed, kv_grid = block_logits(kv_rows, key_ids, key_start)
        new_max = jnp.maximum(run_max, jnp.max(jnp.where(allowed, logits, -1e30), axis=3))
        weights = jnp.where(allowed, jnp.exp(logits - new_max[..., None]), 0.0)
        factor = jnp.exp(run_max - new_max)
        run_sum = run_sum * factor + jnp.sum(weights, axis=3)
        values = kv_grid[:, :, 1].astype(jnp.float32)
        accum = accum * factor[..., None] + jnp.einsum(
            "gitr,rge->gite", weights, values, precision=lax.Precision.HIGHEST
        )
        return (new_max, run_sum, accum)

    stat_shape = (kv_local, group_size, tok_rows)
    forward_init = (
        jnp.full(stat_shape, -1e30, jnp.float32),
        jnp.zeros(stat_shape, jnp.float32),
        jnp.zeros(stat_shape + (HD,), jnp.float32),
    )
    run_max, run_sum, accum = over_blocks(
        forward_step,
        forward_init,
        (
            lax.all_gather(keyval, "seq", axis=0, tiled=True),
            lax.all_gather(doc_ids, "seq", axis=0, tiled=True),
        ),
    )
    log_total = run_max + jnp.log(run_sum)
    attn_out = accum / run_sum[..., None]
    row_dot = jnp.einsum(
        "tgie,gite->git", out_grid.astype(jnp.float32), attn_out, precision=lax.Precision.HIGHEST
    )

    def backward_step(carry, kv_rows, key_ids, key_start):
        query_accum = carry[0]
        width = kv_rows.shape[0]
        logits, allowed, kv_grid = block_logits(kv_rows, key_ids, key_start)
        probs = jnp.where(allowed, jnp.exp(logits - log_total[..., None]), 0.0)
        grad_probs = jnp.einsum(
            "tgie,rge->gitr", out_grid, kv_grid[:, :, 1], preferred_element_type=jnp.float32
        )
        grad_logits = (probs * (grad_probs - row_dot[..., None])).astype(jnp.bfloat16)
        query_accum = (
            query_accum
            + jnp.einsum(
                "gitr,rge->gite", grad_logits, kv_grid[:, :, 0], preferred_element_type=jnp.float32
            )
            * score_scale
        )
        probs_low = probs.astype(jnp.bfloat16)
        grad_keys = (
            jnp.einsum(
                "gitr,tgie->rge", grad_logits, query_grid, preferred_element_type=jnp.float32
            )
            * score_scale
        )
        grad_values = jnp.einsum(
            "gitr,tgie->rge", probs_low, out_grid, preferred_element_type=jnp.float32
        )
        block_grad = jnp.stack((grad_keys, grad_values), axis=2).reshape(width, kv_local * 2 * HD)
        kv_buffer = lax.dynamic_update_slice(
            carry[1], block_grad, (key_start, jnp.zeros((), jnp.int32))
        )
        return (query_accum, kv_buffer)

    query_zero = jnp.zeros(stat_shape + (HD,), jnp.float32)
    backward_init = (query_zero, jnp.zeros((seq_total, kv_local * 2 * HD), jnp.float32))
    backward_out = over_blocks(
        backward_step,
        backward_init,
        (
            lax.all_gather(keyval, "seq", axis=0, tiled=True),
            lax.all_gather(doc_ids, "seq", axis=0, tiled=True),
        ),
    )
    query_accum = backward_out[0]
    grad_query = (
        jnp.transpose(query_accum, (2, 0, 1, 3))
        .reshape(tok_rows, kv_local * group_size * HD)
        .astype(jnp.bfloat16)
    )
    grad_keyval = lax.psum_scatter(
        backward_out[1].astype(jnp.bfloat16), "seq", scatter_dimension=0, tiled=True
    )
    width_deltas = lax.all_to_all(deltas, "head", split_axis=2, concat_axis=0, tiled=True)
    grad_rows = lax.all_gather(grad_keyval, "head", axis=1, tiled=True)
    layer_count = width_deltas.shape[0]
    node_count = grad_rows.shape[1] // HD
    projected = jnp.einsum(
        "ltd,dc->ltc",
        width_deltas,
        lax.all_gather(node_weights, "seq", axis=1, tiled=True),
        preferred_element_type=jnp.float32,
    )
    grad_cols = grad_rows.astype(jnp.float32)
    per_column = jnp.sum(projected * grad_cols[None], axis=1)
    partial_value = jnp.sum(per_column.reshape(layer_count, node_count, HD), axis=2)
    totals = lax.psum(partial_value / math.sqrt(seq_total), ("seq", "head"))
    placing = (layer_slot[:, None] == jnp.arange(layer_count, dtype=jnp.int32)[None, :]).astype(
        jnp.float32
    )
    scores = jnp.dot(placing.T, totals, precision=lax.Precision.HIGHEST)
    return (grad_query, grad_keyval, scores)


def solution(mesh):
    return jax.shard_map(
        on_device,
        mesh=mesh,
        in_specs=(
            P("seq", "head"),
            P("seq", "head"),
            P("seq", "head"),
            P("seq"),
            P("head", "seq", None),
            P("head", "seq"),
            P(),
        ),
        out_specs=(P("seq", "head"), P("seq", "head"), P()),
        check_vma=False,
    )
```

profile of v0, /device:TPU:0, one launch (start us, length us, event | category | flops | bytes accessed | tf_op | source)
XLA Modules:
  0.0 495.3 jit_solution(12276462753868386483)
XLA Ops:
  12.8 23.1 %all-gather = s32[16,1,128]{2,1,0:T(1,128)S(1)} all-gather(s32[1,1,128]{2,1,0:T(1,128)S(1)} %bitcast.193), channel_id=1, replica_groups=mesh['seq'=16,'head'=2] {'seq'}, dimensions={0}, use_global_device_ids=true | all-gather | bytes 8704 | tf_op jit(solution)/shard_map/all_gather | solution.py:122
  35.9 30.6 %all-gather.4.cloned.1.call-done = bf16[2048,1024]{0,1:T(8,128)(2,1)} async-done(((bf16[128,1024]{0,1:T(8,128)(2,1)}), bf16[2048,1024]{0,1:T(8,128)(2,1)}) %all-gather.4.cloned.1.call-update) | async-done | bytes 4194320 | tf_op jit(solution)/shard_map/all_gather | solution.py:121
  66.5 86.9 %while.34 = (s32[]{:T(128)}, f32[4,8,128]{2,1,0:T(8,128)S(1)}, f32[4,8,128]{2,1,0:T(8,128)S(1)}, f32[4,8,128,128]{3,2,1,0:T(8,128)}, s32[2048]{0:T(1024)S(1)}, /...) while((s32[]{:T(128)}, f32[4,8,128]{2,1,0:T(8,128)S(1)}, ...), condition=%wide.region_3.4_spmd.clone, body=%wide.region_0.3_spmd.clone.sunk | while | flops 3780858368 | bytes 67645152 | solution.py:22
  72.8 5.3 %fusion.80 = f32[4,8,128]{2,1,0:T(8,128)S(1)} fusion(f32[4,512,128,8]{2,1,3,0:T(8,128)} %get-tuple-element.617, f32[4,8,128]{2,1,0:T(8,128)S(1)} %select_maximum_fusion.2, pred[128,512]{0,1:T(8,128)(4,1)S(1)} %compare_and_fusion.4), kind=kLoop, calls=%fused_computation.8.clone.1 | loop fusion | flops 8384512 | bytes 8486912 | tf_op jit(solution)/shard_map/while/body/eval_jaxpr/reduce_sum | solution.py:56
  78.5 8.8 %fusion.82 = f32[4,8,128,128]{3,2,1,0:T(8,128)} fusion(f32[4,8,128,128]{3,2,1,0:T(8,128)} %get-tuple-element.647, f32[4,512,128,8]{2,1,3,0:T(8,128)S(1)} %copy-done, f32[4,8,128]{2,1,0:T(8,128)S(1)} %select_maximum_fusion.2, pred[128,512]{0,1:T(8,128)(4,1)S(1)} %compare_and_fusion.4, f32[4,8,128]{2,1,0:T(8,128)S(1)} %get-tuple-element.619, ...), kind=kOutput, calls=%fused_computation.14.clone.1 | convolution fusion | flops 3229089792 | bytes 13205505 | tf_op jit(solution)/shard_map/while/body/eval_jaxpr/gitr,rge->gite/dot_general | solution.py:58
  93.6 5.3 %fusion.80 = f32[4,8,128]{2,1,0:T(8,128)S(1)} fusion(f32[4,512,128,8]{2,1,3,0:T(8,128)} %get-tuple-element.617, f32[4,8,128]{2,1,0:T(8,128)S(1)} %select_maximum_fusion.2, pred[128,512]{0,1:T(8,128)(4,1)S(1)} %compare_and_fusion.4), kind=kLoop, calls=%fused_computation.8.clone.1 | loop fusion | flops 8384512 | bytes 8486912 | tf_op jit(solution)/shard_map/while/body/eval_jaxpr/reduce_sum | solution.py:56
  99.3 10.0 %fusion.82 = f32[4,8,128,128]{3,2,1,0:T(8,128)} fusion(f32[4,8,128,128]{3,2,1,0:T(8,128)} %get-tuple-element.647, f32[4,512,128,8]{2,1,3,0:T(8,128)S(1)} %copy-done, f32[4,8,128]{2,1,0:T(8,128)S(1)} %select_maximum_fusion.2, pred[128,512]{0,1:T(8,128)(4,1)S(1)} %compare_and_fusion.4, f32[4,8,128]{2,1,0:T(8,128)S(1)} %get-tuple-element.619, ...), kind=kOutput, calls=%fused_computation.14.clone.1 | convolution fusion | flops 3229089792 | bytes 13205505 | tf_op jit(solution)/shard_map/while/body/eval_jaxpr/gitr,rge->gite/dot_general | solution.py:58
  110.9 4.7 fusion.79
  115.6 5.3 %fusion.80 = f32[4,8,128]{2,1,0:T(8,128)S(1)} fusion(f32[4,512,128,8]{2,1,3,0:T(8,128)} %get-tuple-element.617, f32[4,8,128]{2,1,0:T(8,128)S(1)} %select_maximum_fusion.2, pred[128,512]{0,1:T(8,128)(4,1)S(1)} %compare_and_fusion.4), kind=kLoop, calls=%fused_computation.8.clone.1 | loop fusion | flops 8384512 | bytes 8486912 | tf_op jit(solution)/shard_map/while/body/eval_jaxpr/reduce_sum | solution.py:56
  121.3 10.0 %fusion.82 = f32[4,8,128,128]{3,2,1,0:T(8,128)} fusion(f32[4,8,128,128]{3,2,1,0:T(8,128)} %get-tuple-element.647, f32[4,512,128,8]{2,1,3,0:T(8,128)S(1)} %copy-done, f32[4,8,128]{2,1,0:T(8,128)S(1)} %select_maximum_fusion.2, pred[128,512]{0,1:T(8,128)(4,1)S(1)} %compare_and_fusion.4, f32[4,8,128]{2,1,0:T(8,128)S(1)} %get-tuple-element.619, ...), kind=kOutput, calls=%fused_computation.14.clone.1 | convolution fusion | flops 3229089792 | bytes 13205505 | tf_op jit(solution)/shard_map/while/body/eval_jaxpr/gitr,rge->gite/dot_general | solution.py:58
  137.6 5.3 %fusion.80 = f32[4,8,128]{2,1,0:T(8,128)S(1)} fusion(f32[4,512,128,8]{2,1,3,0:T(8,128)} %get-tuple-element.617, f32[4,8,128]{2,1,0:T(8,128)S(1)} %select_maximum_fusion.2, pred[128,512]{0,1:T(8,128)(4,1)S(1)} %compare_and_fusion.4), kind=kLoop, calls=%fused_computation.8.clone.1 | loop fusion | flops 8384512 | bytes 8486912 | tf_op jit(solution)/shard_map/while/body/eval_jaxpr/reduce_sum | solution.py:56
  143.4 10.0 %fusion.82 = f32[4,8,128,128]{3,2,1,0:T(8,128)} fusion(f32[4,8,128,128]{3,2,1,0:T(8,128)} %get-tuple-element.647, f32[4,512,128,8]{2,1,3,0:T(8,128)S(1)} %copy-done, f32[4,8,128]{2,1,0:T(8,128)S(1)} %select_maximum_fusion.2, pred[128,512]{0,1:T(8,128)(4,1)S(1)} %compare_and_fusion.4, f32[4,8,128]{2,1,0:T(8,128)S(1)} %get-tuple-element.619, ...), kind=kOutput, calls=%fused_computation.14.clone.1 | convolution fusion | flops 3229089792 | bytes 13205505 | tf_op jit(solution)/shard_map/while/body/eval_jaxpr/gitr,rge->gite/dot_general | solution.py:58
  162.3 74.5 %while.35 = (s32[]{:T(128)}, f32[4,8,128,128]{3,2,1,0:T(8,128)}, bf16[2048,1024]{1,0:T(8,128)(2,1)}, s32[2048]{0:T(1024)S(1)}, s32[128]{0:T(128)S(1)}, /*index=5...) while((s32[]{:T(128)}, f32[4,8,128,128]{3,2,1,0:T(8,128)}, ...), condition=%wide.region_5.6_spmd.clone, body=%wide.region_4.5_spmd.clone.sunk | while | flops 2708144640 | bytes 88862544 | solution.py:22
  175.1 5.3 %select_add_fusion.2 = f32[4,8,128,128]{3,2,1,0:T(8,128)} fusion(f32[4,8,128,128]{3,2,1,0:T(8,128)} %get-tuple-element.686, bf16[4,8,128,512]{2,3,1,0:T(8,128)(2,1)} %copy-done.1, pred[]{:T(512)S(6)} %compare.7, bf16[512,4,2,128]{0,3,2,1:T(8,128)(2,1)S(1)} %bitcast.179), kind=kOutput, calls=%fused_computation.38.clone.1 | convolution fusion | flops 538443776 | bytes 8912897 | tf_op jit(solution)/shard_map/while/body/eval_jaxpr/gitr,rge->gite/dot_general | solution.py:94
  193.2 6.0 %select_add_fusion.2 = f32[4,8,128,128]{3,2,1,0:T(8,128)} fusion(f32[4,8,128,128]{3,2,1,0:T(8,128)} %get-tuple-element.686, bf16[4,8,128,512]{2,3,1,0:T(8,128)(2,1)} %copy-done.1, pred[]{:T(512)S(6)} %compare.7, bf16[512,4,2,128]{0,3,2,1:T(8,128)(2,1)S(1)} %bitcast.179), kind=kOutput, calls=%fused_computation.38.clone.1 | convolution fusion | flops 538443776 | bytes 8912897 | tf_op jit(solution)/shard_map/while/body/eval_jaxpr/gitr,rge->gite/dot_general | solution.py:94
  212.0 6.0 %select_add_fusion.2 = f32[4,8,128,128]{3,2,1,0:T(8,128)} fusion(f32[4,8,128,128]{3,2,1,0:T(8,128)} %get-tuple-element.686, bf16[4,8,128,512]{2,3,1,0:T(8,128)(2,1)} %copy-done.1, pred[]{:T(512)S(6)} %compare.7, bf16[512,4,2,128]{0,3,2,1:T(8,128)(2,1)S(1)} %bitcast.179), kind=kOutput, calls=%fused_computation.38.clone.1 | convolution fusion | flops 538443776 | bytes 8912897 | tf_op jit(solution)/shard_map/while/body/eval_jaxpr/gitr,rge->gite/dot_general | solution.py:94
  230.8 6.0 %select_add_fusion.2 = f32[4,8,128,128]{3,2,1,0:T(8,128)} fusion(f32[4,8,128,128]{3,2,1,0:T(8,128)} %get-tuple-element.686, bf16[4,8,128,512]{2,3,1,0:T(8,128)(2,1)} %copy-done.1, pred[]{:T(512)S(6)} %compare.7, bf16[512,4,2,128]{0,3,2,1:T(8,128)(2,1)S(1)} %bitcast.179), kind=kOutput, calls=%fused_computation.38.clone.1 | convolution fusion | flops 538443776 | bytes 8912897 | tf_op jit(solution)/shard_map/while/body/eval_jaxpr/gitr,rge->gite/dot_general | solution.py:94
  238.4 6.9 %copy.75 = bf16[1,128,8192]{1,0,2:T(2,128)(2,1)} copy(bf16[1,128,8192]{2,1,0:T(8,128)(2,1)S(1)} %copy-done.7) | data formatting | bytes 4194304 | tf_op args[4]
  245.8 45.2 %reduce.2 = bf16[8192,128]{1,0:T(8,128)(2,1)S(1)} reduce(bf16[8192,1,128]{2,1,0:T(2,128)(2,1)} %bitcast.185, bf16[]{:T(256)} %broadcast.111), dimensions={1}, to_apply=%bitcast.116.reduce_sub_computation | reduce | bytes 4194306
  292.6 29.3 %all_to_all.18 = bf16[2,2,262144]{2,1,0:T(2,128)(2,1)S(1)} all-to-all(bf16[2,2,262144]{2,1,0:T(2,128)(2,1)} %reshape.77), channel_id=1, replica_groups=mesh['seq'=16,'head'=2] {'head'}, dimensions={0} | all-to-all | bytes 4194304 | tf_op jit(solution)/shard_map/all_to_all | solution.py:134
  333.9 8.7 %all_gather.17 = bf16[128,2048]{1,0:T(8,128)(2,1)S(1)} all-gather(bf16[128,1024]{1,0:T(8,128)(2,1)} %reduce-scatter.2.cloned.1.call-done), channel_id=1, replica_groups=mesh['seq'=16,'head'=2] {'head'}, dimensions={1}, use_global_device_ids=true | all-gather | bytes 786432 | tf_op jit(solution)/shard_map/all_gather | solution.py:135
  343.6 95.8 %all-gather.6.cloned.1.call-done = bf16[4096,2048]{1,0:T(8,128)(2,1)} async-done(((bf16[4096,128]{1,0:T(8,128)(2,1)}), bf16[4096,2048]{1,0:T(8,128)(2,1)}) %all-gather.6.cloned.1.call-update) | async-done | bytes 16777232 | tf_op jit(solution)/shard_map/all_gather | solution.py:141
  439.4 8.6 %fusion.43 = f32[2,2048]{1,0:T(2,128)S(1)} fusion(bf16[4096,2048]{1,0:T(8,128)(2,1)} %all-gather.6.cloned.1.call-done, bf16[1,128,2,4096]{3,1,2,0:T(8,128)(2,1)S(1)} %copy-done.8, f32[128,2048]{1,0:T(8,128)} %convert_element_type.38), kind=kOutput, calls=%fused_computation.58 | convolution fusion | flops 4296011776 | bytes 19939328 | tf_op jit(solution)/shard_map/ltd,dc->ltc/dot_general | solution.py:138
  449.6 38.4 %psum.7 = f32[2,16]{1,0:T(2,128)S(1)} all-reduce(f32[2,16]{1,0:T(2,128)S(1)} %broadcast_multiply_fusion), channel_id=1, replica_groups=mesh['seq'=16,'head'=2] {'seq','head'}, use_global_device_ids=true, to_apply=%region_9.10 | all-reduce | flops 32 | bytes 256 | tf_op jit(solution)/shard_map/psum | solution.py:147
  (173 shorter events, 106.6 us)
Async XLA Ops:
  7.2 4.4 copy-start.9
  7.2 5.7 %copy-start.10 = (s32[128]{0:T(128)S(1)}, s32[128]{0:T(128)}, u32[]{:S(2)}) copy-start(s32[128]{0:T(128)} %param.14) | copy-start | bytes 1540
  7.2 59.3 %all-gather.4.cloned.1.call-start = ((), (), s32[]{:S(2)}) async-start(), calls=%async_computation.2 | async-start | bytes 4456448 | tf_op jit(solution)/shard_map/all_gather | solution.py:121
  9.1 324.8 %reduce-scatter.2.cloned.1.call-start = ((), (), s32[]{:S(2)}) async-start(), calls=%async_computation.3 | async-start | bytes 4456448 | tf_op jit(solution)/shard_map/reduce_scatter | solution.py:131
  72.8 5.8 %copy-start = (f32[4,512,128,8]{2,1,3,0:T(8,128)S(1)}, f32[4,512,128,8]{2,1,3,0:T(8,128)}, u32[]{:S(2)}) copy-start(f32[4,512,128,8]{2,1,3,0:T(8,128)} %get-tuple-element.617) | copy-start | bytes 25165828 | tf_op jit(solution)/shard_map/while
  93.6 5.8 %copy-start = (f32[4,512,128,8]{2,1,3,0:T(8,128)S(1)}, f32[4,512,128,8]{2,1,3,0:T(8,128)}, u32[]{:S(2)}) copy-start(f32[4,512,128,8]{2,1,3,0:T(8,128)} %get-tuple-element.617) | copy-start | bytes 25165828 | tf_op jit(solution)/shard_map/while
  115.6 5.8 %copy-start = (f32[4,512,128,8]{2,1,3,0:T(8,128)S(1)}, f32[4,512,128,8]{2,1,3,0:T(8,128)}, u32[]{:S(2)}) copy-start(f32[4,512,128,8]{2,1,3,0:T(8,128)} %get-tuple-element.617) | copy-start | bytes 25165828 | tf_op jit(solution)/shard_map/while
  137.6 5.8 %copy-start = (f32[4,512,128,8]{2,1,3,0:T(8,128)S(1)}, f32[4,512,128,8]{2,1,3,0:T(8,128)}, u32[]{:S(2)}) copy-start(f32[4,512,128,8]{2,1,3,0:T(8,128)} %get-tuple-element.617) | copy-start | bytes 25165828 | tf_op jit(solution)/shard_map/while
  162.3 5.8 %copy-start.2 = (bf16[128,4,8,128]{0,3,2,1:T(8,128)(2,1)}, bf16[128,4,8,128]{0,3,2,1:T(8,128)(2,1)S(1)}, u32[]{:S(2)}) copy-start(bf16[128,4,8,128]{0,3,2,1:T(8,128)(2,1)S(1)} %get-tuple-element.706) | copy-start | bytes 3145732 | tf_op jit(solution)/shard_map/while
  175.1 5.3 %copy-start.3 = (bf16[128,4,8,128]{0,3,2,1:T(8,128)(2,1)S(1)}, bf16[128,4,8,128]{0,3,2,1:T(8,128)(2,1)}, u32[]{:S(2)}) copy-start(bf16[128,4,8,128]{0,3,2,1:T(8,128)(2,1)} %copy-done.2) | copy-start | bytes 3145732 | tf_op jit(solution)/shard_map/while
  175.1 5.3 %copy-start.6 = (bf16[128,4096]{0,1:T(8,128)(2,1)S(1)}, bf16[128,4096]{0,1:T(8,128)(2,1)}, u32[]{:S(2)}) copy-start(bf16[128,4096]{0,1:T(8,128)(2,1)} %get-tuple-element.737) | copy-start | bytes 3145732 | tf_op jit(solution)/shard_map/while
  180.4 5.8 %copy-start.2 = (bf16[128,4,8,128]{0,3,2,1:T(8,128)(2,1)}, bf16[128,4,8,128]{0,3,2,1:T(8,128)(2,1)S(1)}, u32[]{:S(2)}) copy-start(bf16[128,4,8,128]{0,3,2,1:T(8,128)(2,1)S(1)} %get-tuple-element.706) | copy-start | bytes 3145732 | tf_op jit(solution)/shard_map/while
  193.2 6.0 %copy-start.3 = (bf16[128,4,8,128]{0,3,2,1:T(8,128)(2,1)S(1)}, bf16[128,4,8,128]{0,3,2,1:T(8,128)(2,1)}, u32[]{:S(2)}) copy-start(bf16[128,4,8,128]{0,3,2,1:T(8,128)(2,1)} %copy-done.2) | copy-start | bytes 3145732 | tf_op jit(solution)/shard_map/while
  193.2 6.0 %copy-start.6 = (bf16[128,4096]{0,1:T(8,128)(2,1)S(1)}, bf16[128,4096]{0,1:T(8,128)(2,1)}, u32[]{:S(2)}) copy-start(bf16[128,4096]{0,1:T(8,128)(2,1)} %get-tuple-element.737) | copy-start | bytes 3145732 | tf_op jit(solution)/shard_map/while
  199.2 5.8 %copy-start.2 = (bf16[128,4,8,128]{0,3,2,1:T(8,128)(2,1)}, bf16[128,4,8,128]{0,3,2,1:T(8,128)(2,1)S(1)}, u32[]{:S(2)}) copy-start(bf16[128,4,8,128]{0,3,2,1:T(8,128)(2,1)S(1)} %get-tuple-element.706) | copy-start | bytes 3145732 | tf_op jit(solution)/shard_map/while
  212.0 6.0 %copy-start.3 = (bf16[128,4,8,128]{0,3,2,1:T(8,128)(2,1)S(1)}, bf16[128,4,8,128]{0,3,2,1:T(8,128)(2,1)}, u32[]{:S(2)}) copy-start(bf16[128,4,8,128]{0,3,2,1:T(8,128)(2,1)} %copy-done.2) | copy-start | bytes 3145732 | tf_op jit(solution)/shard_map/while
  212.0 6.0 %copy-start.6 = (bf16[128,4096]{0,1:T(8,128)(2,1)S(1)}, bf16[128,4096]{0,1:T(8,128)(2,1)}, u32[]{:S(2)}) copy-start(bf16[128,4096]{0,1:T(8,128)(2,1)} %get-tuple-element.737) | copy-start | bytes 3145732 | tf_op jit(solution)/shard_map/while
  218.0 5.8 %copy-start.2 = (bf16[128,4,8,128]{0,3,2,1:T(8,128)(2,1)}, bf16[128,4,8,128]{0,3,2,1:T(8,128)(2,1)S(1)}, u32[]{:S(2)}) copy-start(bf16[128,4,8,128]{0,3,2,1:T(8,128)(2,1)S(1)} %get-tuple-element.706) | copy-start | bytes 3145732 | tf_op jit(solution)/shard_map/while
  230.8 6.0 %copy-start.3 = (bf16[128,4,8,128]{0,3,2,1:T(8,128)(2,1)S(1)}, bf16[128,4,8,128]{0,3,2,1:T(8,128)(2,1)}, u32[]{:S(2)}) copy-start(bf16[128,4,8,128]{0,3,2,1:T(8,128)(2,1)} %copy-done.2) | copy-start | bytes 3145732 | tf_op jit(solution)/shard_map/while
  230.8 6.0 %copy-start.6 = (bf16[128,4096]{0,1:T(8,128)(2,1)S(1)}, bf16[128,4096]{0,1:T(8,128)(2,1)}, u32[]{:S(2)}) copy-start(bf16[128,4096]{0,1:T(8,128)(2,1)} %get-tuple-element.737) | copy-start | bytes 3145732 | tf_op jit(solution)/shard_map/while
  236.9 202.5 %all-gather.6.cloned.1.call-start = ((), (), s32[]{:S(2)}) async-start(), calls=%async_computation.4 | async-start | bytes 17825792 | tf_op jit(solution)/shard_map/all_gather | solution.py:141
  325.0 8.0 %copy-start.4 = (f32[4,8,128,128]{3,2,1,0:T(8,128)S(1)}, f32[4,8,128,128]{3,2,1,0:T(8,128)}, u32[]{:S(2)}) copy-start(f32[4,8,128,128]{3,2,1,0:T(8,128)} %get-tuple-element.723) | copy-start | bytes 6291460
  333.2 106.2 %copy-start.8 = (bf16[1,128,2,4096]{3,1,2,0:T(8,128)(2,1)S(1)}, bf16[1,128,2,4096]{3,1,2,0:T(8,128)(2,1)}, u32[]{:S(2)}) copy-start(bf16[1,128,2,4096]{3,1,2,0:T(8,128)(2,1)} %copy.76) | copy-start | bytes 6291460
  343.6 144.3 %copy-start.11 = (s32[2]{0:T(128)S(1)}, s32[2]{0:T(128)}, u32[]{:S(2)}) copy-start(s32[2]{0:T(128)} %param.17) | copy-start | bytes 28
  (6 other events, 11.8 us)
Sparse Core Ops, SparseCore 0:
  10.7 55.7 all-gather.3
  237.0 70.4 reduce-scatter.1
  309.9 129.4 all-gather.5
where the time goes:
time: 496 us; the launch traced here: 495 us
  waiting for transfers between devices  127 us (26%)
  matrix products  120 us (24%)
  blocking collectives  99.4 us (20%)
  other arithmetic  74.3 us (15%)
  local copies, waits for them, and re-layouts  60.4 us (12%)
  between operations  13.9 us (3%)
    all_gather x1, waiting for transfers between devices, on_device(): lax.all_gather(node_weights, 'seq', axis=1, tiled=True)  95.8 us
    unnamed x5, other arithmetic  45.2 us
    dot_general x4, matrix products, forward_step(): jnp.einsum('gitr,rge->gite', weights, values, precision=lax.Precision.HIG...  38.8 us
    psum x1, blocking collectives, on_device(): totals = lax.psum(partial_value / math.sqrt(seq_total), ('seq', 'head'))  38.4 us
    all_gather x1, waiting for transfers between devices, on_device(): lax.all_gather(keyval, 'seq', axis=0, tiled=True)  30.6 us
    all_to_all x1, blocking collectives, on_device(): lax.all_to_all(deltas, 'head', split_axis=2, concat_axis=0, tiled=True)  29.3 us
    unnamed x25, local copies, waits for them, and re-layouts  25.6 us
    dot_general x8, matrix products, block_logits(): jnp.einsum('tgie,rge->gitr', query_grid, kv_grid[:, :, 0], preferred_elem...  23.8 us
  transfers between devices with their start and end apart: 3, of which 2 were waited for; matrix products, arithmetic and copies ran while one was open for 14% of the time, Pallas kernels for 0%

commit v1 on v0

v1 whole, which is shorter than its diff:
```python
import functools
import math

import jax
import jax.numpy as jnp
from jax import lax
from jax.experimental import pallas as pl
from jax.experimental.pallas import tpu as pltpu
from jax.sharding import PartitionSpec as P

H = 64
KVH = 8
HD = 128
DOC_ROWS = 16
NEG = -1e30
ANY = pl.BlockSpec(memory_space=pl.ANY)
SMEM = pl.BlockSpec(memory_space=pltpu.SMEM)
VMEM = pl.BlockSpec(memory_space=pltpu.VMEM)
F32 = jnp.float32
BF16 = jnp.bfloat16


def head_of(member, members, per_head):
    fold = min(per_head, members)
    return lax.div(member, fold) + lax.rem(member, fold) * (members // fold)


def cols(index, width):
    return pl.ds(pl.multiple_of(index * width, width), width)


def run_copies(copies):
    for copy in copies:
        copy.start()
    for copy in copies:
        copy.wait()


def pack_keys_kernel(members, per_head, place_ref, doc_ref, kv_ref, *outs):
    tok = kv_ref.shape[0]
    ids = (doc_ref[...] + 1).astype(F32)
    ids = jnp.concatenate([ids] * (2 * HD // tok), axis=1)
    for r, out in enumerate(outs):
        head = head_of(place_ref[0] ^ r, members, per_head)
        out[:tok, :] = kv_ref[:, cols(head, 2 * HD)]
        out[tok:, :] = jnp.broadcast_to(ids, (DOC_ROWS, 2 * HD)).astype(BF16)


def pack_keys(place, doc_ids, keyval, members, per_head):
    tok = keyval.shape[0]
    return pl.pallas_call(
        functools.partial(pack_keys_kernel, members, per_head),
        out_shape=[jax.ShapeDtypeStruct((tok + DOC_ROWS, 2 * HD), BF16)] * members,
        in_specs=[SMEM, VMEM, VMEM],
        out_specs=[VMEM] * members,
        name="pack_keys",
    )(place, doc_ids.reshape(1, tok), keyval)


def pack_queries_kernel(members, per_head, width, place_ref, q_ref, o_ref, *outs):
    tok = q_ref.shape[0]
    for r, out in enumerate(outs):
        head = head_of(place_ref[0] ^ (r + 1), members, per_head)
        out[:tok, :] = q_ref[:, cols(head, width)]
        out[tok:, :] = o_ref[:, cols(head, width)]


def pack_queries(place, queries, grad_out, members, per_head, width):
    if members == 1:
        return []
    return pl.pallas_call(
        functools.partial(pack_queries_kernel, members, per_head, width),
        out_shape=[jax.ShapeDtypeStruct((2 * queries.shape[0], width), BF16)] * (members - 1),
        in_specs=[SMEM, VMEM, VMEM],
        out_specs=[VMEM] * (members - 1),
        name="pack_queries",
    )(place, queries, grad_out)


def split_kernel(place_ref, d_ref, mine_ref, theirs_ref):
    width = mine_ref.shape[1]
    mine_ref[...] = d_ref[:, cols(place_ref[1], width)]
    theirs_ref[...] = d_ref[:, cols(1 - place_ref[1], width)]


def split_width(place, rows):
    half = jax.ShapeDtypeStruct((rows.shape[0], rows.shape[1] // 2), BF16)
    return pl.pallas_call(
        split_kernel,
        out_shape=[half, half],
        in_specs=[SMEM, VMEM],
        out_specs=[VMEM, VMEM],
        name="split_deltas",
    )(place, rows)


def attention_kernel(members, per_head, group_size, tok, back, window, n_after, *refs):
    n_kv = back + 1
    n_in = 2 + members + n_kv
    refs = refs[:n_in] + refs[n_in + n_after :]
    place_ref, q_ref, o_ref = refs[:3]
    qo_refs = refs[3 : 2 + members]
    kv_refs = refs[2 + members : 2 + members + n_kv]
    outs = refs[2 + members + n_kv :]
    dq_outs, own_out, prev_outs = outs[:members], outs[members], outs[members + 1 : members + 1 + back]
    qs, dos, kvs, docs, k_t, bias, dqs, dk, dv, sems = outs[members + 1 + back :]
    plane = members * tok
    me = place_ref[0]
    width = group_size * HD
    tile = bias.shape[2]
    span = bias.shape[1]
    n_tiles = plane // tile
    copies = []

    def add(src, dst):
        copies.append(pltpu.make_async_copy(src, dst, sems.at[len(copies)]))

    def rows(shard, size=None):
        size = tok if size is None else size
        return pl.ds(pl.multiple_of(shard * size, size), size)

    for r in range(members):
        shard = me ^ r
        for b in range(n_kv):
            at = (back - b) * members + shard
            add(kv_refs[b].at[r, pl.ds(0, tok), :], kvs.at[rows(at), :])
            add(kv_refs[b].at[r, pl.ds(tok, DOC_ROWS), :], docs.at[rows(at, DOC_ROWS), :])
    head = head_of(me, members, per_head)
    add(q_ref.at[:, cols(head, width)], qs.at[rows(me), :])
    add(o_ref.at[:, cols(head, width)], dos.at[rows(me), :])
    for r in range(1, members):
        add(qo_refs[r - 1].at[pl.ds(0, tok), :], qs.at[rows(me ^ r), :])
        add(qo_refs[r - 1].at[pl.ds(tok, tok), :], dos.at[rows(me ^ r), :])
    for copy in copies:
        copy.start()
    dk[...] = jnp.zeros_like(dk)
    dv[...] = jnp.zeros_like(dv)
    for copy in copies[: 2 * members * n_kv]:
        copy.wait()

    n_blocks = n_kv * plane // tok
    eye = lax.broadcasted_iota(jnp.int32, (tok, tok), 0) == lax.broadcasted_iota(jnp.int32, (tok, tok), 1)
    for b in range(n_blocks):
        k_t[:, b * tok : (b + 1) * tok] = kvs[b * tok : (b + 1) * tok, :HD].astype(F32).T.astype(BF16)
    first = back * plane - window

    def doc_row(b):
        return docs[b * DOC_ROWS : (b + 1) * DOC_ROWS, :tok].astype(F32)[:1]

    for b in range(n_blocks):
        column = jnp.sum(jnp.where(eye, jnp.broadcast_to(doc_row(b), (tok, tok)), 0.0), axis=1, keepdims=True)
        for i in range(n_tiles):
            low = first + i * tile
            if b * tok < low or b * tok >= low + span:
                continue
            at = b * tok - low
            here = back * plane + i * tile
            q_row = jnp.concatenate([doc_row(here // tok + k) for k in range(tile // tok)], axis=1)
            key_pos = b * tok + lax.broadcasted_iota(jnp.int32, (tok, tile), 0)
            query_pos = here + lax.broadcasted_iota(jnp.int32, (tok, tile), 1)
            ok = (column == q_row) & (key_pos <= query_pos)
            bias[i, at : at + tok, :] = jnp.where(ok, 0.0, NEG)
    for copy in copies[2 * members * n_kv :]:
        copy.wait()

    scale = 1.0 / math.sqrt(HD)
    to_log2 = scale * math.log2(math.e)
    nt = (((1,), (1,)), ((), ()))

    def one_head(h, _):
        at_h = cols(h, HD)
        for i in range(n_tiles):
            low = first + i * tile
            q = qs[i * tile : (i + 1) * tile, at_h]
            do = dos[i * tile : (i + 1) * tile, at_h]
            keys = kvs[low : low + span, :HD]
            values = kvs[low : low + span, HD:]
            st = lax.dot_general(keys, q, nt, preferred_element_type=F32) * to_log2 + bias[i]
            top = jnp.max(st, axis=0, keepdims=True)
            e = jnp.exp2(st - top)
            inv = 1.0 / jnp.sum(e, axis=0, keepdims=True)
            dpt = lax.dot_general(values, do, nt, preferred_element_type=F32)
            p = e * inv
            row_dot = jnp.sum(p * dpt, axis=0, keepdims=True)
            ds = (p * (dpt - row_dot)).astype(BF16)
            dv[low : low + span, :] += jnp.dot(p.astype(BF16), do, preferred_element_type=F32)
            dk[low : low + span, :] += jnp.dot(ds, q, preferred_element_type=F32)
            dqt = jnp.dot(k_t[:, low : low + span], ds, preferred_element_type=F32)
            dqs[i * tile : (i + 1) * tile, at_h] = (dqt.T * scale).astype(BF16)
        return 0

    lax.fori_loop(0, group_size, one_head, 0)
    own_out[:, :HD] = dk[back * plane :, :] * scale
    own_out[:, HD:] = dv[back * plane :, :]
    for b in range(1, n_kv):
        low = (back - b) * plane
        prev_outs[b - 1][:, :HD] = (dk[low : low + plane, :] * scale).astype(BF16)
        prev_outs[b - 1][:, HD:] = dv[low : low + plane, :].astype(BF16)
    run_copies(
        [pltpu.make_async_copy(dqs.at[rows(me ^ r), :], dq_outs[r], sems.at[r]) for r in range(members)]
    )


def attention(place, queries, grad_out, qo, kv, members, per_head, group_size, window, after):
    tok = queries.shape[0]
    plane = members * tok
    back = len(kv) - 1
    tile = min(256, plane)
    span = window + tile
    keys = (back + 1) * plane
    width = group_size * HD
    n_copies = 2 * members * len(kv) + 2 * members
    flops = 40 * group_size * plane * span * HD
    return pl.pallas_call(
        functools.partial(attention_kernel, members, per_head, group_size, tok, back, window, len(after)),
        out_shape=[jax.ShapeDtypeStruct((tok, width), BF16)] * members
        + [jax.ShapeDtypeStruct((plane, 2 * HD), F32)]
        + [jax.ShapeDtypeStruct((plane, 2 * HD), BF16)] * back,
        in_specs=[SMEM] + [ANY] * (2 + len(qo) + len(kv) + len(after)),
        out_specs=[ANY] * members + [VMEM] * (1 + back),
        scratch_shapes=[
            pltpu.VMEM((plane, width), BF16),
            pltpu.VMEM((plane, width), BF16),
            pltpu.VMEM((keys, 2 * HD), BF16),
            pltpu.VMEM((keys // tok * DOC_ROWS, 2 * HD), BF16),
            pltpu.VMEM((HD, keys), BF16),
            pltpu.VMEM((plane // tile, span, tile), F32),
            pltpu.VMEM((plane, width), BF16),
            pltpu.VMEM((keys, HD), F32),
            pltpu.VMEM((keys, HD), F32),
            pltpu.SemaphoreType.DMA((n_copies,)),
        ],
        compiler_params=pltpu.CompilerParams(vmem_limit_bytes=48 * 2**20),
        cost_estimate=pl.CostEstimate(
            flops=flops, bytes_accessed=6 * plane * width, transcendentals=group_size * plane * span
        ),
        name="attention_both_ways",
    )(place, queries, grad_out, *qo, *kv, *after)


def combine_kernel(members, tok, n_prev, place_ref, own_ref, *refs):
    prev, outs = refs[:n_prev], refs[n_prev:]
    token_outs, part_outs = outs[:members], outs[members : members + 2]
    total = outs[-1]
    g = own_ref[...]
    for part in prev:
        g = g + part[...].astype(F32)
    total[...] = g.astype(BF16)
    me = place_ref[0]
    kind = lax.rem(me, 2)
    part_outs[0][...] = total[:, cols(kind, HD)]
    part_outs[1][...] = total[:, cols(1 - kind, HD)]
    for r in range(members):
        token_outs[r][...] = total[pl.ds(pl.multiple_of((me ^ r) * tok, tok), tok), :]


def combine(place, own, prev, members, tok, after):
    plane = own.shape[0]
    n_after = len(after)

    def kernel(place_ref, own_ref, *refs):
        combine_kernel(members, tok, len(prev), place_ref, own_ref, *refs[: len(prev)], *refs[len(prev) + n_after :])

    return pl.pallas_call(
        kernel,
        out_shape=[jax.ShapeDtypeStruct((tok, 2 * HD), BF16)] * members
        + [jax.ShapeDtypeStruct((plane, HD), BF16)] * 2,
        in_specs=[SMEM] + [VMEM] * (1 + len(prev)) + [ANY] * n_after,
        out_specs=[VMEM] * (members + 2),
        scratch_shapes=[pltpu.VMEM((plane, 2 * HD), BF16)],
        name="sum_key_value_gradients",
    )(place, own, *prev, *after)


def settle_kernel(members, per_head, place_ref, *refs):
    dq, dkv = refs[:members], refs[members : 2 * members]
    out_q, out_kv = refs[2 * members :]
    for r in range(members):
        head = head_of(place_ref[0] ^ r, members, per_head)
        out_q[:, cols(head, dq[r].shape[1])] = dq[r][...]
        out_kv[:, cols(head, dkv[r].shape[1])] = dkv[r][...]


def settle(place, dq, dkv, per_head):
    members = len(dq)
    tok = dq[0].shape[0]
    return pl.pallas_call(
        functools.partial(settle_kernel, members, per_head),
        out_shape=[
            jax.ShapeDtypeStruct((tok, members * dq[0].shape[1]), BF16),
            jax.ShapeDtypeStruct((tok, members * dkv[0].shape[1]), BF16),
        ],
        in_specs=[SMEM] + [VMEM] * (2 * members),
        out_specs=[VMEM, VMEM],
        name="place_heads",
    )(place, *dq, *dkv)


def project_kernel(place_ref, *refs):
    d_refs, (w0, wa, wb0, wb1, wc0, wc1, out_ref, ds, ws, sems) = refs[:8], refs[8:]
    me, plane_at = place_ref[0], place_ref[2]
    tok = d_refs[0].shape[0]
    inner = jnp.logical_or(plane_at == 1, plane_at == 2)
    w_copies = []
    for k, pair in enumerate(((w0, w0), (wa, wa), (wb0, wb1), (wc0, wc1))):
        dst = ws.at[:, k * HD : (k + 1) * HD]
        if pair[0] is pair[1]:
            copy = pltpu.make_async_copy(pair[0], dst, sems.at[k])
            copy.start()
        else:
            copy = pltpu.make_async_copy(pair[1], dst, sems.at[k])

            @pl.when(inner)
            def _():
                pltpu.make_async_copy(pair[0], dst, sems.at[k]).start()

            @pl.when(jnp.logical_not(inner))
            def _():
                copy.start()

        w_copies.append(copy)
    copies = []
    for layer in range(2):
        for r in range(4):
            shard = layer * 4 + (me ^ r)
            dst = ds.at[pl.ds(pl.multiple_of(shard * tok, tok), tok), :]
            copies.append(pltpu.make_async_copy(d_refs[layer * 4 + r], dst, sems.at[4 + len(copies)]))
            copies[-1].start()
    for copy in w_copies + copies:
        copy.wait()
    step = 256

    def one(i, _):
        at = pl.ds(pl.multiple_of(i * step, step), step)
        out_ref[at, :] = jnp.dot(ds[at, :], ws[...], preferred_element_type=F32)
        return 0

    lax.fori_loop(0, ds.shape[0] // step, one, 0)


def project(place, pieces, blocks):
    tok, depth = pieces[0].shape
    rows = tok * len(pieces)
    return pl.pallas_call(
        project_kernel,
        out_shape=jax.ShapeDtypeStruct((rows, 4 * HD), F32),
        in_specs=[SMEM] + [ANY] * (len(pieces) + len(blocks)),
        out_specs=VMEM,
        scratch_shapes=[
            pltpu.VMEM((rows, depth), BF16),
            pltpu.VMEM((depth, 4 * HD), BF16),
            pltpu.SemaphoreType.DMA((4 + len(pieces),)),
        ],
        compiler_params=pltpu.CompilerParams(vmem_limit_bytes=48 * 2**20),
        cost_estimate=pl.CostEstimate(
            flops=2 * rows * depth * 4 * HD, bytes_accessed=2 * depth * (rows + 4 * HD), transcendentals=0
        ),
        name="project_deltas",
    )(place, *pieces, *blocks)


def contract_kernel(norm, place_ref, slot_ref, p_ref, g0, g1, g2, g3, out_ref):
    me, side, plane_at = place_ref[0], place_ref[1], place_ref[2]
    kind = lax.rem(me, 2)
    row = lax.broadcasted_iota(jnp.int32, out_ref.shape, 0)
    lane = lax.broadcasted_iota(jnp.int32, out_ref.shape, 1)
    total = jnp.zeros(out_ref.shape, F32)
    n_tok = g0.shape[0]
    for k, g_ref in enumerate((g0, g1, g2, g3)):
        block = 2 * (side ^ (k // 2)) + (kind ^ (k % 2))
        far = jnp.where(plane_at < 2, 2, 1)
        slot = jnp.where(
            block == plane_at, 0, jnp.where(block == (plane_at ^ 1), 1, jnp.where(block == far, 2, 3))
        )
        g = g_ref[...].astype(F32)
        for layer in range(2):
            part = p_ref[layer * n_tok : (layer + 1) * n_tok, cols(slot, HD)] * g
            value = jnp.sum(jnp.sum(part, axis=0, keepdims=True), axis=1, keepdims=True) * norm
            here = (row == slot_ref[side ^ layer]) & (lane == 4 * block + me)
            total = total + jnp.where(here, value, 0.0)
    out_ref[...] = total


def contract(place, layer_slot, projected, parts, norm):
    return pl.pallas_call(
        functools.partial(contract_kernel, norm),
        out_shape=jax.ShapeDtypeStruct((8, HD), F32),
        in_specs=[SMEM, SMEM] + [VMEM] * 5,
        out_specs=VMEM,
        compiler_params=pltpu.CompilerParams(vmem_limit_bytes=32 * 2**20),
        name="contract_scores",
    )(place, layer_slot, projected, *parts)


def on_device(queries, keyval, grad_out, doc_ids, deltas, node_weights, layer_slot):
    tok = queries.shape[0]
    members = keyval.shape[1] // (2 * HD)
    group_size = H // KVH
    n_seq, n_head = lax.axis_size("seq"), lax.axis_size("head")
    planes = n_seq // members
    plane_tok = members * tok
    window = n_seq * tok // 2
    back = -(-window // plane_tok)
    block_width = node_weights.shape[1]
    per_head = 2 * HD // block_width
    at_seq, at_head = lax.axis_index("seq"), lax.axis_index("head")
    place = jnp.stack([lax.rem(at_seq, members), at_head, lax.div(at_seq, members)]).astype(jnp.int32)

    def to_member(x, r):
        return lax.ppermute(x, "seq", [(s, s - s % members + ((s % members) ^ r)) for s in range(n_seq)])

    def to_plane(x, pairs):
        return lax.ppermute(
            x, "seq", [(a * members + k, b * members + k) for a, b in pairs for k in range(members)]
        )

    def shift(x, step):
        return to_plane(x, [(a, a + step) for a in range(planes) if 0 <= a + step < planes])

    def other_head(x):
        return lax.ppermute(x, "head", [(0, 1), (1, 0)])

    def other_head_and_member(x):
        pairs = [(2 * s + h, 2 * (s ^ 1) + (h ^ 1)) for s in range(n_seq) for h in range(2)]
        return lax.ppermute(x, ("seq", "head"), pairs)

    spread = n_head == 2 and members == 4 and planes == 4 and per_head == 2 and deltas.shape[0] == 1
    if spread:
        w_pair = to_plane(node_weights, [(0, 1), (1, 0), (2, 3), (3, 2)])
        w_mid = to_plane(node_weights, [(1, 2), (2, 1)])

    packed = pack_keys(place, doc_ids, keyval, members, per_head)
    kv_pieces = [packed[0]] + [to_member(packed[r], r) for r in range(1, members)]
    packed = pack_queries(place, queries, grad_out, members, per_head, group_size * HD)
    qo = [to_member(packed[r - 1], r) for r in range(1, members)]
    kv_plane = jnp.stack(kv_pieces)
    kv = [kv_plane] + [shift(kv_plane, k) for k in range(1, back + 1)]

    first, second = [], []
    if spread:
        mine, theirs = split_width(place, deltas.reshape(tok, deltas.shape[2]))
        crossed = other_head(theirs)
        near = [mine, to_member(mine, 2), crossed, to_member(crossed, 2)]
        far = [to_member(d, 1) for d in near]
        pieces = [near[0], far[0], near[1], far[1], near[2], far[2], near[3], far[3]]
        w_end = to_plane(w_mid, [(1, 0), (2, 3)])
        w_mid2 = to_plane(w_pair, [(1, 2), (2, 1)])
        w_end2 = to_plane(w_mid2, [(1, 0), (2, 3)])
        first = [w_pair, w_mid]
        second = [w_end, w_mid2]

    out = attention(place, queries, grad_out, qo, kv, members, per_head, group_size, window, first)
    dq, own, prev = out[:members], out[members], out[members + 1 :]
    prev = [shift(prev[k], -(k + 1)) for k in range(back)]
    dq = [dq[0]] + [to_member(dq[r], r) for r in range(1, members)]
    summed = combine(place, own, prev, members, tok, second)
    token_parts, kinds = summed[:members], summed[members:]
    if spread:
        parts = [kinds[0], to_member(kinds[1], 1), other_head(kinds[0]), other_head_and_member(kinds[1])]
    dkv = [token_parts[0]] + [to_member(token_parts[r], r) for r in range(1, members)]
    grad_query, grad_keyval = settle(place, dq, dkv, per_head)
    norm = 1.0 / math.sqrt(n_seq * tok)
    if spread:
        projected = project(place, pieces, [node_weights, w_pair, w_mid, w_end, w_mid2, w_end2])
        mine = contract(place, layer_slot, projected, parts, norm)
        n_dev = n_seq * n_head
        copies = lax.all_to_all(
            jnp.broadcast_to(mine[None], (n_dev,) + mine.shape), ("seq", "head"), 0, 0, tiled=True
        )
        scores = jnp.sum(copies, axis=0)[: layer_slot.shape[0], : n_seq * block_width // HD]
        return grad_query, grad_keyval, scores

    width_deltas = lax.all_to_all(deltas, "head", split_axis=2, concat_axis=0, tiled=True)
    grad_rows = lax.all_gather(grad_keyval, "head", axis=1, tiled=True)
    layer_count = width_deltas.shape[0]
    weights = lax.all_gather(node_weights, "seq", axis=1, tiled=True)
    projected = jnp.einsum("ltd,dc->ltc", width_deltas, weights, preferred_element_type=F32)
    per_column = jnp.sum(projected * grad_rows.astype(F32)[None], axis=1)
    partial_value = jnp.sum(per_column.reshape(layer_count, grad_rows.shape[1] // HD, HD), axis=2)
    totals = lax.psum(partial_value * norm, ("seq", "head"))
    placing = (layer_slot[:, None] == jnp.arange(layer_count, dtype=jnp.int32)[None, :]).astype(F32)
    scores = jnp.dot(placing.T, totals, precision=lax.Precision.HIGHEST)
    return grad_query, grad_keyval, scores


def solution(mesh):
    return jax.shard_map(
        on_device,
        mesh=mesh,
        in_specs=(
            P("seq", "head"),
            P("seq", "head"),
            P("seq", "head"),
            P("seq"),
            P("head", "seq", None),
            P("head", "seq"),
            P(),
        ),
        out_specs=(P("seq", "head"), P("seq", "head"), P()),
        check_vma=False,
    )
```

time: 496 us -> 196 us (0.40)
  matrix products: 120 us -> 0 us
  blocking collectives: 99.4 us -> 0 us
  other arithmetic: 74.3 us -> 1.58 us
  Pallas kernels: 0 us -> 52.7 us
  local copies, waits for them, and re-layouts: 60.4 us -> 8.58 us
  starting transfers between devices: 0.12 us -> 36.8 us
  waiting for transfers between devices: 127 us -> 95.1 us
  between operations: 13.9 us -> 0.86 us
    all_gather x2 -> x0, waiting for transfers between devices: 126 us -> none  [the longest x1 95.8 us: on_device(): lax.all_gather(node_weights, 'seq', axis=1, tiled=True)]
    dot_general x30 -> x0, matrix products: 120 us -> none  [the longest x4 38.8 us: forward_step(): jnp.einsum('gitr,rge->gite', weights, values, precision=lax.Precision.HIG...]
    ppermute x0 -> x31, waiting for transfers between devices: none -> 95.1 us  [the longest x9 65.8 us: to_plane(): lax.ppermute(x, 'seq', [(a * members + k, b * members + k) for a, b in pa...]
    pallas_call x0 -> x8, Pallas kernels: none -> 52.7 us  [the longest x1 28.8 us: attention(): pl.pallas_call(functools.partial(attention_kernel, members, per_head, gro...]
    unnamed x5 -> x0, other arithmetic: 45.2 us -> none
    psum x1 -> x0, blocking collectives: 38.4 us -> none  [on_device(): totals = lax.psum(partial_value / math.sqrt(seq_total), ('seq', 'head'))]
    ppermute x0 -> x31, starting transfers between devices: none -> 34.2 us  [the longest x9 18 us: to_plane(): lax.ppermute(x, 'seq', [(a * members + k, b * members + k) for a, b in pa...]
    all_gather x2 -> x0, blocking collectives: 31.7 us -> none  [the longest x1 23.1 us: on_device(): lax.all_gather(doc_ids, 'seq', axis=0, tiled=True)]
  transfers between devices with their start and end apart: 3 -> 32, of which waited for: 2 -> 12; matrix products, arithmetic and copies ran while one was open for 14% -> 0% of each run, Pallas kernels for 0% -> 26%
where the time goes in v1:
time: 196 us
  waiting for transfers between devices  95.1 us (49%)
  Pallas kernels  52.7 us (27%)
  starting transfers between devices  36.8 us (19%)
  local copies, waits for them, and re-layouts  8.58 us (4%)
    ppermute x9, waiting for transfers between devices, to_plane(): lax.ppermute(x, 'seq', [(a * members + k, b * members + k) for a, b in pa...  65.8 us
    ppermute x19, waiting for transfers between devices, to_member(): lax.ppermute(x, 'seq', [(s, s - s % members + (s % members ^ r)) for s in...  29.3 us
    pallas_call x1, Pallas kernels, attention(): pl.pallas_call(functools.partial(attention_kernel, members, per_head, gro...  28.8 us
    ppermute x9, starting transfers between devices, to_plane(): lax.ppermute(x, 'seq', [(a * members + k, b * members + k) for a, b in pa...  18 us
    ppermute x19, starting transfers between devices, to_member(): lax.ppermute(x, 'seq', [(s, s - s % members + (s % members ^ r)) for s in...  11.5 us
    pallas_call x1, Pallas kernels, project(): pl.pallas_call(project_kernel, out_shape=jax.ShapeDtypeStruct((rows, 4 *...  10.7 us
    unnamed x46, local copies, waits for them, and re-layouts  7.35 us
  transfers between devices with their start and end apart: 32, of which 12 were waited for; matrix products, arithmetic and copies ran while one was open for 0% of the time, Pallas kernels for 26%

profile of v1, /device:TPU:0, one launch (start us, length us, event | category | flops | bytes accessed | tf_op | source)
XLA Modules:
  0.0 195.6 jit_solution(2705980328849277183)
XLA Ops:
  1.3 1.7 pack_keys.1
  3.4 2.5 %collective-permute-start.4 = (bf16[144,256]{1,0:T(8,128)(2,1)}, bf16[144,256]{1,0:T(8,128)(2,1)S(1)}, u32[]{:S(2)}, u32[]{:S(2)}) collective-permute-start(bf16[144,256]{1,0:T(8,128)(2,1)} %get-tuple-element.32), channel_id=1, source_target_pairs={{0,4},{2,6},{4,0},{6,2},{8,12},{10,14},{12,8},{14,10},{16,20},{18,... | collective-permute-start | bytes 221192 | tf_op jit(solution)/shard_map/ppermute | solution.py:410
  6.1 3.0 %collective-permute-done.4 = bf16[144,256]{1,0:T(8,128)(2,1)S(1)} collective-permute-done((bf16[144,256]{1,0:T(8,128)(2,1)}, bf16[144,256]{1,0:T(8,128)(2,1)S(1)}, u32[]{:S(2)}, u32[]{:S(2)}) %collective-permute-start.4) | collective-permute-done | bytes 73760 | tf_op jit(solution)/shard_map/ppermute | solution.py:410
  11.4 3.7 %collective-permute-start.6 = (bf16[4,144,256]{2,1,0:T(8,128)(2,1)S(1)}, bf16[4,144,256]{2,1,0:T(8,128)(2,1)S(1)}, u32[]{:S(2)}, u32[]{:S(2)}) collective-permute-start(bf16[4,144,256]{2,1,0:T(8,128)(2,1)S(1)} %pad_maximum_fusion.refs_6_), channel_id=1, source_target_pairs={{0,8},{2,10},{4,12},{6,14},{8,16},{10,18},{12,20},{14,22},{16,24},... | collective-permute-start | bytes 884744 | tf_op jit(solution)/shard_map/ppermute | solution.py:413
  15.1 1.6 collective-permute-start.8
  16.7 1.6 collective-permute-start.9
  18.4 3.1 %split_deltas.1 = (bf16[128,4096]{1,0:T(8,128)(2,1)}, bf16[128,4096]{1,0:T(8,128)(2,1)}) custom-call(s32[3]{0:T(128)} %pad_add_fusion.place_ref.refs_0_, bf16[128,8192]{1,0:T(8,128)(2,1)} %bitcast.9), custom_call_target="tpu_custom_call" | custom-call | tf_op jit(solution)/shard_map/split_deltas/pallas_call | solution.py:88
  22.9 2.8 %pack_queries.1 = (bf16[256,1024]{1,0:T(8,128)(2,1)}, bf16[256,1024]{1,0:T(8,128)(2,1)}, bf16[256,1024]{1,0:T(8,128)(2,1)}) custom-call(s32[3]{0:T(128)} %pad_add_fusion.place_ref.refs_0_, bf16[128,4096]{1,0:T(8,128)(2,1)} %refs_1_.1, bf16[128,4096]{1,0:T(8,128)(2,1)} %refs_2_.1), custom_call_target="tpu_custom_call" | custom-call | tf_op jit(solution)/shard_map/pack_queries/pallas_call | solution.py:71
  26.5 4.1 %collective-permute-start.7 = (bf16[4,144,256]{2,1,0:T(8,128)(2,1)S(1)}, bf16[4,144,256]{2,1,0:T(8,128)(2,1)S(1)}, u32[]{:S(2)}, u32[]{:S(2)}) collective-permute-start(bf16[4,144,256]{2,1,0:T(8,128)(2,1)S(1)} %pad_maximum_fusion.refs_6_), channel_id=1, source_target_pairs={{0,16},{2,18},{4,20},{6,22},{8,24},{10,26},{12,28},{14,30},{1,17},... | collective-permute-start | bytes 884744 | tf_op jit(solution)/shard_map/ppermute | solution.py:413
  30.7 19.8 %collective-permute-done.7.refs_8_ = bf16[4,144,256]{2,1,0:T(8,128)(2,1)S(1)} collective-permute-done((bf16[4,144,256]{2,1,0:T(8,128)(2,1)S(1)}, bf16[4,144,256]{2,1,0:T(8,128)(2,1)S(1)}, u32[]{:S(2)}, u32[]{:S(2)}) %collective-permute-start.7) | collective-permute-done | bytes 294944 | tf_op jit(solution)/shard_map/ppermute | solution.py:413
  51.9 13.6 %collective-permute-done.1.refs_4_ = bf16[256,1024]{1,0:T(8,128)(2,1)S(1)} collective-permute-done((bf16[256,1024]{1,0:T(8,128)(2,1)}, bf16[256,1024]{1,0:T(8,128)(2,1)S(1)}, u32[]{:S(2)}, u32[]{:S(2)}) %collective-permute-start.1) | collective-permute-done | bytes 524320 | tf_op jit(solution)/shard_map/ppermute | solution.py:410
  67.6 1.6 collective-permute-start.16
  70.5 5.3 %collective-permute-done.2.refs_5_ = bf16[256,1024]{1,0:T(8,128)(2,1)S(1)} collective-permute-done((bf16[256,1024]{1,0:T(8,128)(2,1)}, bf16[256,1024]{1,0:T(8,128)(2,1)S(1)}, u32[]{:S(2)}, u32[]{:S(2)}) %collective-permute-start.2) | collective-permute-done | bytes 524320 | tf_op jit(solution)/shard_map/ppermute | solution.py:410
  78.0 28.8 %attention_both_ways.1 = (bf16[128,1024]{1,0:T(8,128)(2,1)S(1)}, bf16[128,1024]{1,0:T(8,128)(2,1)S(1)}, bf16[128,1024]{1,0:T(8,128)(2,1)S(1)}, bf16[128,1024]{1,...) custom-call(s32[3]{0:T(128)S(1)} %copy-done.6, ...), custom_call_target="tpu_custom_call" | custom-call | flops 26843545600 | bytes 3145728 | tf_op jit(solution)/shard_map/attention_both_ways/pallas_call | solution.py:214
  111.8 13.9 %collective-permute-done.13.refs_0_ = bf16[512,256]{1,0:T(8,128)(2,1)S(1)} collective-permute-done((bf16[512,256]{1,0:T(8,128)(2,1)S(1)}, bf16[512,256]{1,0:T(8,128)(2,1)S(1)}, u32[]{:S(2)}, u32[]{:S(2)}) %collective-permute-start.13) | collective-permute-done | bytes 262176 | tf_op jit(solution)/shard_map/ppermute | solution.py:413
  125.9 12.7 %collective-permute-done.14.refs_1_ = bf16[512,256]{1,0:T(8,128)(2,1)S(1)} collective-permute-done((bf16[512,256]{1,0:T(8,128)(2,1)S(1)}, bf16[512,256]{1,0:T(8,128)(2,1)S(1)}, u32[]{:S(2)}, u32[]{:S(2)}) %collective-permute-start.14) | collective-permute-done | bytes 262176 | tf_op jit(solution)/shard_map/ppermute | solution.py:413
  140.6 2.2 %sum_key_value_gradients.1 = (bf16[128,256]{1,0:T(8,128)(2,1)}, bf16[128,256]{1,0:T(8,128)(2,1)}, bf16[128,256]{1,0:T(8,128)(2,1)}, bf16[128,256]{1,0:T(8,128)(2...) custom-call(s32[3]{0:T(128)} %pad_add_fusion.place_ref.refs_0_, f32[512,256]{1,0:T(8,128)} %copy-done.3, ...), custom_call_target="tpu_custom_call" | custom-call | tf_op jit(solution)/shard_map/sum_key_value_gradients/pallas_call | solution.py:264
  145.9 1.7 collective-permute-start.30
  147.7 19.3 %collective-permute-done.27.refs_13_ = bf16[4096,128]{1,0:T(8,128)(2,1)} collective-permute-done((bf16[4096,128]{1,0:T(8,128)(2,1)}, bf16[4096,128]{1,0:T(8,128)(2,1)}, u32[]{:S(2)}, u32[]{:S(2)}) %collective-permute-start.27) | collective-permute-done | bytes 1048608 | tf_op jit(solution)/shard_map/ppermute | solution.py:413
  168.5 10.7 %project_deltas.1.p_ref = f32[1024,512]{1,0:T(8,128)} custom-call(s32[3]{0:T(128)S(1)} %copy-done.7, bf16[128,4096]{1,0:T(8,128)(2,1)S(1)} %copy-done.1, bf16[128,4096]{1,0:T(8,128)(2,1)} %collective-permute-done.20.refs_1_, bf16[128,4096]{1,0:T(8,128)(2,1)S(1)} %collective-permute-done.21.refs_2_, bf16[128,4096]{1,0:T(8,128)(2,1)} %collective-permute-done.22.refs_3_, ...), custom_call_target="tpu_custom_call" | custom-call | flops 4294967296 | bytes 12582912 | tf_op jit(solution)/shard_map/project_deltas/pallas_call | solution.py:344
  182.5 2.6 %all-to-all-start = ((f32[32,8,128]{2,1,0:T(8,128)}), f32[32,8,128]{2,1,0:T(8,128)S(1)}, u32[]{:S(2)}, u32[]{:S(2)}) async-start(f32[32,8,128]{2,1,0:T(8,128)} %broadcast_in_dim.2), calls=%async_computation | async-start | bytes 262144 | tf_op jit(solution)/shard_map/all_to_all | solution.py:467
  185.2 1.7 collective-permute-start.18
  187.1 3.6 %collective-permute-done.18.refs_6_ = bf16[128,256]{1,0:T(8,128)(2,1)S(1)} collective-permute-done((bf16[128,256]{1,0:T(8,128)(2,1)S(1)}, bf16[128,256]{1,0:T(8,128)(2,1)S(1)}, u32[]{:S(2)}, u32[]{:S(2)}) %collective-permute-start.18) | collective-permute-done | bytes 65568 | tf_op jit(solution)/shard_map/ppermute | solution.py:410
  192.6 2.4 %place_heads.1 = (bf16[128,4096]{1,0:T(8,128)(2,1)}, bf16[128,1024]{1,0:T(8,128)(2,1)}) custom-call(s32[3]{0:T(128)} %pad_add_fusion.place_ref.refs_0_, bf16[128,1024]{1,0:T(8,128)(2,1)} %copy-done.4, bf16[128,1024]{1,0:T(8,128)(2,1)} %collective-permute-done.10.refs_1_, bf16[128,1024]{1,0:T(8,128)(2,1)} %collective-permute-done.11.refs_2_, ...), custom_call_target="tpu_custom_call" | custom-call | tf_op jit(solution)/shard_map/place_heads/pallas_call | solution.py:287
  (99 shorter events, 30.4 us)
Async XLA Ops:
  11.4 14.4 %collective-permute-start.6 = (bf16[4,144,256]{2,1,0:T(8,128)(2,1)S(1)}, bf16[4,144,256]{2,1,0:T(8,128)(2,1)S(1)}, u32[]{:S(2)}, u32[]{:S(2)}) collective-permute-start(bf16[4,144,256]{2,1,0:T(8,128)(2,1)S(1)} %pad_maximum_fusion.refs_6_), channel_id=1, source_target_pairs={{0,8},{2,10},{4,12},{6,14},{8,16},{10,18},{12,20},{14,22},{16,24},... | collective-permute-start | bytes 884744 | tf_op jit(solution)/shard_map/ppermute | solution.py:413
  15.1 52.5 %collective-permute-start.8 = (bf16[4096,128]{1,0:T(8,128)(2,1)}, bf16[4096,128]{1,0:T(8,128)(2,1)}, u32[]{:S(2)}, u32[]{:S(2)}) collective-permute-start(bf16[4096,128]{1,0:T(8,128)(2,1)} %refs_8_.1), channel_id=1, source_target_pairs={{0,8},{2,10},{4,12},{6,14},{8,0},{10,2},{12,4},{14,6},{16,24},{18,... | collective-permute-start | bytes 3145736 | tf_op jit(solution)/shard_map/ppermute | solution.py:413
  16.7 52.5 %collective-permute-start.9 = (bf16[4096,128]{1,0:T(8,128)(2,1)}, bf16[4096,128]{1,0:T(8,128)(2,1)}, u32[]{:S(2)}, u32[]{:S(2)}) collective-permute-start(bf16[4096,128]{1,0:T(8,128)(2,1)} %refs_8_.1), channel_id=1, source_target_pairs={{8,16},{10,18},{12,20},{14,22},{16,8},{18,10},{20,12},{22,14},{9,1... | collective-permute-start | bytes 3145736 | tf_op jit(solution)/shard_map/ppermute | solution.py:413
  21.5 45.5 %collective-permute-start.23 = (bf16[128,4096]{1,0:T(8,128)(2,1)}, bf16[128,4096]{1,0:T(8,128)(2,1)S(1)}, u32[]{:S(2)}, u32[]{:S(2)}) collective-permute-start(bf16[128,4096]{1,0:T(8,128)(2,1)} %get-tuple-element.48), channel_id=1, source_target_pairs={{0,1},{1,0},{2,3},{3,2},{4,5},{5,4},{6,7},{7,6},{8,9},{9,8},{10,11... | collective-permute-start | bytes 3145736 | tf_op jit(solution)/shard_map/ppermute | solution.py:421
  25.8 26.2 %collective-permute-start = (bf16[256,1024]{1,0:T(8,128)(2,1)}, bf16[256,1024]{1,0:T(8,128)(2,1)S(1)}, u32[]{:S(2)}, u32[]{:S(2)}) collective-permute-start(bf16[256,1024]{1,0:T(8,128)(2,1)} %get-tuple-element.27), channel_id=1, source_target_pairs={{0,2},{2,0},{4,6},{6,4},{8,10},{10,8},{12,14},{14,12},{16,18},{18,... | collective-permute-start | bytes 1572872 | tf_op jit(solution)/shard_map/ppermute | solution.py:410
  26.5 23.9 %collective-permute-start.7 = (bf16[4,144,256]{2,1,0:T(8,128)(2,1)S(1)}, bf16[4,144,256]{2,1,0:T(8,128)(2,1)S(1)}, u32[]{:S(2)}, u32[]{:S(2)}) collective-permute-start(bf16[4,144,256]{2,1,0:T(8,128)(2,1)S(1)} %pad_maximum_fusion.refs_6_), channel_id=1, source_target_pairs={{0,16},{2,18},{4,20},{6,22},{8,24},{10,26},{12,28},{14,30},{1,17},... | collective-permute-start | bytes 884744 | tf_op jit(solution)/shard_map/ppermute | solution.py:413
  50.5 15.1 %collective-permute-start.1 = (bf16[256,1024]{1,0:T(8,128)(2,1)}, bf16[256,1024]{1,0:T(8,128)(2,1)S(1)}, u32[]{:S(2)}, u32[]{:S(2)}) collective-permute-start(bf16[256,1024]{1,0:T(8,128)(2,1)} %get-tuple-element.28), channel_id=1, source_target_pairs={{0,4},{2,6},{4,0},{6,2},{8,12},{10,14},{12,8},{14,10},{16,20},{18,... | collective-permute-start | bytes 1572872 | tf_op jit(solution)/shard_map/ppermute | solution.py:410
  51.9 23.9 %collective-permute-start.2 = (bf16[256,1024]{1,0:T(8,128)(2,1)}, bf16[256,1024]{1,0:T(8,128)(2,1)S(1)}, u32[]{:S(2)}, u32[]{:S(2)}) collective-permute-start(bf16[256,1024]{1,0:T(8,128)(2,1)} %get-tuple-element.29), channel_id=1, source_target_pairs={{0,6},{2,4},{4,2},{6,0},{8,14},{10,12},{12,10},{14,8},{16,22},{18,... | collective-permute-start | bytes 1572872 | tf_op jit(solution)/shard_map/ppermute | solution.py:410
  65.5 45.0 %collective-permute-start.21 = (bf16[128,4096]{1,0:T(8,128)(2,1)S(1)}, bf16[128,4096]{1,0:T(8,128)(2,1)S(1)}, u32[]{:S(2)}, u32[]{:S(2)}) collective-permute-start(bf16[128,4096]{1,0:T(8,128)(2,1)S(1)} %copy-done.1), channel_id=1, source_target_pairs={{0,4},{2,6},{4,0},{6,2},{8,12},{10,14},{12,8},{14,10},{16,20},{18,... | collective-permute-start | bytes 3145736 | tf_op jit(solution)/shard_map/ppermute | solution.py:410
  67.0 71.7 %collective-permute-start.25 = (bf16[128,4096]{1,0:T(8,128)(2,1)S(1)}, bf16[128,4096]{1,0:T(8,128)(2,1)}, u32[]{:S(2)}, u32[]{:S(2)}) collective-permute-start(bf16[128,4096]{1,0:T(8,128)(2,1)S(1)} %collective-permute-done.23.refs_4_), channel_id=1, source_target_pairs={{0,4},{2,6},{4,0},{6,2},{8,12},{10,14},{12,8},{14,10},{16,20},{18,... | collective-permute-start | bytes 3145736 | tf_op jit(solution)/shard_map/ppermute | solution.py:410
  67.6 71.6 %collective-permute-start.16 = (bf16[4096,128]{1,0:T(8,128)(2,1)}, bf16[4096,128]{1,0:T(8,128)(2,1)}, u32[]{:S(2)}, u32[]{:S(2)}) collective-permute-start(bf16[4096,128]{1,0:T(8,128)(2,1)} %collective-permute-done.8.refs_9_), channel_id=1, source_target_pairs={{8,16},{10,18},{12,20},{14,22},{16,8},{18,10},{20,12},{22,14},{9,1... | collective-permute-start | bytes 3145736 | tf_op jit(solution)/shard_map/ppermute | solution.py:413
  69.2 70.1 %collective-permute-start.15 = (bf16[4096,128]{1,0:T(8,128)(2,1)}, bf16[4096,128]{1,0:T(8,128)(2,1)}, u32[]{:S(2)}, u32[]{:S(2)}) collective-permute-start(bf16[4096,128]{1,0:T(8,128)(2,1)} %collective-permute-done.9.refs_10_), channel_id=1, source_target_pairs={{8,0},{10,2},{12,4},{14,6},{16,24},{18,26},{20,28},{22,30},{9,1},{... | collective-permute-start | bytes 3145736 | tf_op jit(solution)/shard_map/ppermute | solution.py:413
  109.0 16.7 %collective-permute-start.13 = (bf16[512,256]{1,0:T(8,128)(2,1)S(1)}, bf16[512,256]{1,0:T(8,128)(2,1)S(1)}, u32[]{:S(2)}, u32[]{:S(2)}) collective-permute-start(bf16[512,256]{1,0:T(8,128)(2,1)S(1)} %get-tuple-element.39), channel_id=1, source_target_pairs={{8,0},{10,2},{12,4},{14,6},{16,8},{18,10},{20,12},{22,14},{24,16},... | collective-permute-start | bytes 786440 | tf_op jit(solution)/shard_map/ppermute | solution.py:413
  110.5 28.1 %collective-permute-start.14 = (bf16[512,256]{1,0:T(8,128)(2,1)S(1)}, bf16[512,256]{1,0:T(8,128)(2,1)S(1)}, u32[]{:S(2)}, u32[]{:S(2)}) collective-permute-start(bf16[512,256]{1,0:T(8,128)(2,1)S(1)} %get-tuple-element.40), channel_id=1, source_target_pairs={{16,0},{18,2},{20,4},{22,6},{24,8},{26,10},{28,12},{30,14},{17,1},... | collective-permute-start | bytes 786440 | tf_op jit(solution)/shard_map/ppermute | solution.py:413
  125.7 17.1 %collective-permute-start.20 = (bf16[128,4096]{1,0:T(8,128)(2,1)S(1)}, bf16[128,4096]{1,0:T(8,128)(2,1)}, u32[]{:S(2)}, u32[]{:S(2)}) collective-permute-start(bf16[128,4096]{1,0:T(8,128)(2,1)S(1)} %copy-done.1), channel_id=1, source_target_pairs={{0,2},{2,0},{4,6},{6,4},{8,10},{10,8},{12,14},{14,12},{16,18},{18,... | collective-permute-start | bytes 3145736 | tf_op jit(solution)/shard_map/ppermute | solution.py:410
  138.7 5.7 %collective-permute-start.24 = (bf16[128,4096]{1,0:T(8,128)(2,1)S(1)}, bf16[128,4096]{1,0:T(8,128)(2,1)}, u32[]{:S(2)}, u32[]{:S(2)}) collective-permute-start(bf16[128,4096]{1,0:T(8,128)(2,1)S(1)} %collective-permute-done.23.refs_4_), channel_id=1, source_target_pairs={{0,2},{2,0},{4,6},{6,4},{8,10},{10,8},{12,14},{14,12},{16,18},{18,... | collective-permute-start | bytes 3145736 | tf_op jit(solution)/shard_map/ppermute | solution.py:410
  139.1 6.8 %collective-permute-start.26 = (bf16[128,4096]{1,0:T(8,128)(2,1)}, bf16[128,4096]{1,0:T(8,128)(2,1)}, u32[]{:S(2)}, u32[]{:S(2)}) collective-permute-start(bf16[128,4096]{1,0:T(8,128)(2,1)} %collective-permute-done.25.refs_6_), channel_id=1, source_target_pairs={{0,2},{2,0},{4,6},{6,4},{8,10},{10,8},{12,14},{14,12},{16,18},{18,... | collective-permute-start | bytes 3145736 | tf_op jit(solution)/shard_map/ppermute | solution.py:410
  139.3 27.7 %collective-permute-start.27 = (bf16[4096,128]{1,0:T(8,128)(2,1)}, bf16[4096,128]{1,0:T(8,128)(2,1)}, u32[]{:S(2)}, u32[]{:S(2)}) collective-permute-start(bf16[4096,128]{1,0:T(8,128)(2,1)} %collective-permute-done.16.refs_3_.refs_12_), channel_id=1, source_target_pairs={{8,0},{10,2},{12,4},{14,6},{16,24},{18,26},{20,28},{22,30},{9,1},{... | collective-permute-start | bytes 3145736 | tf_op jit(solution)/shard_map/ppermute | solution.py:413
  143.2 43.7 %collective-permute-start.10 = (bf16[128,1024]{1,0:T(8,128)(2,1)}, bf16[128,1024]{1,0:T(8,128)(2,1)}, u32[]{:S(2)}, u32[]{:S(2)}) collective-permute-start(bf16[128,1024]{1,0:T(8,128)(2,1)} %copy-done.14), channel_id=1, source_target_pairs={{0,2},{2,0},{4,6},{6,4},{8,10},{10,8},{12,14},{14,12},{16,18},{18,... | collective-permute-start | bytes 786440 | tf_op jit(solution)/shard_map/ppermute | solution.py:410
  144.4 42.6 %collective-permute-start.11 = (bf16[128,1024]{1,0:T(8,128)(2,1)}, bf16[128,1024]{1,0:T(8,128)(2,1)}, u32[]{:S(2)}, u32[]{:S(2)}) collective-permute-start(bf16[128,1024]{1,0:T(8,128)(2,1)} %copy-done.13), channel_id=1, source_target_pairs={{0,4},{2,6},{4,0},{6,2},{8,12},{10,14},{12,8},{14,10},{16,20},{18,... | collective-permute-start | bytes 786440 | tf_op jit(solution)/shard_map/ppermute | solution.py:410
  144.7 42.4 %collective-permute-start.12 = (bf16[128,1024]{1,0:T(8,128)(2,1)S(1)}, bf16[128,1024]{1,0:T(8,128)(2,1)}, u32[]{:S(2)}, u32[]{:S(2)}) collective-permute-start(bf16[128,1024]{1,0:T(8,128)(2,1)S(1)} %copy-done.12), channel_id=1, source_target_pairs={{0,6},{2,4},{4,2},{6,0},{8,14},{10,12},{12,10},{14,8},{16,22},{18,... | collective-permute-start | bytes 786440 | tf_op jit(solution)/shard_map/ppermute | solution.py:410
  145.9 33.3 %collective-permute-start.30 = (bf16[512,128]{1,0:T(8,128)(2,1)}, bf16[512,128]{1,0:T(8,128)(2,1)S(1)}, u32[]{:S(2)}, u32[]{:S(2)}) collective-permute-start(bf16[512,128]{1,0:T(8,128)(2,1)} %get-tuple-element.50), channel_id=1, source_target_pairs={{0,3},{1,2},{2,1},{3,0},{4,7},{5,6},{6,5},{7,4},{8,11},{9,10},{10,... | collective-permute-start | bytes 393224 | tf_op jit(solution)/shard_map/ppermute | solution.py:425
  167.0 12.2 %collective-permute-start.29 = (bf16[512,128]{1,0:T(8,128)(2,1)}, bf16[512,128]{1,0:T(8,128)(2,1)S(1)}, u32[]{:S(2)}, u32[]{:S(2)}) collective-permute-start(bf16[512,128]{1,0:T(8,128)(2,1)} %get-tuple-element.49.g0), channel_id=1, source_target_pairs={{0,1},{1,0},{2,3},{3,2},{4,5},{5,4},{6,7},{7,6},{8,9},{9,8},{10,11... | collective-permute-start | bytes 393224 | tf_op jit(solution)/shard_map/ppermute | solution.py:421
  182.5 12.5 %all-to-all-start = ((f32[32,8,128]{2,1,0:T(8,128)}), f32[32,8,128]{2,1,0:T(8,128)S(1)}, u32[]{:S(2)}, u32[]{:S(2)}) async-start(f32[32,8,128]{2,1,0:T(8,128)} %broadcast_in_dim.2), calls=%async_computation | async-start | bytes 262144 | tf_op jit(solution)/shard_map/all_to_all | solution.py:467
  (31 other events, 380.3 us)

commit v2 on v1

--- a/solution.py
+++ b/solution.py
@@ -36,11 +36,21 @@
         copy.wait()
 
 
+def by_halves(outs, members):
+    half = max(members // 2, 1)
+    return [outs[r // half].at[r % half] for r in range(members)]
+
+
+def half_shapes(members, shape, dtype):
+    half = max(members // 2, 1)
+    return [jax.ShapeDtypeStruct((half,) + shape, dtype)] * (members // half)
+
+
 def pack_keys_kernel(members, per_head, place_ref, doc_ref, kv_ref, *outs):
     tok = kv_ref.shape[0]
     ids = (doc_ref[...] + 1).astype(F32)
     ids = jnp.concatenate([ids] * (2 * HD // tok), axis=1)
-    for r, out in enumerate(outs):
+    for r, out in enumerate(by_halves(outs, members)):
         head = head_of(place_ref[0] ^ r, members, per_head)
         out[:tok, :] = kv_ref[:, cols(head, 2 * HD)]
         out[tok:, :] = jnp.broadcast_to(ids, (DOC_ROWS, 2 * HD)).astype(BF16)
@@ -48,33 +58,36 @@
 
 def pack_keys(place, doc_ids, keyval, members, per_head):
     tok = keyval.shape[0]
+    shapes = half_shapes(members, (tok + DOC_ROWS, 2 * HD), BF16)
     return pl.pallas_call(
         functools.partial(pack_keys_kernel, members, per_head),
-        out_shape=[jax.ShapeDtypeStruct((tok + DOC_ROWS, 2 * HD), BF16)] * members,
+        out_shape=shapes,
         in_specs=[SMEM, VMEM, VMEM],
-        out_specs=[VMEM] * members,
+        out_specs=[VMEM] * len(shapes),
         name="pack_keys",
     )(place, doc_ids.reshape(1, tok), keyval)
 
 
-def pack_queries_kernel(members, per_head, width, place_ref, q_ref, o_ref, *outs):
+def pack_queries_kernel(members, per_head, width, n_after, place_ref, q_ref, o_ref, *refs):
+    outs = refs[n_after:]
     tok = q_ref.shape[0]
-    for r, out in enumerate(outs):
-        head = head_of(place_ref[0] ^ (r + 1), members, per_head)
+    for r, out in enumerate(by_halves(outs, members)):
+        if r == 0 and members > 2:
+            continue
+        head = head_of(place_ref[0] ^ r, members, per_head)
         out[:tok, :] = q_ref[:, cols(head, width)]
         out[tok:, :] = o_ref[:, cols(head, width)]
 
 
-def pack_queries(place, queries, grad_out, members, per_head, width):
-    if members == 1:
-        return []
-    return pl.pallas_call(
-        functools.partial(pack_queries_kernel, members, per_head, width),
-        out_shape=[jax.ShapeDtypeStruct((2 * queries.shape[0], width), BF16)] * (members - 1),
-        in_specs=[SMEM, VMEM, VMEM],
-        out_specs=[VMEM] * (members - 1),
+def pack_queries(place, queries, grad_out, members, per_head, width, after):
+    shapes = half_shapes(members, (2 * queries.shape[0], width), BF16)
+    return pl.pallas_call(
+        functools.partial(pack_queries_kernel, members, per_head, width, len(after)),
+        out_shape=shapes,
+        in_specs=[SMEM, VMEM, VMEM] + [ANY] * len(after),
+        out_specs=[VMEM] * len(shapes),
         name="pack_queries",
-    )(place, queries, grad_out)
+    )(place, queries, grad_out, *after)
 
 
 def split_kernel(place_ref, d_ref, mine_ref, theirs_ref):
@@ -94,16 +107,18 @@
     )(place, rows)
 
 
-def attention_kernel(members, per_head, group_size, tok, back, window, n_after, *refs):
+def attention_kernel(members, per_head, group_size, tok, back, window, qo_slots, n_after, *refs):
     n_kv = back + 1
     n_in = 2 + members + n_kv
     refs = refs[:n_in] + refs[n_in + n_after :]
     place_ref, q_ref, o_ref = refs[:3]
-    qo_refs = refs[3 : 2 + members]
+    qo_refs = [ref.at[k] for ref, k in zip(refs[3 : 2 + members], qo_slots, strict=True)]
     kv_refs = refs[2 + members : 2 + members + n_kv]
     outs = refs[2 + members + n_kv :]
-    dq_outs, own_out, prev_outs = outs[:members], outs[members], outs[members + 1 : members + 1 + back]
-    qs, dos, kvs, docs, k_t, bias, dqs, dk, dv, sems = outs[members + 1 + back :]
+    n_dq = min(members, 2)
+    dq_outs = by_halves(outs[:n_dq], members)
+    own_out, prev_outs = outs[n_dq], outs[n_dq + 1 : n_dq + 1 + back]
+    qs, dos, kvs, docs, k_t, bias, dqs, dk, dv, sems = outs[n_dq + 1 + back :]
     plane = members * tok
     me = place_ref[0]
     width = group_size * HD
@@ -210,14 +225,17 @@
     keys = (back + 1) * plane
     width = group_size * HD
     n_copies = 2 * members * len(kv) + 2 * members
-    flops = 40 * group_size * plane * span * HD
-    return pl.pallas_call(
-        functools.partial(attention_kernel, members, per_head, group_size, tok, back, window, len(after)),
-        out_shape=[jax.ShapeDtypeStruct((tok, width), BF16)] * members
+    flops = 2 * group_size * plane * span * HD
+    dq_shapes = half_shapes(members, (tok, width), BF16)
+    return pl.pallas_call(
+        functools.partial(
+            attention_kernel, members, per_head, group_size, tok, back, window, [k for _, k in qo], len(after)
+        ),
+        out_shape=dq_shapes
         + [jax.ShapeDtypeStruct((plane, 2 * HD), F32)]
         + [jax.ShapeDtypeStruct((plane, 2 * HD), BF16)] * back,
         in_specs=[SMEM] + [ANY] * (2 + len(qo) + len(kv) + len(after)),
-        out_specs=[ANY] * members + [VMEM] * (1 + back),
+        out_specs=[ANY] * len(dq_shapes) + [VMEM] * (1 + back),
         scratch_shapes=[
             pltpu.VMEM((plane, width), BF16),
             pltpu.VMEM((plane, width), BF16),
@@ -230,17 +248,17 @@
             pltpu.VMEM((keys, HD), F32),
             pltpu.SemaphoreType.DMA((n_copies,)),
         ],
-        compiler_params=pltpu.CompilerParams(vmem_limit_bytes=48 * 2**20),
+        compiler_params=pltpu.CompilerParams(vmem_limit_bytes=24 * 2**20),
         cost_estimate=pl.CostEstimate(
             flops=flops, bytes_accessed=6 * plane * width, transcendentals=group_size * plane * span
         ),
         name="attention_both_ways",
-    )(place, queries, grad_out, *qo, *kv, *after)
+    )(place, queries, grad_out, *[array for array, _ in qo], *kv, *after)
 
 
 def combine_kernel(members, tok, n_prev, place_ref, own_ref, *refs):
     prev, outs = refs[:n_prev], refs[n_prev:]
-    token_outs, part_outs = outs[:members], outs[members : members + 2]
+    token_outs, part_outs = by_halves(outs[:-3], members), outs[-3:-1]
     total = outs[-1]
     g = own_ref[...]
     for part in prev:
@@ -257,76 +275,71 @@
 def combine(place, own, prev, members, tok, after):
     plane = own.shape[0]
     n_after = len(after)
+    shapes = half_shapes(members, (tok, 2 * HD), BF16)
 
     def kernel(place_ref, own_ref, *refs):
         combine_kernel(members, tok, len(prev), place_ref, own_ref, *refs[: len(prev)], *refs[len(prev) + n_after :])
 
     return pl.pallas_call(
         kernel,
-        out_shape=[jax.ShapeDtypeStruct((tok, 2 * HD), BF16)] * members
-        + [jax.ShapeDtypeStruct((plane, HD), BF16)] * 2,
+        out_shape=shapes + [jax.ShapeDtypeStruct((plane, HD), BF16)] * 2,
         in_specs=[SMEM] + [VMEM] * (1 + len(prev)) + [ANY] * n_after,
-        out_specs=[VMEM] * (members + 2),
+        out_specs=[VMEM] * (len(shapes) + 2),
         scratch_shapes=[pltpu.VMEM((plane, 2 * HD), BF16)],
         name="sum_key_value_gradients",
     )(place, own, *prev, *after)
 
 
-def settle_kernel(members, per_head, place_ref, *refs):
-    dq, dkv = refs[:members], refs[members : 2 * members]
+def settle_kernel(members, per_head, slots, place_ref, *refs):
+    pieces = [ref.at[k] for ref, k in zip(refs[: 2 * members], slots, strict=True)]
     out_q, out_kv = refs[2 * members :]
     for r in range(members):
         head = head_of(place_ref[0] ^ r, members, per_head)
-        out_q[:, cols(head, dq[r].shape[1])] = dq[r][...]
-        out_kv[:, cols(head, dkv[r].shape[1])] = dkv[r][...]
+        for piece, out in ((pieces[r], out_q), (pieces[members + r], out_kv)):
+            out[:, cols(head, piece.shape[1])] = piece[...]
 
 
 def settle(place, dq, dkv, per_head):
     members = len(dq)
-    tok = dq[0].shape[0]
-    return pl.pallas_call(
-        functools.partial(settle_kernel, members, per_head),
+    tok = dq[0][0].shape[1]
+    pieces = dq + dkv
+    return pl.pallas_call(
+        functools.partial(settle_kernel, members, per_head, [k for _, k in pieces]),
         out_shape=[
-            jax.ShapeDtypeStruct((tok, members * dq[0].shape[1]), BF16),
-            jax.ShapeDtypeStruct((tok, members * dkv[0].shape[1]), BF16),
+            jax.ShapeDtypeStruct((tok, members * part[0][0].shape[2]), BF16) for part in (dq, dkv)
         ],
         in_specs=[SMEM] + [VMEM] * (2 * members),
         out_specs=[VMEM, VMEM],
         name="place_heads",
-    )(place, *dq, *dkv)
-
-
-def project_kernel(place_ref, *refs):
-    d_refs, (w0, wa, wb0, wb1, wc0, wc1, out_ref, ds, ws, sems) = refs[:8], refs[8:]
+    )(place, *[array for array, _ in pieces])
+
+
+def project_kernel(slots, counts, place_ref, *refs):
+    n_pieces, n_blocks = len(slots), sum(counts)
+    d_refs = [ref.at[k] for ref, k in zip(refs[:n_pieces], slots, strict=True)]
+    w_refs = refs[n_pieces : n_pieces + n_blocks]
+    out_ref, ds, ws, sems = refs[n_pieces + n_blocks :]
     me, plane_at = place_ref[0], place_ref[2]
     tok = d_refs[0].shape[0]
     inner = jnp.logical_or(plane_at == 1, plane_at == 2)
-    w_copies = []
-    for k, pair in enumerate(((w0, w0), (wa, wa), (wb0, wb1), (wc0, wc1))):
+    copies = []
+    at = 0
+    for k, count in enumerate(counts):
         dst = ws.at[:, k * HD : (k + 1) * HD]
-        if pair[0] is pair[1]:
-            copy = pltpu.make_async_copy(pair[0], dst, sems.at[k])
-            copy.start()
+        copies.append(pltpu.make_async_copy(w_refs[at], dst, sems.at[k]))
+        if count == 1:
+            copies[k].start()
         else:
-            copy = pltpu.make_async_copy(pair[1], dst, sems.at[k])
-
-            @pl.when(inner)
-            def _():
-                pltpu.make_async_copy(pair[0], dst, sems.at[k]).start()
-
-            @pl.when(jnp.logical_not(inner))
-            def _():
-                copy.start()
-
-        w_copies.append(copy)
-    copies = []
-    for layer in range(2):
-        for r in range(4):
-            shard = layer * 4 + (me ^ r)
-            dst = ds.at[pl.ds(pl.multiple_of(shard * tok, tok), tok), :]
-            copies.append(pltpu.make_async_copy(d_refs[layer * 4 + r], dst, sems.at[4 + len(copies)]))
-            copies[-1].start()
-    for copy in w_copies + copies:
+            from_end = pltpu.make_async_copy(w_refs[at + 1], dst, sems.at[k])
+            pl.when(inner)(copies[k].start)
+            pl.when(jnp.logical_not(inner))(from_end.start)
+        at += count
+    for i, d_ref in enumerate(d_refs):
+        shard = i // 4 * 4 + (me ^ (i % 4))
+        dst = ds.at[pl.ds(pl.multiple_of(shard * tok, tok), tok), :]
+        copies.append(pltpu.make_async_copy(d_ref, dst, sems.at[len(copies)]))
+        copies[-1].start()
+    for copy in copies:
         copy.wait()
     step = 256
 
@@ -339,27 +352,28 @@
 
 
 def project(place, pieces, blocks):
-    tok, depth = pieces[0].shape
-    rows = tok * len(pieces)
-    return pl.pallas_call(
-        project_kernel,
-        out_shape=jax.ShapeDtypeStruct((rows, 4 * HD), F32),
-        in_specs=[SMEM] + [ANY] * (len(pieces) + len(blocks)),
+    _, tok, depth = pieces[0][0].shape
+    rows, width = tok * len(pieces), HD * len(blocks)
+    arrays = [array for block in blocks for array in block]
+    return pl.pallas_call(
+        functools.partial(project_kernel, [k for _, k in pieces], [len(block) for block in blocks]),
+        out_shape=jax.ShapeDtypeStruct((rows, width), F32),
+        in_specs=[SMEM] + [ANY] * (len(pieces) + len(arrays)),
         out_specs=VMEM,
         scratch_shapes=[
             pltpu.VMEM((rows, depth), BF16),
-            pltpu.VMEM((depth, 4 * HD), BF16),
-            pltpu.SemaphoreType.DMA((4 + len(pieces),)),
+            pltpu.VMEM((depth, width), BF16),
+            pltpu.SemaphoreType.DMA((len(blocks) + len(pieces),)),
         ],
-        compiler_params=pltpu.CompilerParams(vmem_limit_bytes=48 * 2**20),
+        compiler_params=pltpu.CompilerParams(vmem_limit_bytes=20 * 2**20),
         cost_estimate=pl.CostEstimate(
-            flops=2 * rows * depth * 4 * HD, bytes_accessed=2 * depth * (rows + 4 * HD), transcendentals=0
+            flops=2 * rows * depth * width, bytes_accessed=2 * depth * (rows + width), transcendentals=0
         ),
         name="project_deltas",
-    )(place, *pieces, *blocks)
-
-
-def contract_kernel(norm, place_ref, slot_ref, p_ref, g0, g1, g2, g3, out_ref):
+    )(place, *[array for array, _ in pieces], *arrays)
+
+
+def contract_kernel(norm, place_ref, slot_ref, p_ref, p_last_ref, g0, g1, g2, g3, out_ref):
     me, side, plane_at = place_ref[0], place_ref[1], place_ref[2]
     kind = lax.rem(me, 2)
     row = lax.broadcasted_iota(jnp.int32, out_ref.shape, 0)
@@ -374,7 +388,8 @@
         )
         g = g_ref[...].astype(F32)
         for layer in range(2):
-            part = p_ref[layer * n_tok : (layer + 1) * n_tok, cols(slot, HD)] * g
+            rows = slice(layer * n_tok, (layer + 1) * n_tok)
+            part = jnp.where(slot == 3, p_last_ref[rows, :], p_ref[rows, cols(jnp.minimum(slot, 2), HD)]) * g
             value = jnp.sum(jnp.sum(part, axis=0, keepdims=True), axis=1, keepdims=True) * norm
             here = (row == slot_ref[side ^ layer]) & (lane == 4 * block + me)
             total = total + jnp.where(here, value, 0.0)
@@ -385,11 +400,11 @@
     return pl.pallas_call(
         functools.partial(contract_kernel, norm),
         out_shape=jax.ShapeDtypeStruct((8, HD), F32),
-        in_specs=[SMEM, SMEM] + [VMEM] * 5,
+        in_specs=[SMEM, SMEM] + [VMEM] * 6,
         out_specs=VMEM,
-        compiler_params=pltpu.CompilerParams(vmem_limit_bytes=32 * 2**20),
+        compiler_params=pltpu.CompilerParams(vmem_limit_bytes=16 * 2**20),
         name="contract_scores",
-    )(place, layer_slot, projected, *parts)
+    )(place, layer_slot, *projected, *parts)
 
 
 def on_device(queries, keyval, grad_out, doc_ids, deltas, node_weights, layer_slot):
@@ -424,44 +439,69 @@
         pairs = [(2 * s + h, 2 * (s ^ 1) + (h ^ 1)) for s in range(n_seq) for h in range(2)]
         return lax.ppermute(x, ("seq", "head"), pairs)
 
+    def follow(x, after):
+        return lax.optimization_barrier((x, *after))[0] if after else x
+
+    def exchange(halves, before=(), between=()):
+        if members == 1:
+            return [(halves[0], 0)]
+        bit = members // 2
+        got = to_member(follow(halves[1], before), bit)
+        views = [(halves[0], r) for r in range(bit)] + [(got, r) for r in range(bit)]
+        while bit > 1:
+            bit //= 2
+            chosen = [r for r in range(members) if r & bit]
+            message = jnp.stack([views[r][0][views[r][1]] for r in chosen])
+            got = to_member(follow(message, between), bit)
+            for k, r in enumerate(chosen):
+                views[r] = (got, k)
+        return views
+
     spread = n_head == 2 and members == 4 and planes == 4 and per_head == 2 and deltas.shape[0] == 1
-    if spread:
-        w_pair = to_plane(node_weights, [(0, 1), (1, 0), (2, 3), (3, 2)])
-        w_mid = to_plane(node_weights, [(1, 2), (2, 1)])
-
-    packed = pack_keys(place, doc_ids, keyval, members, per_head)
-    kv_pieces = [packed[0]] + [to_member(packed[r], r) for r in range(1, members)]
-    packed = pack_queries(place, queries, grad_out, members, per_head, group_size * HD)
-    qo = [to_member(packed[r - 1], r) for r in range(1, members)]
-    kv_plane = jnp.stack(kv_pieces)
-    kv = [kv_plane] + [shift(kv_plane, k) for k in range(1, back + 1)]
-
     first, second = [], []
     if spread:
+        pairs, middle, ends = [(0, 1), (1, 0), (2, 3), (3, 2)], [(1, 2), (2, 1)], [(1, 0), (2, 3)]
+        w_pair, w_middle = to_plane(node_weights, pairs), to_plane(node_weights, middle)
+        first = [w_pair, w_middle]
         mine, theirs = split_width(place, deltas.reshape(tok, deltas.shape[2]))
         crossed = other_head(theirs)
-        near = [mine, to_member(mine, 2), crossed, to_member(crossed, 2)]
-        far = [to_member(d, 1) for d in near]
-        pieces = [near[0], far[0], near[1], far[1], near[2], far[2], near[3], far[3]]
-        w_end = to_plane(w_mid, [(1, 0), (2, 3)])
-        w_mid2 = to_plane(w_pair, [(1, 2), (2, 1)])
-        w_end2 = to_plane(w_mid2, [(1, 0), (2, 3)])
-        first = [w_pair, w_mid]
-        second = [w_end, w_mid2]
-
-    out = attention(place, queries, grad_out, qo, kv, members, per_head, group_size, window, first)
-    dq, own, prev = out[:members], out[members], out[members + 1 :]
-    prev = [shift(prev[k], -(k + 1)) for k in range(back)]
-    dq = [dq[0]] + [to_member(dq[r], r) for r in range(1, members)]
-    summed = combine(place, own, prev, members, tok, second)
-    token_parts, kinds = summed[:members], summed[members:]
+
+    keys = exchange(pack_keys(place, doc_ids, keyval, members, per_head))
+    kv_plane = jnp.stack([array[k] for array, k in keys])
+    ready = follow(kv_plane, first)
+    kv = [kv_plane] + [shift(ready, k) for k in range(1, back + 1)]
+    queries_out = pack_queries(place, queries, grad_out, members, per_head, group_size * HD, ())
+    qo = exchange(queries_out, [array for array, _ in keys[1:]], kv[1:])
+
+    if spread:
+        near = jnp.stack([mine, crossed])
+        other = to_member(follow(near, [qo[-2][0]] + kv[1:]), 2)
+        near_c = to_member(near, 1)
+        w_ends = to_plane(follow(w_middle, kv[1:]), ends)
+        w_middle2 = to_plane(follow(w_pair, kv[1:]), middle)
+        w_ends2 = to_plane(w_middle2, ends)
+        second = [w_ends, w_middle2]
+
+    out = attention(place, queries, grad_out, qo[1:], kv, members, per_head, group_size, window, ())
+    n_dq = min(members, 2)
+    dq, own, prev = out[:n_dq], out[n_dq], out[n_dq + 1 :]
+    prev = [shift(follow(prev[k], second), -(k + 1)) for k in range(back)]
+    dq = exchange(dq)
+    if spread:
+        other_c = to_member(follow(other, prev), 1)
+        pieces = [(array, layer) for layer in range(2) for array in (near, near_c, other, other_c)]
+    summed = combine(place, own, prev, members, tok, ())
+    token_parts, kinds = summed[:-2], summed[-2:]
     if spread:
         parts = [kinds[0], to_member(kinds[1], 1), other_head(kinds[0]), other_head_and_member(kinds[1])]
-    dkv = [token_parts[0]] + [to_member(token_parts[r], r) for r in range(1, members)]
+    dkv = exchange(token_parts)
     grad_query, grad_keyval = settle(place, dq, dkv, per_head)
     norm = 1.0 / math.sqrt(n_seq * tok)
     if spread:
-        projected = project(place, pieces, [node_weights, w_pair, w_mid, w_end, w_mid2, w_end2])
+        projected = [
+            project(place, pieces, [(node_weights,), (w_pair,), (w_middle, w_ends)]),
+            project(place, pieces, [(w_middle2, w_ends2)]),
+        ]
         mine = contract(place, layer_slot, projected, parts, norm)
         n_dev = n_seq * n_head
         copies = lax.all_to_all(

time: 196 us -> 174 us (0.89)
  waiting for transfers between devices: 95.1 us -> 70.2 us
  Pallas kernels: 52.7 us -> 58 us
  starting transfers between devices: 36.8 us -> 33.6 us
    ppermute x9, waiting for transfers between devices: 65.8 us -> 51.4 us  [to_plane(): lax.ppermute(x, 'seq', [(a * members + k, b * members + k) for a, b in pa...]
    ppermute x19 -> x12, waiting for transfers between devices: 29.3 us -> 15.9 us  [to_member(): lax.ppermute(x, 'seq', [(s, s - s % members + (s % members ^ r)) for s in...]
    ppermute x19 -> x12, starting transfers between devices: 11.5 us -> 5.82 us  [to_member(): lax.ppermute(x, 'seq', [(s, s - s % members + (s % members ^ r)) for s in...]
    pallas_call x3 -> x4, Pallas kernels: 15.3 us -> 20.6 us  [the longest x2 15.6 us: project(): pl.pallas_call(functools.partial(project_kernel, [k for _, k in pieces],...]
    ppermute x9, starting transfers between devices: 18 us -> 21.5 us  [to_plane(): lax.ppermute(x, 'seq', [(a * members + k, b * members + k) for a, b in pa...]
    all_to_all x1, waiting for transfers between devices: 0.01 us -> 2.83 us  [on_device(): lax.all_to_all(jnp.broadcast_to(mine[None], (n_dev,) + mine.shape), ('seq...]
    unnamed x46 -> x42, local copies, waits for them, and re-layouts: 7.35 us -> 5.44 us
  transfers between devices with their start and end apart: 32 -> 25, of which waited for: 12 -> 10; matrix products, arithmetic and copies ran while one was open for 0% -> 3% of each run, Pallas kernels for 26% -> 33%
where the time goes in v2:
time: 174 us
  waiting for transfers between devices  70.2 us (40%)
  Pallas kernels  58 us (33%)
  starting transfers between devices  33.6 us (19%)
  local copies, waits for them, and re-layouts  7.78 us (4%)
  other arithmetic  3.23 us (2%)
    ppermute x9, waiting for transfers between devices, to_plane(): lax.ppermute(x, 'seq', [(a * members + k, b * members + k) for a, b in pa...  51.4 us
    pallas_call x1, Pallas kernels, attention(): pl.pallas_call(functools.partial(attention_kernel, members, per_head, gro...  28.6 us
    ppermute x9, starting transfers between devices, to_plane(): lax.ppermute(x, 'seq', [(a * members + k, b * members + k) for a, b in pa...  21.5 us
    ppermute x12, waiting for transfers between devices, to_member(): lax.ppermute(x, 'seq', [(s, s - s % members + (s % members ^ r)) for s in...  15.9 us
    pallas_call x2, Pallas kernels, project(): pl.pallas_call(functools.partial(project_kernel, [k for _, k in pieces],...  15.6 us
    ppermute x12, starting transfers between devices, to_member(): lax.ppermute(x, 'seq', [(s, s - s % members + (s % members ^ r)) for s in...  5.82 us
    unnamed x42, local copies, waits for them, and re-layouts  5.44 us
  transfers between devices with their start and end apart: 25, of which 10 were waited for; matrix products, arithmetic and copies ran while one was open for 3% of the time, Pallas kernels for 33%

profile of v2, /device:TPU:0, one launch (start us, length us, event | category | flops | bytes accessed | tf_op | source)
XLA Modules:
  0.0 173.8 jit_solution(8964697133246080868)
XLA Ops:
  0.6 3.1 %collective-permute-start.3 = (bf16[4096,128]{1,0:T(8,128)(2,1)}, bf16[4096,128]{1,0:T(8,128)(2,1)}, u32[]{:S(2)}, u32[]{:S(2)}) collective-permute-start(bf16[4096,128]{1,0:T(8,128)(2,1)} %refs_8_.1), channel_id=1, source_target_pairs={{0,8},{2,10},{4,12},{6,14},{8,0},{10,2},{12,4},{14,6},{16,24},{18,... | collective-permute-start | bytes 3145736 | tf_op jit(solution)/shard_map/ppermute | solution.py:428
  3.7 1.7 collective-permute-start.4
  6.1 1.7 pack_keys.1
  7.8 1.5 collective-permute-start
  9.3 3.0 %split_deltas.1 = (bf16[128,4096]{1,0:T(8,128)(2,1)}, bf16[128,4096]{1,0:T(8,128)(2,1)}) custom-call(s32[3]{0:T(128)} %pad_add_fusion.place_ref.refs_0_, bf16[128,8192]{1,0:T(8,128)(2,1)} %bitcast.7), custom_call_target="tpu_custom_call" | custom-call | tf_op jit(solution)/shard_map/split_deltas/pallas_call | solution.py:101
  14.0 3.0 %pack_queries.1 = (bf16[2,256,1024]{2,1,0:T(8,128)(2,1)}, bf16[2,256,1024]{2,1,0:T(8,128)(2,1)}) custom-call(s32[3]{0:T(128)} %pad_add_fusion.place_ref.refs_0_, bf16[128,4096]{1,0:T(8,128)(2,1)} %refs_1_.1, bf16[128,4096]{1,0:T(8,128)(2,1)} %refs_2_.1), custom_call_target="tpu_custom_call" | custom-call | tf_op jit(solution)/shard_map/pack_queries/pallas_call | solution.py:84
  18.0 9.2 %collective-permute-done.3.refs_9_ = bf16[4096,128]{1,0:T(8,128)(2,1)} collective-permute-done((bf16[4096,128]{1,0:T(8,128)(2,1)}, bf16[4096,128]{1,0:T(8,128)(2,1)}, u32[]{:S(2)}, u32[]{:S(2)}) %collective-permute-start.3) | collective-permute-done | bytes 1048608 | tf_op jit(solution)/shard_map/ppermute | solution.py:428
  27.2 6.7 %collective-permute-start.5 = (bf16[4,144,256]{2,1,0:T(8,128)(2,1)S(1)}, bf16[4,144,256]{2,1,0:T(8,128)(2,1)S(1)}, u32[]{:S(2)}, u32[]{:S(2)}) collective-permute-start(bf16[4,144,256]{2,1,0:T(8,128)(2,1)S(1)} %pad_maximum_fusion.3.refs_6_), channel_id=1, source_target_pairs={{0,8},{2,10},{4,12},{6,14},{8,16},{10,18},{12,20},{14,22},{16,24},... | collective-permute-start | bytes 884744 | tf_op jit(solution)/shard_map/ppermute | solution.py:428
  33.9 3.1 %collective-permute-start.6 = (bf16[4,144,256]{2,1,0:T(8,128)(2,1)S(1)}, bf16[4,144,256]{2,1,0:T(8,128)(2,1)S(1)}, u32[]{:S(2)}, u32[]{:S(2)}) collective-permute-start(bf16[4,144,256]{2,1,0:T(8,128)(2,1)S(1)} %pad_maximum_fusion.3.refs_6_), channel_id=1, source_target_pairs={{0,16},{2,18},{4,20},{6,22},{8,24},{10,26},{12,28},{14,30},{1,17},... | collective-permute-start | bytes 884744 | tf_op jit(solution)/shard_map/ppermute | solution.py:428
  39.5 3.3 %collective-permute-done.2.refs_4_ = bf16[2,256,1024]{2,1,0:T(8,128)(2,1)S(1)} collective-permute-done((bf16[2,256,1024]{2,1,0:T(8,128)(2,1)}, bf16[2,256,1024]{2,1,0:T(8,128)(2,1)S(1)}, u32[]{:S(2)}, u32[]{:S(2)}) %collective-permute-start.2) | collective-permute-done | bytes 1048608 | tf_op jit(solution)/shard_map/ppermute | solution.py:425
  42.8 2.8 %collective-permute-done.6.refs_8_ = bf16[4,144,256]{2,1,0:T(8,128)(2,1)S(1)} collective-permute-done((bf16[4,144,256]{2,1,0:T(8,128)(2,1)S(1)}, bf16[4,144,256]{2,1,0:T(8,128)(2,1)S(1)}, u32[]{:S(2)}, u32[]{:S(2)}) %collective-permute-start.6) | collective-permute-done | bytes 294944 | tf_op jit(solution)/shard_map/ppermute | solution.py:428
  45.6 1.5 collective-permute-start.18
  48.8 1.6 collective-permute-start.11
  50.5 28.6 %attention_both_ways.1 = (bf16[2,128,1024]{2,1,0:T(8,128)(2,1)S(1)}, bf16[2,128,1024]{2,1,0:T(8,128)(2,1)S(1)}, f32[512,256]{1,0:T(8,128)S(1)}, bf16[512,256]{1,0:T(8,128)(2,1)S(1)}, bf16[512,256]{1,0:T(8,128)(2,1)S(1)}) custom-call(s32[3]{0:T(128)S(1)} %copy-done.8, bf16[128,4096]{1,0:T(8,128)(2,1)S(1)} %copy-done.4, bf16[128,4096]{1,0:T(8,128)(2,1)S(1)} %copy-done.5, ...), custom_call_target="tpu_custom_call" | custom-call | flops 1342177280 | bytes 3145728 | tf_op jit(solution)/shard_map/attention_both_ways/pallas_call | solution.py:230
  84.0 17.7 %collective-permute-done.12.refs_0_ = bf16[512,256]{1,0:T(8,128)(2,1)S(1)} collective-permute-done((bf16[512,256]{1,0:T(8,128)(2,1)S(1)}, bf16[512,256]{1,0:T(8,128)(2,1)S(1)}, u32[]{:S(2)}, u32[]{:S(2)}) %collective-permute-start.12) | collective-permute-done | bytes 262176 | tf_op jit(solution)/shard_map/ppermute | solution.py:428
  101.7 12.4 %collective-permute-done.13.refs_1_ = bf16[512,256]{1,0:T(8,128)(2,1)S(1)} collective-permute-done((bf16[512,256]{1,0:T(8,128)(2,1)S(1)}, bf16[512,256]{1,0:T(8,128)(2,1)S(1)}, u32[]{:S(2)}, u32[]{:S(2)}) %collective-permute-start.13) | collective-permute-done | bytes 262176 | tf_op jit(solution)/shard_map/ppermute | solution.py:428
  116.0 2.2 %sum_key_value_gradients.1 = (bf16[2,128,256]{2,1,0:T(8,128)(2,1)}, bf16[2,128,256]{2,1,0:T(8,128)(2,1)}, bf16[512,128]{1,0:T(8,128)(2,1)}, bf16[512,128]{1,0:T(8,128)(2,1)}) custom-call(s32[3]{0:T(128)} %pad_add_fusion.place_ref.refs_0_, f32[512,256]{1,0:T(8,128)} %copy-done.6, bf16[512,256]{1,0:T(8,128)(2,1)} %copy-done.18, bf16[512,256]{1,0:T(8,128)(2,1)} %copy-done.19), custom_call_target="tpu_custom_call" | custom-call | tf_op jit(solution)/shard_map/sum_key_value_gradients/pallas_call | solution.py:283
  118.4 11.5 %collective-permute-done.8.refs_2_ = bf16[2,128,1024]{2,1,0:T(8,128)(2,1)} collective-permute-done((bf16[2,128,1024]{2,1,0:T(8,128)(2,1)S(1)}, bf16[2,128,1024]{2,1,0:T(8,128)(2,1)}, u32[]{:S(2)}, u32[]{:S(2)}) %collective-permute-start.8) | collective-permute-done | bytes 524320 | tf_op jit(solution)/shard_map/ppermute | solution.py:425
  133.0 8.8 %collective-permute-done.20.refs_9_ = bf16[4096,128]{1,0:T(8,128)(2,1)} collective-permute-done((bf16[4096,128]{1,0:T(8,128)(2,1)}, bf16[4096,128]{1,0:T(8,128)(2,1)}, u32[]{:S(2)}, u32[]{:S(2)}) %collective-permute-start.20) | collective-permute-done | bytes 1048608 | tf_op jit(solution)/shard_map/ppermute | solution.py:428
  144.6 9.0 %project_deltas.2.p_ref = f32[1024,384]{1,0:T(8,128)S(1)} custom-call(s32[3]{0:T(128)S(1)} %copy-done.9, bf16[2,128,4096]{2,1,0:T(8,128)(2,1)S(1)} %pad_maximum_fusion.refs_0_.refs_4_, bf16[2,128,4096]{2,1,0:T(8,128)(2,1)} %collective-permute-done.17.refs_1_.refs_5_, bf16[2,128,4096]{2,1,0:T(8,128)(2,1)} %collective-permute-done.18.refs_2_.refs_6_, ...), custom_call_target="tpu_custom_call" | custom-call | flops 3221225472 | bytes 11534336 | tf_op jit(solution)/shard_map/project_deltas/pallas_call | solution.py:358
  153.7 6.6 %project_deltas.3.p_last_ref = f32[1024,128]{1,0:T(8,128)S(1)} custom-call(s32[3]{0:T(128)S(1)} %copy-done.9, bf16[2,128,4096]{2,1,0:T(8,128)(2,1)S(1)} %pad_maximum_fusion.refs_0_.refs_4_, bf16[2,128,4096]{2,1,0:T(8,128)(2,1)} %collective-permute-done.17.refs_1_.refs_5_, bf16[2,128,4096]{2,1,0:T(8,128)(2,1)} %collective-permute-done.18.refs_2_.refs_6_, ...), custom_call_target="tpu_custom_call" | custom-call | flops 1073741824 | bytes 9437184 | tf_op jit(solution)/shard_map/project_deltas/pallas_call | solution.py:358
  162.0 2.6 %all-to-all-start = ((f32[32,8,128]{2,1,0:T(8,128)}), f32[32,8,128]{2,1,0:T(8,128)S(1)}, u32[]{:S(2)}, u32[]{:S(2)}) async-start(f32[32,8,128]{2,1,0:T(8,128)} %broadcast_in_dim.2), calls=%async_computation | async-start | bytes 262144 | tf_op jit(solution)/shard_map/all_to_all | solution.py:507
  167.5 2.9 %place_heads.1 = (bf16[128,4096]{1,0:T(8,128)(2,1)}, bf16[128,1024]{1,0:T(8,128)(2,1)}) custom-call(s32[3]{0:T(128)} %pad_add_fusion.place_ref.refs_0_, bf16[2,128,1024]{2,1,0:T(8,128)(2,1)} %copy-done, bf16[2,128,1024]{2,1,0:T(8,128)(2,1)} %copy-done.11, bf16[2,128,1024]{2,1,0:T(8,128)(2,1)} %collective-permute-done.8.refs_2_, ...), custom_call_target="tpu_custom_call" | custom-call | tf_op jit(solution)/shard_map/place_heads/pallas_call | solution.py:306
  170.3 2.8 %all-to-all-done = f32[32,8,128]{2,1,0:T(8,128)S(1)} async-done(((f32[32,8,128]{2,1,0:T(8,128)}), f32[32,8,128]{2,1,0:T(8,128)S(1)}, u32[]{:S(2)}, u32[]{:S(2)}) %all-to-all-start) | async-done | bytes 131104 | tf_op jit(solution)/shard_map/all_to_all | solution.py:507
  (96 shorter events, 25.5 us)
Async XLA Ops:
  0.6 26.6 %collective-permute-start.3 = (bf16[4096,128]{1,0:T(8,128)(2,1)}, bf16[4096,128]{1,0:T(8,128)(2,1)}, u32[]{:S(2)}, u32[]{:S(2)}) collective-permute-start(bf16[4096,128]{1,0:T(8,128)(2,1)} %refs_8_.1), channel_id=1, source_target_pairs={{0,8},{2,10},{4,12},{6,14},{8,0},{10,2},{12,4},{14,6},{16,24},{18,... | collective-permute-start | bytes 3145736 | tf_op jit(solution)/shard_map/ppermute | solution.py:428
  3.7 23.5 %collective-permute-start.4 = (bf16[4096,128]{1,0:T(8,128)(2,1)}, bf16[4096,128]{1,0:T(8,128)(2,1)}, u32[]{:S(2)}, u32[]{:S(2)}) collective-permute-start(bf16[4096,128]{1,0:T(8,128)(2,1)} %refs_8_.1), channel_id=1, source_target_pairs={{8,16},{10,18},{12,20},{14,22},{16,8},{18,10},{20,12},{22,14},{9,1... | collective-permute-start | bytes 3145736 | tf_op jit(solution)/shard_map/ppermute | solution.py:428
  7.8 6.1 %collective-permute-start = (bf16[2,144,256]{2,1,0:T(8,128)(2,1)}, bf16[2,144,256]{2,1,0:T(8,128)(2,1)S(1)}, u32[]{:S(2)}, u32[]{:S(2)}) collective-permute-start(bf16[2,144,256]{2,1,0:T(8,128)(2,1)} %get-tuple-element.32), channel_id=1, source_target_pairs={{0,4},{2,6},{4,0},{6,2},{8,12},{10,14},{12,8},{14,10},{16,20},{18,... | collective-permute-start | bytes 442376 | tf_op jit(solution)/shard_map/ppermute | solution.py:425
  12.3 24.6 %collective-permute-start.16 = (bf16[128,4096]{1,0:T(8,128)(2,1)}, bf16[128,4096]{1,0:T(8,128)(2,1)S(1)}, u32[]{:S(2)}, u32[]{:S(2)}) collective-permute-start(bf16[128,4096]{1,0:T(8,128)(2,1)} %get-tuple-element.50), channel_id=1, source_target_pairs={{0,1},{1,0},{2,3},{3,2},{4,5},{5,4},{6,7},{7,6},{8,9},{9,8},{10,11... | collective-permute-start | bytes 3145736 | tf_op jit(solution)/shard_map/ppermute | solution.py:436
  13.9 3.1 %collective-permute-start.1 = (bf16[2,144,256]{2,1,0:T(8,128)(2,1)S(1)}, bf16[2,144,256]{2,1,0:T(8,128)(2,1)S(1)}, u32[]{:S(2)}, u32[]{:S(2)}) collective-permute-start(bf16[2,144,256]{2,1,0:T(8,128)(2,1)S(1)} %pad_maximum_fusion.4), channel_id=1, source_target_pairs={{0,2},{2,0},{4,6},{6,4},{8,10},{10,8},{12,14},{14,12},{16,18},{18,... | collective-permute-start | bytes 442376 | tf_op jit(solution)/shard_map/ppermute | solution.py:425
  17.0 25.8 %collective-permute-start.2 = (bf16[2,256,1024]{2,1,0:T(8,128)(2,1)}, bf16[2,256,1024]{2,1,0:T(8,128)(2,1)S(1)}, u32[]{:S(2)}, u32[]{:S(2)}) collective-permute-start(bf16[2,256,1024]{2,1,0:T(8,128)(2,1)} %get-tuple-element.33), channel_id=1, source_target_pairs={{0,4},{2,6},{4,0},{6,2},{8,12},{10,14},{12,8},{14,10},{16,20},{18,... | collective-permute-start | bytes 3145736 | tf_op jit(solution)/shard_map/ppermute | solution.py:425
  27.2 15.6 %collective-permute-start.5 = (bf16[4,144,256]{2,1,0:T(8,128)(2,1)S(1)}, bf16[4,144,256]{2,1,0:T(8,128)(2,1)S(1)}, u32[]{:S(2)}, u32[]{:S(2)}) collective-permute-start(bf16[4,144,256]{2,1,0:T(8,128)(2,1)S(1)} %pad_maximum_fusion.3.refs_6_), channel_id=1, source_target_pairs={{0,8},{2,10},{4,12},{6,14},{8,16},{10,18},{12,20},{14,22},{16,24},... | collective-permute-start | bytes 884744 | tf_op jit(solution)/shard_map/ppermute | solution.py:428
  33.9 11.7 %collective-permute-start.6 = (bf16[4,144,256]{2,1,0:T(8,128)(2,1)S(1)}, bf16[4,144,256]{2,1,0:T(8,128)(2,1)S(1)}, u32[]{:S(2)}, u32[]{:S(2)}) collective-permute-start(bf16[4,144,256]{2,1,0:T(8,128)(2,1)S(1)} %pad_maximum_fusion.3.refs_6_), channel_id=1, source_target_pairs={{0,16},{2,18},{4,20},{6,22},{8,24},{10,26},{12,28},{14,30},{1,17},... | collective-permute-start | bytes 884744 | tf_op jit(solution)/shard_map/ppermute | solution.py:428
  45.6 68.5 %collective-permute-start.18 = (bf16[2,128,4096]{2,1,0:T(8,128)(2,1)S(1)}, bf16[2,128,4096]{2,1,0:T(8,128)(2,1)}, u32[]{:S(2)}, u32[]{:S(2)}) collective-permute-start(bf16[2,128,4096]{2,1,0:T(8,128)(2,1)S(1)} %pad_maximum_fusion.refs_0_.refs_4_), channel_id=1, source_target_pairs={{0,4},{2,6},{4,0},{6,2},{8,12},{10,14},{12,8},{14,10},{16,20},{18,... | collective-permute-start | bytes 6291464 | tf_op jit(solution)/shard_map/ppermute | solution.py:425
  47.3 3.1 %collective-permute-start.7 = (bf16[2,256,1024]{2,1,0:T(8,128)(2,1)S(1)}, bf16[2,256,1024]{2,1,0:T(8,128)(2,1)S(1)}, u32[]{:S(2)}, u32[]{:S(2)}) collective-permute-start(bf16[2,256,1024]{2,1,0:T(8,128)(2,1)S(1)} %pad_maximum_fusion.1), channel_id=1, source_target_pairs={{0,2},{2,0},{4,6},{6,4},{8,10},{10,8},{12,14},{14,12},{16,18},{18,... | collective-permute-start | bytes 3145736 | tf_op jit(solution)/shard_map/ppermute | solution.py:425
  47.4 33.0 %collective-permute-start.10 = (bf16[4096,128]{1,0:T(8,128)(2,1)}, bf16[4096,128]{1,0:T(8,128)(2,1)S(1)}, u32[]{:S(2)}, u32[]{:S(2)}) collective-permute-start(bf16[4096,128]{1,0:T(8,128)(2,1)} %collective-permute-done.4.refs_10_), channel_id=1, source_target_pairs={{8,0},{10,2},{12,4},{14,6},{16,24},{18,26},{20,28},{22,30},{9,1},{... | collective-permute-start | bytes 3145736 | tf_op jit(solution)/shard_map/ppermute | solution.py:428
  48.8 32.5 %collective-permute-start.11 = (bf16[4096,128]{1,0:T(8,128)(2,1)}, bf16[4096,128]{1,0:T(8,128)(2,1)}, u32[]{:S(2)}, u32[]{:S(2)}) collective-permute-start(bf16[4096,128]{1,0:T(8,128)(2,1)} %collective-permute-done.3.refs_9_), channel_id=1, source_target_pairs={{8,16},{10,18},{12,20},{14,22},{16,8},{18,10},{20,12},{22,14},{9,1... | collective-permute-start | bytes 3145736 | tf_op jit(solution)/shard_map/ppermute | solution.py:428
  81.4 20.3 %collective-permute-start.12 = (bf16[512,256]{1,0:T(8,128)(2,1)S(1)}, bf16[512,256]{1,0:T(8,128)(2,1)S(1)}, u32[]{:S(2)}, u32[]{:S(2)}) collective-permute-start(bf16[512,256]{1,0:T(8,128)(2,1)S(1)} %get-tuple-element.42), channel_id=1, source_target_pairs={{8,0},{10,2},{12,4},{14,6},{16,8},{18,10},{20,12},{22,14},{24,16},... | collective-permute-start | bytes 786440 | tf_op jit(solution)/shard_map/ppermute | solution.py:428
  82.7 31.4 %collective-permute-start.13 = (bf16[512,256]{1,0:T(8,128)(2,1)S(1)}, bf16[512,256]{1,0:T(8,128)(2,1)S(1)}, u32[]{:S(2)}, u32[]{:S(2)}) collective-permute-start(bf16[512,256]{1,0:T(8,128)(2,1)S(1)} %get-tuple-element.44), channel_id=1, source_target_pairs={{16,0},{18,2},{20,4},{22,6},{24,8},{26,10},{28,12},{30,14},{17,1},... | collective-permute-start | bytes 786440 | tf_op jit(solution)/shard_map/ppermute | solution.py:428
  84.0 48.6 %collective-permute-start.17 = (bf16[2,128,4096]{2,1,0:T(8,128)(2,1)S(1)}, bf16[2,128,4096]{2,1,0:T(8,128)(2,1)}, u32[]{:S(2)}, u32[]{:S(2)}) collective-permute-start(bf16[2,128,4096]{2,1,0:T(8,128)(2,1)S(1)} %pad_maximum_fusion.refs_0_.refs_4_), channel_id=1, source_target_pairs={{0,2},{2,0},{4,6},{6,4},{8,10},{10,8},{12,14},{14,12},{16,18},{18,... | collective-permute-start | bytes 6291464 | tf_op jit(solution)/shard_map/ppermute | solution.py:425
  114.1 29.3 %collective-permute-start.19 = (bf16[2,128,4096]{2,1,0:T(8,128)(2,1)}, bf16[2,128,4096]{2,1,0:T(8,128)(2,1)}, u32[]{:S(2)}, u32[]{:S(2)}) collective-permute-start(bf16[2,128,4096]{2,1,0:T(8,128)(2,1)} %collective-permute-done.18.refs_2_.refs_6_), channel_id=1, source_target_pairs={{0,2},{2,0},{4,6},{6,4},{8,10},{10,8},{12,14},{14,12},{16,18},{18,... | collective-permute-start | bytes 6291464 | tf_op jit(solution)/shard_map/ppermute | solution.py:425
  114.1 27.8 %collective-permute-start.20 = (bf16[4096,128]{1,0:T(8,128)(2,1)}, bf16[4096,128]{1,0:T(8,128)(2,1)}, u32[]{:S(2)}, u32[]{:S(2)}) collective-permute-start(bf16[4096,128]{1,0:T(8,128)(2,1)} %collective-permute-done.11.refs_8_), channel_id=1, source_target_pairs={{8,0},{10,2},{12,4},{14,6},{16,24},{18,26},{20,28},{22,30},{9,1},{... | collective-permute-start | bytes 3145736 | tf_op jit(solution)/shard_map/ppermute | solution.py:428
  115.4 14.5 %collective-permute-start.8 = (bf16[2,128,1024]{2,1,0:T(8,128)(2,1)S(1)}, bf16[2,128,1024]{2,1,0:T(8,128)(2,1)}, u32[]{:S(2)}, u32[]{:S(2)}) collective-permute-start(bf16[2,128,1024]{2,1,0:T(8,128)(2,1)S(1)} %get-tuple-element.37), channel_id=1, source_target_pairs={{0,4},{2,6},{4,0},{6,2},{8,12},{10,14},{12,8},{14,10},{16,20},{18,... | collective-permute-start | bytes 1572872 | tf_op jit(solution)/shard_map/ppermute | solution.py:425
  118.2 42.1 %collective-permute-start.21 = (bf16[512,128]{1,0:T(8,128)(2,1)}, bf16[512,128]{1,0:T(8,128)(2,1)S(1)}, u32[]{:S(2)}, u32[]{:S(2)}) collective-permute-start(bf16[512,128]{1,0:T(8,128)(2,1)} %get-tuple-element.54), channel_id=1, source_target_pairs={{0,2},{2,0},{4,6},{6,4},{8,10},{10,8},{12,14},{14,12},{16,18},{18,... | collective-permute-start | bytes 393224 | tf_op jit(solution)/shard_map/ppermute | solution.py:425
  129.9 30.4 %collective-permute-start.23 = (bf16[512,128]{1,0:T(8,128)(2,1)}, bf16[512,128]{1,0:T(8,128)(2,1)S(1)}, u32[]{:S(2)}, u32[]{:S(2)}) collective-permute-start(bf16[512,128]{1,0:T(8,128)(2,1)} %get-tuple-element.54), channel_id=1, source_target_pairs={{0,3},{1,2},{2,1},{3,0},{4,7},{5,6},{6,5},{7,4},{8,11},{9,10},{10,... | collective-permute-start | bytes 393224 | tf_op jit(solution)/shard_map/ppermute | solution.py:440
  132.5 32.0 %collective-permute-start.14 = (bf16[2,128,256]{2,1,0:T(8,128)(2,1)}, bf16[2,128,256]{2,1,0:T(8,128)(2,1)S(1)}, u32[]{:S(2)}, u32[]{:S(2)}) collective-permute-start(bf16[2,128,256]{2,1,0:T(8,128)(2,1)} %get-tuple-element.46), channel_id=1, source_target_pairs={{0,4},{2,6},{4,0},{6,2},{8,12},{10,14},{12,8},{14,10},{16,20},{18,... | collective-permute-start | bytes 393224 | tf_op jit(solution)/shard_map/ppermute | solution.py:425
  141.9 18.4 %collective-permute-start.22 = (bf16[512,128]{1,0:T(8,128)(2,1)}, bf16[512,128]{1,0:T(8,128)(2,1)S(1)}, u32[]{:S(2)}, u32[]{:S(2)}) collective-permute-start(bf16[512,128]{1,0:T(8,128)(2,1)} %get-tuple-element.53.g0), channel_id=1, source_target_pairs={{0,1},{1,0},{2,3},{3,2},{4,5},{5,4},{6,7},{7,6},{8,9},{9,8},{10,11... | collective-permute-start | bytes 393224 | tf_op jit(solution)/shard_map/ppermute | solution.py:436
  143.4 22.7 %collective-permute-start.9 = (bf16[2,128,1024]{2,1,0:T(8,128)(2,1)}, bf16[2,128,1024]{2,1,0:T(8,128)(2,1)S(1)}, u32[]{:S(2)}, u32[]{:S(2)}) collective-permute-start(bf16[2,128,1024]{2,1,0:T(8,128)(2,1)} %pad_maximum_fusion.2), channel_id=1, source_target_pairs={{0,2},{2,0},{4,6},{6,4},{8,10},{10,8},{12,14},{14,12},{16,18},{18,... | collective-permute-start | bytes 1572872 | tf_op jit(solution)/shard_map/ppermute | solution.py:425
  162.0 11.2 %all-to-all-start = ((f32[32,8,128]{2,1,0:T(8,128)}), f32[32,8,128]{2,1,0:T(8,128)S(1)}, u32[]{:S(2)}, u32[]{:S(2)}) async-start(f32[32,8,128]{2,1,0:T(8,128)} %broadcast_in_dim.2), calls=%async_computation | async-start | bytes 262144 | tf_op jit(solution)/shard_map/all_to_all | solution.py:507
  (22 other events, 255.4 us)

commit v3 on v2

--- a/solution.py
+++ b/solution.py
@@ -88,6 +88,22 @@
         out_specs=[VMEM] * len(shapes),
         name="pack_queries",
     )(place, queries, grad_out, *after)
+
+
+def join(views, after=()):
+    arrays = [array for array, _ in views]
+
+    def kernel(*refs):
+        for k, (ref, (_, slot)) in enumerate(zip(refs, views)):
+            refs[-1][k] = ref[slot]
+
+    return pl.pallas_call(
+        kernel,
+        out_shape=jax.ShapeDtypeStruct((len(views),) + arrays[0].shape[1:], arrays[0].dtype),
+        in_specs=[VMEM] * (len(views) + len(after)),
+        out_specs=VMEM,
+        name="join",
+    )(*arrays, *after)
 
 
 def split_kernel(place_ref, d_ref, mine_ref, theirs_ref):
@@ -248,7 +264,7 @@
             pltpu.VMEM((keys, HD), F32),
             pltpu.SemaphoreType.DMA((n_copies,)),
         ],
-        compiler_params=pltpu.CompilerParams(vmem_limit_bytes=24 * 2**20),
+        compiler_params=pltpu.CompilerParams(vmem_limit_bytes=18 * 2**20),
         cost_estimate=pl.CostEstimate(
             flops=flops, bytes_accessed=6 * plane * width, transcendentals=group_size * plane * span
         ),
@@ -283,7 +299,7 @@
     return pl.pallas_call(
         kernel,
         out_shape=shapes + [jax.ShapeDtypeStruct((plane, HD), BF16)] * 2,
-        in_specs=[SMEM] + [VMEM] * (1 + len(prev)) + [ANY] * n_after,
+        in_specs=[SMEM] + [VMEM] * (1 + len(prev) + n_after),
         out_specs=[VMEM] * (len(shapes) + 2),
         scratch_shapes=[pltpu.VMEM((plane, 2 * HD), BF16)],
         name="sum_key_value_gradients",
@@ -314,71 +330,56 @@
     )(place, *[array for array, _ in pieces])
 
 
-def project_kernel(slots, counts, place_ref, *refs):
-    n_pieces, n_blocks = len(slots), sum(counts)
-    d_refs = [ref.at[k] for ref, k in zip(refs[:n_pieces], slots, strict=True)]
-    w_refs = refs[n_pieces : n_pieces + n_blocks]
-    out_ref, ds, ws, sems = refs[n_pieces + n_blocks :]
+def project_kernel(layout, place_ref, *refs):
+    d_refs, w_refs = refs[:4], list(refs[4:-2])
+    out_ref, ws = refs[-2:]
     me, plane_at = place_ref[0], place_ref[2]
-    tok = d_refs[0].shape[0]
-    inner = jnp.logical_or(plane_at == 1, plane_at == 2)
-    copies = []
-    at = 0
-    for k, count in enumerate(counts):
-        dst = ws.at[:, k * HD : (k + 1) * HD]
-        copies.append(pltpu.make_async_copy(w_refs[at], dst, sems.at[k]))
-        if count == 1:
-            copies[k].start()
-        else:
-            from_end = pltpu.make_async_copy(w_refs[at + 1], dst, sems.at[k])
-            pl.when(inner)(copies[k].start)
-            pl.when(jnp.logical_not(inner))(from_end.start)
-        at += count
-    for i, d_ref in enumerate(d_refs):
-        shard = i // 4 * 4 + (me ^ (i % 4))
-        dst = ds.at[pl.ds(pl.multiple_of(shard * tok, tok), tok), :]
-        copies.append(pltpu.make_async_copy(d_ref, dst, sems.at[len(copies)]))
-        copies[-1].start()
-    for copy in copies:
-        copy.wait()
-    step = 256
-
-    def one(i, _):
-        at = pl.ds(pl.multiple_of(i * step, step), step)
-        out_ref[at, :] = jnp.dot(ds[at, :], ws[...], preferred_element_type=F32)
-        return 0
-
-    lax.fori_loop(0, ds.shape[0] // step, one, 0)
+    layers, tok, depth = d_refs[0].shape
+    for k, counts in enumerate(layout):
+        end = 0
+        for count in counts:
+            start, end = end, end + min(w_ref.shape[0] for w_ref in w_refs[:count])
+            rows, size = slice(start, end), end - start
+            for z in range(count):
+                w_ref = w_refs.pop(0)
+
+                @pl.when(jnp.logical_or(count == 1, plane_at == z))
+                def _():
+                    ws[rows, k * HD : (k + 1) * HD] = w_ref[...] if w_ref.shape[0] == size else w_ref[rows, :]
+
+    for r, d_ref in enumerate(d_refs):
+        rows = d_ref[...].reshape(layers * tok, depth)
+        out = jnp.dot(rows, ws[...], preferred_element_type=F32)
+        for layer in range(layers):
+            shard = layer * len(d_refs) + (me ^ r)
+            out_ref[pl.ds(pl.multiple_of(shard * tok, tok), tok), :] = out[layer * tok : (layer + 1) * tok]
 
 
 def project(place, pieces, blocks):
-    _, tok, depth = pieces[0][0].shape
-    rows, width = tok * len(pieces), HD * len(blocks)
-    arrays = [array for block in blocks for array in block]
-    return pl.pallas_call(
-        functools.partial(project_kernel, [k for _, k in pieces], [len(block) for block in blocks]),
+    layers, tok, depth = pieces[0].shape
+    rows, width = layers * tok * len(pieces), HD * len(blocks)
+    arrays = [array for block in blocks for part in block for array in part]
+    return pl.pallas_call(
+        functools.partial(project_kernel, [[len(part) for part in block] for block in blocks]),
         out_shape=jax.ShapeDtypeStruct((rows, width), F32),
-        in_specs=[SMEM] + [ANY] * (len(pieces) + len(arrays)),
+        in_specs=[SMEM] + [VMEM] * (len(pieces) + len(arrays)),
         out_specs=VMEM,
-        scratch_shapes=[
-            pltpu.VMEM((rows, depth), BF16),
-            pltpu.VMEM((depth, width), BF16),
-            pltpu.SemaphoreType.DMA((len(blocks) + len(pieces),)),
-        ],
+        scratch_shapes=[pltpu.VMEM((depth, width), BF16)],
         compiler_params=pltpu.CompilerParams(vmem_limit_bytes=20 * 2**20),
         cost_estimate=pl.CostEstimate(
             flops=2 * rows * depth * width, bytes_accessed=2 * depth * (rows + width), transcendentals=0
         ),
         name="project_deltas",
-    )(place, *[array for array, _ in pieces], *arrays)
-
-
-def contract_kernel(norm, place_ref, slot_ref, p_ref, p_last_ref, g0, g1, g2, g3, out_ref):
+    )(place, *pieces, *arrays)
+
+
+def contract_kernel(norm, place_ref, slot_ref, p_ref, g0, g1, g2, g3, out_ref):
     me, side, plane_at = place_ref[0], place_ref[1], place_ref[2]
     kind = lax.rem(me, 2)
-    row = lax.broadcasted_iota(jnp.int32, out_ref.shape, 0)
-    lane = lax.broadcasted_iota(jnp.int32, out_ref.shape, 1)
-    total = jnp.zeros(out_ref.shape, F32)
+    shape = out_ref.shape[1:]
+    row = lax.broadcasted_iota(jnp.int32, shape, 0)
+    lane = lax.broadcasted_iota(jnp.int32, shape, 1)
+    total = jnp.zeros(shape, F32)
     n_tok = g0.shape[0]
     for k, g_ref in enumerate((g0, g1, g2, g3)):
         block = 2 * (side ^ (k // 2)) + (kind ^ (k % 2))
@@ -389,22 +390,22 @@
         g = g_ref[...].astype(F32)
         for layer in range(2):
             rows = slice(layer * n_tok, (layer + 1) * n_tok)
-            part = jnp.where(slot == 3, p_last_ref[rows, :], p_ref[rows, cols(jnp.minimum(slot, 2), HD)]) * g
+            part = p_ref[rows, cols(slot, HD)] * g
             value = jnp.sum(jnp.sum(part, axis=0, keepdims=True), axis=1, keepdims=True) * norm
             here = (row == slot_ref[side ^ layer]) & (lane == 4 * block + me)
             total = total + jnp.where(here, value, 0.0)
-    out_ref[...] = total
-
-
-def contract(place, layer_slot, projected, parts, norm):
+    out_ref[...] = jnp.broadcast_to(total[None], out_ref.shape)
+
+
+def contract(place, layer_slot, projected, parts, norm, n_dev):
     return pl.pallas_call(
         functools.partial(contract_kernel, norm),
-        out_shape=jax.ShapeDtypeStruct((8, HD), F32),
-        in_specs=[SMEM, SMEM] + [VMEM] * 6,
+        out_shape=jax.ShapeDtypeStruct((n_dev, 8, HD), F32),
+        in_specs=[SMEM, SMEM] + [VMEM] * 5,
         out_specs=VMEM,
         compiler_params=pltpu.CompilerParams(vmem_limit_bytes=16 * 2**20),
         name="contract_scores",
-    )(place, layer_slot, *projected, *parts)
+    )(place, layer_slot, projected, *parts)
 
 
 def on_device(queries, keyval, grad_out, doc_ids, deltas, node_weights, layer_slot):
@@ -442,7 +443,7 @@
     def follow(x, after):
         return lax.optimization_barrier((x, *after))[0] if after else x
 
-    def exchange(halves, before=(), between=()):
+    def exchange(halves, before=(), between=(), gate=None):
         if members == 1:
             return [(halves[0], 0)]
         bit = members // 2
@@ -451,14 +452,15 @@
         while bit > 1:
             bit //= 2
             chosen = [r for r in range(members) if r & bit]
-            message = jnp.stack([views[r][0][views[r][1]] for r in chosen])
+            chosen_views = [views[r] for r in chosen]
+            message = join(chosen_views, gate) if gate else jnp.stack([array[k] for array, k in chosen_views])
             got = to_member(follow(message, between), bit)
             for k, r in enumerate(chosen):
                 views[r] = (got, k)
         return views
 
     spread = n_head == 2 and members == 4 and planes == 4 and per_head == 2 and deltas.shape[0] == 1
-    first, second = [], []
+    first, second, third = [], [], []
     if spread:
         pairs, middle, ends = [(0, 1), (1, 0), (2, 3), (3, 2)], [(1, 2), (2, 1)], [(1, 0), (2, 3)]
         w_pair, w_middle = to_plane(node_weights, pairs), to_plane(node_weights, middle)
@@ -479,34 +481,33 @@
         near_c = to_member(near, 1)
         w_ends = to_plane(follow(w_middle, kv[1:]), ends)
         w_middle2 = to_plane(follow(w_pair, kv[1:]), middle)
-        w_ends2 = to_plane(w_middle2, ends)
-        second = [w_ends, w_middle2]
+        w_ends2 = to_plane(follow(w_pair, kv[1:]), [(1, 3), (2, 0)])
+        second = [w_ends, w_middle2, w_ends2]
 
     out = attention(place, queries, grad_out, qo[1:], kv, members, per_head, group_size, window, ())
     n_dq = min(members, 2)
     dq, own, prev = out[:n_dq], out[n_dq], out[n_dq + 1 :]
     prev = [shift(follow(prev[k], second), -(k + 1)) for k in range(back)]
-    dq = exchange(dq)
     if spread:
-        other_c = to_member(follow(other, prev), 1)
-        pieces = [(array, layer) for layer in range(2) for array in (near, near_c, other, other_c)]
-    summed = combine(place, own, prev, members, tok, ())
+        other_c = to_member(follow(other, second + [own]), 1)
+        pieces = [near, near_c, other, other_c]
+    if spread:
+        sides = (w_ends, w_middle, w_middle, w_ends)
+        last = (w_ends2, w_middle2, w_middle2, w_ends2)
+        projected = project(place, pieces, [[(node_weights,)], [(w_pair,)], [sides], [last]])
+        third = [projected]
+    summed = combine(place, own, prev, members, tok, third)
     token_parts, kinds = summed[:-2], summed[-2:]
+    norm = 1.0 / math.sqrt(n_seq * tok)
+    partial = []
     if spread:
         parts = [kinds[0], to_member(kinds[1], 1), other_head(kinds[0]), other_head_and_member(kinds[1])]
-    dkv = exchange(token_parts)
+        partial = [contract(place, layer_slot, projected, parts, norm, n_seq * n_head)]
+    dq = exchange(dq, gate=partial)
+    dkv = exchange(token_parts, gate=partial)
     grad_query, grad_keyval = settle(place, dq, dkv, per_head)
-    norm = 1.0 / math.sqrt(n_seq * tok)
     if spread:
-        projected = [
-            project(place, pieces, [(node_weights,), (w_pair,), (w_middle, w_ends)]),
-            project(place, pieces, [(w_middle2, w_ends2)]),
-        ]
-        mine = contract(place, layer_slot, projected, parts, norm)
-        n_dev = n_seq * n_head
-        copies = lax.all_to_all(
-            jnp.broadcast_to(mine[None], (n_dev,) + mine.shape), ("seq", "head"), 0, 0, tiled=True
-        )
+        copies = lax.all_to_all(partial[0], ("seq", "head"), 0, 0, tiled=True)
         scores = jnp.sum(copies, axis=0)[: layer_slot.shape[0], : n_seq * block_width // HD]
         return grad_query, grad_keyval, scores
 

time: 174 us -> 157 us (0.902)
  waiting for transfers between devices: 70.2 us -> 55.5 us
  Pallas kernels: 58 us -> 52.7 us
  starting transfers between devices: 33.6 us -> 35.9 us
    ppermute x12, waiting for transfers between devices: 15.9 us -> 1 us  [to_member(): lax.ppermute(x, 'seq', [(s, s - s % members + (s % members ^ r)) for s in...]
    ppermute x9, waiting for transfers between devices: 51.4 us -> 43.2 us  [to_plane(): lax.ppermute(x, 'seq', [(a * members + k, b * members + k) for a, b in pa...]
    pallas_call x2 -> x3, Pallas kernels: 15.6 us -> 9.67 us  [the longest x1 5.94 us: project(): pl.pallas_call(functools.partial(project_kernel, [[len(part) for part in...]
    all_to_all x1, starting transfers between devices: 2.56 us -> 7.54 us  [on_device(): copies = lax.all_to_all(partial[0], ('seq', 'head'), 0, 0, tiled=True)]
    ppermute x2, waiting for transfers between devices: 0.01 us -> 3.54 us  [other_head(): return lax.ppermute(x, 'head', [(0, 1), (1, 0)])]
    all_to_all x1, waiting for transfers between devices: 2.83 us -> 6.03 us  [on_device(): copies = lax.all_to_all(partial[0], ('seq', 'head'), 0, 0, tiled=True)]
    ppermute x9, starting transfers between devices: 21.5 us -> 19 us  [to_plane(): lax.ppermute(x, 'seq', [(a * members + k, b * members + k) for a, b in pa...]
    unnamed x42 -> x40, local copies, waits for them, and re-layouts: 5.44 us -> 7.3 us
  transfers between devices with their start and end apart: 25 -> 25, of which waited for: 10 -> 9; matrix products, arithmetic and copies ran while one was open for 3% -> 3% of each run, Pallas kernels for 33% -> 31%
where the time goes in v3:
time: 157 us
  waiting for transfers between devices  55.5 us (35%)
  Pallas kernels  52.7 us (34%)
  starting transfers between devices  35.9 us (23%)
  local copies, waits for them, and re-layouts  8.89 us (6%)
  other arithmetic  2.92 us (2%)
    ppermute x9, waiting for transfers between devices, to_plane(): lax.ppermute(x, 'seq', [(a * members + k, b * members + k) for a, b in pa...  43.2 us
    pallas_call x1, Pallas kernels, attention(): pl.pallas_call(functools.partial(attention_kernel, members, per_head, gro...  28.6 us
    ppermute x9, starting transfers between devices, to_plane(): lax.ppermute(x, 'seq', [(a * members + k, b * members + k) for a, b in pa...  19 us
    all_to_all x1, starting transfers between devices, on_device(): copies = lax.all_to_all(partial[0], ('seq', 'head'), 0, 0, tiled=True)  7.54 us
    unnamed x40, local copies, waits for them, and re-layouts  7.3 us
    ppermute x12, starting transfers between devices, to_member(): lax.ppermute(x, 'seq', [(s, s - s % members + (s % members ^ r)) for s in...  6.41 us
    all_to_all x1, waiting for transfers between devices, on_device(): copies = lax.all_to_all(partial[0], ('seq', 'head'), 0, 0, tiled=True)  6.03 us
    pallas_call x1, Pallas kernels, project(): pl.pallas_call(functools.partial(project_kernel, [[len(part) for part in...  5.94 us
  transfers between devices with their start and end apart: 25, of which 9 were waited for; matrix products, arithmetic and copies ran while one was open for 3% of the time, Pallas kernels for 31%

profile of v3, /device:TPU:0, one launch (start us, length us, event | category | flops | bytes accessed | tf_op | source)
XLA Modules:
  0.0 156.9 jit_solution(15597107327764888659)
XLA Ops:
  0.6 3.1 %collective-permute-start.3 = (bf16[4096,128]{1,0:T(8,128)(2,1)}, bf16[4096,128]{1,0:T(8,128)(2,1)S(1)}, u32[]{:S(2)}, u32[]{:S(2)}) collective-permute-start(bf16[4096,128]{1,0:T(8,128)(2,1)} %refs_4_.1), channel_id=1, source_target_pairs={{0,8},{2,10},{4,12},{6,14},{8,0},{10,2},{12,4},{14,6},{16,24},{18,... | collective-permute-start | bytes 3145736 | tf_op jit(solution)/shard_map/ppermute | solution.py:429
  5.0 1.7 %pack_keys.1 = (bf16[2,144,256]{2,1,0:T(8,128)(2,1)}, bf16[2,144,256]{2,1,0:T(8,128)(2,1)}) custom-call(s32[3]{0:T(128)} %pad_add_fusion.place_ref.refs_0_, s32[1,128]{1,0:T(1,128)} %bitcast.9, bf16[128,1024]{1,0:T(8,128)(2,1)} %kv_ref.1), custom_call_target="tpu_custom_call" | custom-call | tf_op jit(solution)/shard_map/pack_keys/pallas_call | solution.py:62
  6.7 1.5 collective-permute-start
  8.3 3.0 %split_deltas.1 = (bf16[128,4096]{1,0:T(8,128)(2,1)}, bf16[128,4096]{1,0:T(8,128)(2,1)}) custom-call(s32[3]{0:T(128)} %pad_add_fusion.place_ref.refs_0_, bf16[128,8192]{1,0:T(8,128)(2,1)} %bitcast.7), custom_call_target="tpu_custom_call" | custom-call | tf_op jit(solution)/shard_map/split_deltas/pallas_call | solution.py:117
  14.4 3.0 %pack_queries.1 = (bf16[2,256,1024]{2,1,0:T(8,128)(2,1)}, bf16[2,256,1024]{2,1,0:T(8,128)(2,1)}) custom-call(s32[3]{0:T(128)} %pad_add_fusion.place_ref.refs_0_, bf16[128,4096]{1,0:T(8,128)(2,1)} %refs_1_.1, bf16[128,4096]{1,0:T(8,128)(2,1)} %refs_2_.1), custom_call_target="tpu_custom_call" | custom-call | tf_op jit(solution)/shard_map/pack_queries/pallas_call | solution.py:84
  18.0 9.1 %collective-permute-done.3.refs_5_ = bf16[4096,128]{1,0:T(8,128)(2,1)S(1)} collective-permute-done((bf16[4096,128]{1,0:T(8,128)(2,1)}, bf16[4096,128]{1,0:T(8,128)(2,1)S(1)}, u32[]{:S(2)}, u32[]{:S(2)}) %collective-permute-start.3) | collective-permute-done | bytes 1048608 | tf_op jit(solution)/shard_map/ppermute | solution.py:429
  27.1 7.8 %collective-permute-start.6 = (bf16[4,144,256]{2,1,0:T(8,128)(2,1)S(1)}, bf16[4,144,256]{2,1,0:T(8,128)(2,1)S(1)}, u32[]{:S(2)}, u32[]{:S(2)}) collective-permute-start(bf16[4,144,256]{2,1,0:T(8,128)(2,1)S(1)} %pad_maximum_fusion.2.refs_6_), channel_id=1, source_target_pairs={{0,16},{2,18},{4,20},{6,22},{8,24},{10,26},{12,28},{14,30},{1,17},... | collective-permute-start | bytes 884744 | tf_op jit(solution)/shard_map/ppermute | solution.py:429
  36.3 1.5 pad_maximum_fusion.refs_0_
  37.8 4.6 %collective-permute-done.6.refs_8_ = bf16[4,144,256]{2,1,0:T(8,128)(2,1)S(1)} collective-permute-done((bf16[4,144,256]{2,1,0:T(8,128)(2,1)S(1)}, bf16[4,144,256]{2,1,0:T(8,128)(2,1)S(1)}, u32[]{:S(2)}, u32[]{:S(2)}) %collective-permute-start.6) | collective-permute-done | bytes 294944 | tf_op jit(solution)/shard_map/ppermute | solution.py:429
  42.4 4.1 %collective-permute-done.5.refs_7_ = bf16[4,144,256]{2,1,0:T(8,128)(2,1)S(1)} collective-permute-done((bf16[4,144,256]{2,1,0:T(8,128)(2,1)S(1)}, bf16[4,144,256]{2,1,0:T(8,128)(2,1)S(1)}, u32[]{:S(2)}, u32[]{:S(2)}) %collective-permute-start.5) | collective-permute-done | bytes 294944 | tf_op jit(solution)/shard_map/ppermute | solution.py:429
  46.5 1.5 collective-permute-start.11
  52.2 28.6 %attention_both_ways.1 = (bf16[2,128,1024]{2,1,0:T(8,128)(2,1)S(1)}, bf16[2,128,1024]{2,1,0:T(8,128)(2,1)S(1)}, f32[512,256]{1,0:T(8,128)S(1)}, bf16[512,256]{1,0:T(8,128)(2,1)S(1)}, bf16[512,256]{1,0:T(8,128)(2,1)S(1)}) custom-call(s32[3]{0:T(128)S(1)} %copy-done.9, bf16[128,4096]{1,0:T(8,128)(2,1)S(1)} %copy-done.5, bf16[128,4096]{1,0:T(8,128)(2,1)S(1)} %copy-done.6, ...), custom_call_target="tpu_custom_call" | custom-call | flops 1342177280 | bytes 3145728 | tf_op jit(solution)/shard_map/attention_both_ways/pallas_call | solution.py:246
  81.6 19.4 %collective-permute-done.12.refs_6_.refs_9_ = bf16[4096,128]{1,0:T(8,128)(2,1)S(1)} collective-permute-done((bf16[4096,128]{1,0:T(8,128)(2,1)S(1)}, bf16[4096,128]{1,0:T(8,128)(2,1)S(1)}, u32[]{:S(2)}, u32[]{:S(2)}) %collective-permute-start.12) | collective-permute-done | bytes 1048608 | tf_op jit(solution)/shard_map/ppermute | solution.py:429
  105.2 5.9 %project_deltas.1.refs_2_.p_ref = f32[1024,512]{1,0:T(8,128)S(1)} custom-call(s32[3]{0:T(128)S(1)} %copy-done.9, bf16[2,128,4096]{2,1,0:T(8,128)(2,1)S(1)} %pad_maximum_fusion.refs_0_, bf16[2,128,4096]{2,1,0:T(8,128)(2,1)S(1)} %collective-permute-done.10.refs_1_, bf16[2,128,4096]{2,1,0:T(8,128)(2,1)S(1)} %collective-permute-done.11.refs_2_, ...), custom_call_target="tpu_custom_call" | custom-call | flops 4294967296 | bytes 12582912 | tf_op jit(solution)/shard_map/project_deltas/pallas_call | solution.py:362
  112.5 6.1 %collective-permute-done.17.refs_1_ = bf16[512,256]{1,0:T(8,128)(2,1)S(1)} collective-permute-done((bf16[512,256]{1,0:T(8,128)(2,1)S(1)}, bf16[512,256]{1,0:T(8,128)(2,1)S(1)}, u32[]{:S(2)}, u32[]{:S(2)}) %collective-permute-start.17) | collective-permute-done | bytes 262176 | tf_op jit(solution)/shard_map/ppermute | solution.py:429
  119.2 2.9 %sum_key_value_gradients.1 = (bf16[2,128,256]{2,1,0:T(8,128)(2,1)}, bf16[2,128,256]{2,1,0:T(8,128)(2,1)}, bf16[512,128]{1,0:T(8,128)(2,1)}, bf16[512,128]{1,0:T(8,128)(2,1)}) custom-call(s32[3]{0:T(128)} %pad_add_fusion.place_ref.refs_0_, f32[512,256]{1,0:T(8,128)} %copy-done.7, bf16[512,256]{1,0:T(8,128)(2,1)} %collective-permute-done.16.refs_0_, ...), custom_call_target="tpu_custom_call" | custom-call | tf_op jit(solution)/shard_map/sum_key_value_gradients/pallas_call | solution.py:299
  122.2 1.5 collective-permute-start.19
  124.3 3.5 %collective-permute-done.19.g2 = bf16[512,128]{1,0:T(8,128)(2,1)S(1)} collective-permute-done((bf16[512,128]{1,0:T(8,128)(2,1)}, bf16[512,128]{1,0:T(8,128)(2,1)S(1)}, u32[]{:S(2)}, u32[]{:S(2)}) %collective-permute-start.19) | collective-permute-done | bytes 131104 | tf_op jit(solution)/shard_map/ppermute | solution.py:437
  127.8 1.8 %collective-permute-done.20.g3 = bf16[512,128]{1,0:T(8,128)(2,1)S(1)} collective-permute-done((bf16[512,128]{1,0:T(8,128)(2,1)}, bf16[512,128]{1,0:T(8,128)(2,1)S(1)}, u32[]{:S(2)}, u32[]{:S(2)}) %collective-permute-start.20) | collective-permute-done | bytes 131104 | tf_op jit(solution)/shard_map/ppermute | solution.py:441
  133.0 2.0 %join.2 = bf16[2,128,1024]{2,1,0:T(8,128)(2,1)} custom-call(bf16[2,128,1024]{2,1,0:T(8,128)(2,1)} %copy-done.2, bf16[2,128,1024]{2,1,0:T(8,128)(2,1)} %copy-done.12, f32[32,8,128]{2,1,0:T(8,128)} %copy-done.3), custom_call_target="tpu_custom_call" | custom-call | tf_op jit(solution)/shard_map/join/pallas_call | solution.py:100
  135.9 7.5 %all-to-all-start = ((f32[32,8,128]{2,1,0:T(8,128)}), f32[32,8,128]{2,1,0:T(8,128)S(1)}, u32[]{:S(2)}, u32[]{:S(2)}) async-start(f32[32,8,128]{2,1,0:T(8,128)} %copy-done.3), calls=%async_computation | async-start | bytes 262144 | tf_op jit(solution)/shard_map/all_to_all | solution.py:510
  144.1 1.7 %join.3 = bf16[2,128,256]{2,1,0:T(8,128)(2,1)} custom-call(bf16[2,128,256]{2,1,0:T(8,128)(2,1)} %get-tuple-element.51.refs_0_.refs_4_, bf16[2,128,256]{2,1,0:T(8,128)(2,1)} %copy-done.16, f32[32,8,128]{2,1,0:T(8,128)} %copy-done.3), custom_call_target="tpu_custom_call" | custom-call | tf_op jit(solution)/shard_map/join/pallas_call | solution.py:100
  146.0 6.0 %all-to-all-done = f32[32,8,128]{2,1,0:T(8,128)S(1)} async-done(((f32[32,8,128]{2,1,0:T(8,128)}), f32[32,8,128]{2,1,0:T(8,128)S(1)}, u32[]{:S(2)}, u32[]{:S(2)}) %all-to-all-start) | async-done | bytes 131104 | tf_op jit(solution)/shard_map/all_to_all | solution.py:510
  154.1 2.8 %place_heads.1 = (bf16[128,4096]{1,0:T(8,128)(2,1)}, bf16[128,1024]{1,0:T(8,128)(2,1)}) custom-call(s32[3]{0:T(128)} %pad_add_fusion.place_ref.refs_0_, bf16[2,128,1024]{2,1,0:T(8,128)(2,1)} %copy-done.2, bf16[2,128,1024]{2,1,0:T(8,128)(2,1)} %copy-done.13, bf16[2,128,1024]{2,1,0:T(8,128)(2,1)} %copy-done.12, bf16[2,128,1024]{2,1,0:T(8,128)(2,1)} %copy-done.13, ...), custom_call_target="tpu_custom_call" | custom-call | tf_op jit(solution)/shard_map/place_heads/pallas_call | solution.py:322
  (88 shorter events, 25.2 us)
Async XLA Ops:
  0.6 26.5 %collective-permute-start.3 = (bf16[4096,128]{1,0:T(8,128)(2,1)}, bf16[4096,128]{1,0:T(8,128)(2,1)S(1)}, u32[]{:S(2)}, u32[]{:S(2)}) collective-permute-start(bf16[4096,128]{1,0:T(8,128)(2,1)} %refs_4_.1), channel_id=1, source_target_pairs={{0,8},{2,10},{4,12},{6,14},{8,0},{10,2},{12,4},{14,6},{16,24},{18,... | collective-permute-start | bytes 3145736 | tf_op jit(solution)/shard_map/ppermute | solution.py:429
  3.7 23.4 %collective-permute-start.4 = (bf16[4096,128]{1,0:T(8,128)(2,1)}, bf16[4096,128]{1,0:T(8,128)(2,1)S(1)}, u32[]{:S(2)}, u32[]{:S(2)}) collective-permute-start(bf16[4096,128]{1,0:T(8,128)(2,1)} %refs_4_.1), channel_id=1, source_target_pairs={{8,16},{10,18},{12,20},{14,22},{16,8},{18,10},{20,12},{22,14},{9,1... | collective-permute-start | bytes 3145736 | tf_op jit(solution)/shard_map/ppermute | solution.py:429
  6.7 7.0 %collective-permute-start = (bf16[2,144,256]{2,1,0:T(8,128)(2,1)}, bf16[2,144,256]{2,1,0:T(8,128)(2,1)S(1)}, u32[]{:S(2)}, u32[]{:S(2)}) collective-permute-start(bf16[2,144,256]{2,1,0:T(8,128)(2,1)} %get-tuple-element.32), channel_id=1, source_target_pairs={{0,4},{2,6},{4,0},{6,2},{8,12},{10,14},{12,8},{14,10},{16,20},{18,... | collective-permute-start | bytes 442376 | tf_op jit(solution)/shard_map/ppermute | solution.py:426
  11.3 25.0 %collective-permute-start.9 = (bf16[128,4096]{1,0:T(8,128)(2,1)}, bf16[128,4096]{1,0:T(8,128)(2,1)}, u32[]{:S(2)}, u32[]{:S(2)}) collective-permute-start(bf16[128,4096]{1,0:T(8,128)(2,1)} %get-tuple-element.39), channel_id=1, source_target_pairs={{0,1},{1,0},{2,3},{3,2},{4,5},{5,4},{6,7},{7,6},{8,9},{9,8},{10,11... | collective-permute-start | bytes 3145736 | tf_op jit(solution)/shard_map/ppermute | solution.py:437
  17.4 29.0 %collective-permute-start.2 = (bf16[2,256,1024]{2,1,0:T(8,128)(2,1)}, bf16[2,256,1024]{2,1,0:T(8,128)(2,1)S(1)}, u32[]{:S(2)}, u32[]{:S(2)}) collective-permute-start(bf16[2,256,1024]{2,1,0:T(8,128)(2,1)} %get-tuple-element.33), channel_id=1, source_target_pairs={{0,4},{2,6},{4,0},{6,2},{8,12},{10,14},{12,8},{14,10},{16,20},{18,... | collective-permute-start | bytes 3145736 | tf_op jit(solution)/shard_map/ppermute | solution.py:426
  27.1 15.3 %collective-permute-start.6 = (bf16[4,144,256]{2,1,0:T(8,128)(2,1)S(1)}, bf16[4,144,256]{2,1,0:T(8,128)(2,1)S(1)}, u32[]{:S(2)}, u32[]{:S(2)}) collective-permute-start(bf16[4,144,256]{2,1,0:T(8,128)(2,1)S(1)} %pad_maximum_fusion.2.refs_6_), channel_id=1, source_target_pairs={{0,16},{2,18},{4,20},{6,22},{8,24},{10,26},{12,28},{14,30},{1,17},... | collective-permute-start | bytes 884744 | tf_op jit(solution)/shard_map/ppermute | solution.py:429
  34.9 11.5 %collective-permute-start.5 = (bf16[4,144,256]{2,1,0:T(8,128)(2,1)S(1)}, bf16[4,144,256]{2,1,0:T(8,128)(2,1)S(1)}, u32[]{:S(2)}, u32[]{:S(2)}) collective-permute-start(bf16[4,144,256]{2,1,0:T(8,128)(2,1)S(1)} %pad_maximum_fusion.2.refs_6_), channel_id=1, source_target_pairs={{0,8},{2,10},{4,12},{6,14},{8,16},{10,18},{12,20},{14,22},{16,24},... | collective-permute-start | bytes 884744 | tf_op jit(solution)/shard_map/ppermute | solution.py:429
  46.5 54.5 %collective-permute-start.11 = (bf16[2,128,4096]{2,1,0:T(8,128)(2,1)S(1)}, bf16[2,128,4096]{2,1,0:T(8,128)(2,1)S(1)}, u32[]{:S(2)}, u32[]{:S(2)}) collective-permute-start(bf16[2,128,4096]{2,1,0:T(8,128)(2,1)S(1)} %pad_maximum_fusion.refs_0_), channel_id=1, source_target_pairs={{0,4},{2,6},{4,0},{6,2},{8,12},{10,14},{12,8},{14,10},{16,20},{18,... | collective-permute-start | bytes 6291464 | tf_op jit(solution)/shard_map/ppermute | solution.py:426
  48.2 3.5 %collective-permute-start.7 = (bf16[2,256,1024]{2,1,0:T(8,128)(2,1)S(1)}, bf16[2,256,1024]{2,1,0:T(8,128)(2,1)S(1)}, u32[]{:S(2)}, u32[]{:S(2)}) collective-permute-start(bf16[2,256,1024]{2,1,0:T(8,128)(2,1)S(1)} %pad_maximum_fusion.1), channel_id=1, source_target_pairs={{0,2},{2,0},{4,6},{6,4},{8,10},{10,8},{12,14},{14,12},{16,18},{18,... | collective-permute-start | bytes 3145736 | tf_op jit(solution)/shard_map/ppermute | solution.py:426
  48.3 52.6 %collective-permute-start.12 = (bf16[4096,128]{1,0:T(8,128)(2,1)S(1)}, bf16[4096,128]{1,0:T(8,128)(2,1)S(1)}, u32[]{:S(2)}, u32[]{:S(2)}) collective-permute-start(bf16[4096,128]{1,0:T(8,128)(2,1)S(1)} %collective-permute-done.4.refs_7_.refs_8_), channel_id=1, source_target_pairs={{8,0},{10,2},{12,4},{14,6},{16,24},{18,26},{20,28},{22,30},{9,1},{... | collective-permute-start | bytes 3145736 | tf_op jit(solution)/shard_map/ppermute | solution.py:429
  49.7 51.2 %collective-permute-start.14 = (bf16[4096,128]{1,0:T(8,128)(2,1)S(1)}, bf16[4096,128]{1,0:T(8,128)(2,1)S(1)}, u32[]{:S(2)}, u32[]{:S(2)}) collective-permute-start(bf16[4096,128]{1,0:T(8,128)(2,1)S(1)} %collective-permute-done.3.refs_5_), channel_id=1, source_target_pairs={{8,24},{10,26},{12,28},{14,30},{16,0},{18,2},{20,4},{22,6},{9,25},... | collective-permute-start | bytes 3145736 | tf_op jit(solution)/shard_map/ppermute | solution.py:429
  51.0 49.9 %collective-permute-start.13 = (bf16[4096,128]{1,0:T(8,128)(2,1)S(1)}, bf16[4096,128]{1,0:T(8,128)(2,1)S(1)}, u32[]{:S(2)}, u32[]{:S(2)}) collective-permute-start(bf16[4096,128]{1,0:T(8,128)(2,1)S(1)} %collective-permute-done.3.refs_5_), channel_id=1, source_target_pairs={{8,16},{10,18},{12,20},{14,22},{16,8},{18,10},{20,12},{22,14},{9,1... | collective-permute-start | bytes 3145736 | tf_op jit(solution)/shard_map/ppermute | solution.py:429
  51.7 52.4 %collective-permute-start.10 = (bf16[2,128,4096]{2,1,0:T(8,128)(2,1)S(1)}, bf16[2,128,4096]{2,1,0:T(8,128)(2,1)S(1)}, u32[]{:S(2)}, u32[]{:S(2)}) collective-permute-start(bf16[2,128,4096]{2,1,0:T(8,128)(2,1)S(1)} %pad_maximum_fusion.refs_0_), channel_id=1, source_target_pairs={{0,2},{2,0},{4,6},{6,4},{8,10},{10,8},{12,14},{14,12},{16,18},{18,... | collective-permute-start | bytes 6291464 | tf_op jit(solution)/shard_map/ppermute | solution.py:426
  100.9 4.2 %collective-permute-start.15 = (bf16[2,128,4096]{2,1,0:T(8,128)(2,1)S(1)}, bf16[2,128,4096]{2,1,0:T(8,128)(2,1)S(1)}, u32[]{:S(2)}, u32[]{:S(2)}) collective-permute-start(bf16[2,128,4096]{2,1,0:T(8,128)(2,1)S(1)} %collective-permute-done.11.refs_2_), channel_id=1, source_target_pairs={{0,2},{2,0},{4,6},{6,4},{8,10},{10,8},{12,14},{14,12},{16,18},{18,... | collective-permute-start | bytes 6291464 | tf_op jit(solution)/shard_map/ppermute | solution.py:426
  101.0 17.5 %collective-permute-start.17 = (bf16[512,256]{1,0:T(8,128)(2,1)S(1)}, bf16[512,256]{1,0:T(8,128)(2,1)S(1)}, u32[]{:S(2)}, u32[]{:S(2)}) collective-permute-start(bf16[512,256]{1,0:T(8,128)(2,1)S(1)} %get-tuple-element.48), channel_id=1, source_target_pairs={{16,0},{18,2},{20,4},{22,6},{24,8},{26,10},{28,12},{30,14},{17,1},... | collective-permute-start | bytes 786440 | tf_op jit(solution)/shard_map/ppermute | solution.py:429
  102.3 16.2 %collective-permute-start.16 = (bf16[512,256]{1,0:T(8,128)(2,1)S(1)}, bf16[512,256]{1,0:T(8,128)(2,1)}, u32[]{:S(2)}, u32[]{:S(2)}) collective-permute-start(bf16[512,256]{1,0:T(8,128)(2,1)S(1)} %get-tuple-element.46), channel_id=1, source_target_pairs={{8,0},{10,2},{12,4},{14,6},{16,8},{18,10},{20,12},{22,14},{24,16},... | collective-permute-start | bytes 786440 | tf_op jit(solution)/shard_map/ppermute | solution.py:429
  103.6 28.6 %collective-permute-start.8 = (bf16[2,128,1024]{2,1,0:T(8,128)(2,1)S(1)}, bf16[2,128,1024]{2,1,0:T(8,128)(2,1)S(1)}, u32[]{:S(2)}, u32[]{:S(2)}) collective-permute-start(bf16[2,128,1024]{2,1,0:T(8,128)(2,1)S(1)} %get-tuple-element.37), channel_id=1, source_target_pairs={{0,4},{2,6},{4,0},{6,2},{8,12},{10,14},{12,8},{14,10},{16,20},{18,... | collective-permute-start | bytes 1572872 | tf_op jit(solution)/shard_map/ppermute | solution.py:426
  122.2 5.7 %collective-permute-start.19 = (bf16[512,128]{1,0:T(8,128)(2,1)}, bf16[512,128]{1,0:T(8,128)(2,1)S(1)}, u32[]{:S(2)}, u32[]{:S(2)}) collective-permute-start(bf16[512,128]{1,0:T(8,128)(2,1)} %get-tuple-element.49.g0), channel_id=1, source_target_pairs={{0,1},{1,0},{2,3},{3,2},{4,5},{5,4},{6,7},{7,6},{8,9},{9,8},{10,11... | collective-permute-start | bytes 393224 | tf_op jit(solution)/shard_map/ppermute | solution.py:437
  123.7 6.0 %collective-permute-start.20 = (bf16[512,128]{1,0:T(8,128)(2,1)}, bf16[512,128]{1,0:T(8,128)(2,1)S(1)}, u32[]{:S(2)}, u32[]{:S(2)}) collective-permute-start(bf16[512,128]{1,0:T(8,128)(2,1)} %get-tuple-element.50), channel_id=1, source_target_pairs={{0,3},{1,2},{2,1},{3,0},{4,7},{5,6},{6,5},{7,4},{8,11},{9,10},{10,... | collective-permute-start | bytes 393224 | tf_op jit(solution)/shard_map/ppermute | solution.py:441
  123.7 6.0 %collective-permute-start.18 = (bf16[512,128]{1,0:T(8,128)(2,1)}, bf16[512,128]{1,0:T(8,128)(2,1)S(1)}, u32[]{:S(2)}, u32[]{:S(2)}) collective-permute-start(bf16[512,128]{1,0:T(8,128)(2,1)} %get-tuple-element.50), channel_id=1, source_target_pairs={{0,2},{2,0},{4,6},{6,4},{8,10},{10,8},{12,14},{14,12},{16,18},{18,... | collective-permute-start | bytes 393224 | tf_op jit(solution)/shard_map/ppermute | solution.py:426
  135.0 17.6 %collective-permute-start.21 = (bf16[2,128,1024]{2,1,0:T(8,128)(2,1)}, bf16[2,128,1024]{2,1,0:T(8,128)(2,1)S(1)}, u32[]{:S(2)}, u32[]{:S(2)}) collective-permute-start(bf16[2,128,1024]{2,1,0:T(8,128)(2,1)} %join.2), channel_id=1, source_target_pairs={{0,2},{2,0},{4,6},{6,4},{8,10},{10,8},{12,14},{14,12},{16,18},{18,... | collective-permute-start | bytes 1572872 | tf_op jit(solution)/shard_map/ppermute | solution.py:426
  135.4 8.1 %collective-permute-start.22 = (bf16[2,128,256]{2,1,0:T(8,128)(2,1)S(1)}, bf16[2,128,256]{2,1,0:T(8,128)(2,1)S(1)}, u32[]{:S(2)}, u32[]{:S(2)}) collective-permute-start(bf16[2,128,256]{2,1,0:T(8,128)(2,1)S(1)} %copy-done.19), channel_id=1, source_target_pairs={{0,4},{2,6},{4,0},{6,2},{8,12},{10,14},{12,8},{14,10},{16,20},{18,... | collective-permute-start | bytes 393224 | tf_op jit(solution)/shard_map/ppermute | solution.py:426
  135.9 16.2 %all-to-all-start = ((f32[32,8,128]{2,1,0:T(8,128)}), f32[32,8,128]{2,1,0:T(8,128)S(1)}, u32[]{:S(2)}, u32[]{:S(2)}) async-start(f32[32,8,128]{2,1,0:T(8,128)} %copy-done.3), calls=%async_computation | async-start | bytes 262144 | tf_op jit(solution)/shard_map/all_to_all | solution.py:510
  145.8 6.9 %collective-permute-start.23 = (bf16[2,128,256]{2,1,0:T(8,128)(2,1)}, bf16[2,128,256]{2,1,0:T(8,128)(2,1)S(1)}, u32[]{:S(2)}, u32[]{:S(2)}) collective-permute-start(bf16[2,128,256]{2,1,0:T(8,128)(2,1)} %join.3), channel_id=1, source_target_pairs={{0,2},{2,0},{4,6},{6,4},{8,10},{10,8},{12,14},{14,12},{16,18},{18,... | collective-permute-start | bytes 393224 | tf_op jit(solution)/shard_map/ppermute | solution.py:426
  (21 other events, 196.4 us)

commit v4 on v3

--- a/solution.py
+++ b/solution.py
@@ -373,7 +373,8 @@
     )(place, *pieces, *arrays)
 
 
-def contract_kernel(norm, place_ref, slot_ref, p_ref, g0, g1, g2, g3, out_ref):
+def contract_kernel(norm, place_ref, slot_ref, p_ref, g0, g1, g2, g3, *refs):
+    out_ref = refs[-1]
     me, side, plane_at = place_ref[0], place_ref[1], place_ref[2]
     kind = lax.rem(me, 2)
     shape = out_ref.shape[1:]
@@ -397,15 +398,15 @@
     out_ref[...] = jnp.broadcast_to(total[None], out_ref.shape)
 
 
-def contract(place, layer_slot, projected, parts, norm, n_dev):
+def contract(place, layer_slot, projected, parts, norm, n_dev, after):
     return pl.pallas_call(
         functools.partial(contract_kernel, norm),
         out_shape=jax.ShapeDtypeStruct((n_dev, 8, HD), F32),
-        in_specs=[SMEM, SMEM] + [VMEM] * 5,
+        in_specs=[SMEM, SMEM] + [VMEM] * (5 + len(after)),
         out_specs=VMEM,
         compiler_params=pltpu.CompilerParams(vmem_limit_bytes=16 * 2**20),
         name="contract_scores",
-    )(place, layer_slot, projected, *parts)
+    )(place, layer_slot, projected, *parts, *after)
 
 
 def on_device(queries, keyval, grad_out, doc_ids, deltas, node_weights, layer_slot):
@@ -460,11 +461,12 @@
         return views
 
     spread = n_head == 2 and members == 4 and planes == 4 and per_head == 2 and deltas.shape[0] == 1
-    first, second, third = [], [], []
+    first, second, third, down = [], [], [], []
     if spread:
         pairs, middle, ends = [(0, 1), (1, 0), (2, 3), (3, 2)], [(1, 2), (2, 1)], [(1, 0), (2, 3)]
         w_pair, w_middle = to_plane(node_weights, pairs), to_plane(node_weights, middle)
         first = [w_pair, w_middle]
+        down = [to_plane(w_middle, [(1, 0)]), to_plane(w_pair, [(2, 1)])]
         mine, theirs = split_width(place, deltas.reshape(tok, deltas.shape[2]))
         crossed = other_head(theirs)
 
@@ -479,35 +481,35 @@
         near = jnp.stack([mine, crossed])
         other = to_member(follow(near, [qo[-2][0]] + kv[1:]), 2)
         near_c = to_member(near, 1)
-        w_ends = to_plane(follow(w_middle, kv[1:]), ends)
-        w_middle2 = to_plane(follow(w_pair, kv[1:]), middle)
-        w_ends2 = to_plane(follow(w_pair, kv[1:]), [(1, 3), (2, 0)])
-        second = [w_ends, w_middle2, w_ends2]
+        up = [to_plane(follow(w_middle, kv[1:]), [(2, 3)]), to_plane(follow(w_pair, kv[1:]), [(1, 2)])]
+        up.append(to_plane(follow(w_pair, kv[1:]), [(1, 3)]))
+        down.append(to_plane(follow(w_pair, kv[1:] + down), [(2, 0)]))
+        second = up + down
 
     out = attention(place, queries, grad_out, qo[1:], kv, members, per_head, group_size, window, ())
     n_dq = min(members, 2)
     dq, own, prev = out[:n_dq], out[n_dq], out[n_dq + 1 :]
-    prev = [shift(follow(prev[k], second), -(k + 1)) for k in range(back)]
+    prev = [shift(follow(prev[k], down), -(k + 1)) for k in range(back)]
     if spread:
         other_c = to_member(follow(other, second + [own]), 1)
         pieces = [near, near_c, other, other_c]
     if spread:
-        sides = (w_ends, w_middle, w_middle, w_ends)
-        last = (w_ends2, w_middle2, w_middle2, w_ends2)
+        sides = (down[0], w_middle, w_middle, up[0])
+        last = (down[2], down[1], up[1], up[2])
         projected = project(place, pieces, [[(node_weights,)], [(w_pair,)], [sides], [last]])
         third = [projected]
     summed = combine(place, own, prev, members, tok, third)
     token_parts, kinds = summed[:-2], summed[-2:]
     norm = 1.0 / math.sqrt(n_seq * tok)
-    partial = []
     if spread:
         parts = [kinds[0], to_member(kinds[1], 1), other_head(kinds[0]), other_head_and_member(kinds[1])]
-        partial = [contract(place, layer_slot, projected, parts, norm, n_seq * n_head)]
-    dq = exchange(dq, gate=partial)
-    dkv = exchange(token_parts, gate=partial)
+    dq = exchange(dq, gate=[projected] if spread else ())
+    dkv = exchange(token_parts)
+    if spread:
+        partial = contract(place, layer_slot, projected, parts, norm, n_seq * n_head, [dq[1][0], dkv[1][0]])
     grad_query, grad_keyval = settle(place, dq, dkv, per_head)
     if spread:
-        copies = lax.all_to_all(partial[0], ("seq", "head"), 0, 0, tiled=True)
+        copies = lax.all_to_all(partial, ("seq", "head"), 0, 0, tiled=True)
         scores = jnp.sum(copies, axis=0)[: layer_slot.shape[0], : n_seq * block_width // HD]
         return grad_query, grad_keyval, scores
 

time: 157 us -> 149 us (0.949)
  waiting for transfers between devices: 55.5 us -> 46.7 us
    ppermute x9 -> x12, waiting for transfers between devices: 43.2 us -> 29.3 us  [to_plane(): lax.ppermute(x, 'seq', [(a * members + k, b * members + k) for a, b in pa...]
    ppermute x12, waiting for transfers between devices: 1 us -> 7.08 us  [to_member(): lax.ppermute(x, 'seq', [(s, s - s % members + (s % members ^ r)) for s in...]
    ppermute x9 -> x12, starting transfers between devices: 19 us -> 21.1 us  [to_plane(): lax.ppermute(x, 'seq', [(a * members + k, b * members + k) for a, b in pa...]
    unnamed x40 -> x36, local copies, waits for them, and re-layouts: 7.3 us -> 5.35 us
    slice x2 -> x4, local copies, waits for them, and re-layouts: 0.07 us -> 1.96 us  [exchange(): array[k]]
    ppermute x1, waiting for transfers between devices: 1.8 us -> 0.01 us  [other_head_and_member(): return lax.ppermute(x, ('seq', 'head'), pairs)]
    pallas_call x2 -> x1, Pallas kernels: 3.73 us -> 2.75 us  [join(): pl.pallas_call(kernel, out_shape=jax.ShapeDtypeStruct((len(views),) + arr...]
  transfers between devices with their start and end apart: 25 -> 28, of which waited for: 9 -> 10; matrix products, arithmetic and copies ran while one was open for 3% -> 3% of each run, Pallas kernels for 31% -> 34%
where the time goes in v4:
time: 149 us
  Pallas kernels  52.6 us (35%)
  waiting for transfers between devices  46.7 us (31%)
  starting transfers between devices  37.3 us (25%)
  local copies, waits for them, and re-layouts  7.91 us (5%)
  other arithmetic  2.88 us (2%)
    ppermute x12, waiting for transfers between devices, to_plane(): lax.ppermute(x, 'seq', [(a * members + k, b * members + k) for a, b in pa...  29.3 us
    pallas_call x1, Pallas kernels, attention(): pl.pallas_call(functools.partial(attention_kernel, members, per_head, gro...  28.6 us
    ppermute x12, starting transfers between devices, to_plane(): lax.ppermute(x, 'seq', [(a * members + k, b * members + k) for a, b in pa...  21.1 us
    ppermute x12, starting transfers between devices, to_member(): lax.ppermute(x, 'seq', [(s, s - s % members + (s % members ^ r)) for s in...  7.94 us
    ppermute x12, waiting for transfers between devices, to_member(): lax.ppermute(x, 'seq', [(s, s - s % members + (s % members ^ r)) for s in...  7.08 us
    all_to_all x1, starting transfers between devices, on_device(): copies = lax.all_to_all(partial, ('seq', 'head'), 0, 0, tiled=True)  6.24 us
    pallas_call x1, Pallas kernels, project(): pl.pallas_call(functools.partial(project_kernel, [[len(part) for part in...  6.15 us
    all_to_all x1, waiting for transfers between devices, on_device(): copies = lax.all_to_all(partial, ('seq', 'head'), 0, 0, tiled=True)  5.78 us
  transfers between devices with their start and end apart: 28, of which 10 were waited for; matrix products, arithmetic and copies ran while one was open for 3% of the time, Pallas kernels for 34%

profile of v4, /device:TPU:0, one launch (start us, length us, event | category | flops | bytes accessed | tf_op | source)
XLA Modules:
  0.0 148.5 jit_solution(18422432367981787815)
XLA Ops:
  0.6 3.1 %collective-permute-start.3 = (bf16[4096,128]{1,0:T(8,128)(2,1)}, bf16[4096,128]{1,0:T(8,128)(2,1)S(1)}, u32[]{:S(2)}, u32[]{:S(2)}) collective-permute-start(bf16[4096,128]{1,0:T(8,128)(2,1)} %refs_4_.1), channel_id=1, source_target_pairs={{0,8},{2,10},{4,12},{6,14},{8,0},{10,2},{12,4},{14,6},{16,24},{18,... | collective-permute-start | bytes 3145736 | tf_op jit(solution)/shard_map/ppermute | solution.py:430
  5.0 1.7 %pack_keys.1 = (bf16[2,144,256]{2,1,0:T(8,128)(2,1)}, bf16[2,144,256]{2,1,0:T(8,128)(2,1)}) custom-call(s32[3]{0:T(128)} %pad_add_fusion.place_ref.refs_0_, s32[1,128]{1,0:T(1,128)} %bitcast.9, bf16[128,1024]{1,0:T(8,128)(2,1)} %kv_ref.1), custom_call_target="tpu_custom_call" | custom-call | tf_op jit(solution)/shard_map/pack_keys/pallas_call | solution.py:62
  6.8 1.5 %collective-permute-start = (bf16[2,144,256]{2,1,0:T(8,128)(2,1)}, bf16[2,144,256]{2,1,0:T(8,128)(2,1)S(1)}, u32[]{:S(2)}, u32[]{:S(2)}) collective-permute-start(bf16[2,144,256]{2,1,0:T(8,128)(2,1)} %get-tuple-element.33), channel_id=1, source_target_pairs={{0,4},{2,6},{4,0},{6,2},{8,12},{10,14},{12,8},{14,10},{16,20},{18,... | collective-permute-start | bytes 442376 | tf_op jit(solution)/shard_map/ppermute | solution.py:427
  8.3 3.0 %split_deltas.1 = (bf16[128,4096]{1,0:T(8,128)(2,1)}, bf16[128,4096]{1,0:T(8,128)(2,1)}) custom-call(s32[3]{0:T(128)} %pad_add_fusion.place_ref.refs_0_, bf16[128,8192]{1,0:T(8,128)(2,1)} %bitcast.7), custom_call_target="tpu_custom_call" | custom-call | tf_op jit(solution)/shard_map/split_deltas/pallas_call | solution.py:117
  11.3 1.5 %collective-permute-start.9 = (bf16[128,4096]{1,0:T(8,128)(2,1)}, bf16[128,4096]{1,0:T(8,128)(2,1)}, u32[]{:S(2)}, u32[]{:S(2)}) collective-permute-start(bf16[128,4096]{1,0:T(8,128)(2,1)} %get-tuple-element.40), channel_id=1, source_target_pairs={{0,1},{1,0},{2,3},{3,2},{4,5},{5,4},{6,7},{7,6},{8,9},{9,8},{10,11... | collective-permute-start | bytes 3145736 | tf_op jit(solution)/shard_map/ppermute | solution.py:438
  13.5 3.1 %pack_queries.1 = (bf16[2,256,1024]{2,1,0:T(8,128)(2,1)}, bf16[2,256,1024]{2,1,0:T(8,128)(2,1)}) custom-call(s32[3]{0:T(128)} %pad_add_fusion.place_ref.refs_0_, bf16[128,4096]{1,0:T(8,128)(2,1)} %refs_1_.1, bf16[128,4096]{1,0:T(8,128)(2,1)} %refs_2_.1), custom_call_target="tpu_custom_call" | custom-call | tf_op jit(solution)/shard_map/pack_queries/pallas_call | solution.py:84
  18.7 8.3 %collective-permute-done.3.refs_5_ = bf16[4096,128]{1,0:T(8,128)(2,1)S(1)} collective-permute-done((bf16[4096,128]{1,0:T(8,128)(2,1)}, bf16[4096,128]{1,0:T(8,128)(2,1)S(1)}, u32[]{:S(2)}, u32[]{:S(2)}) %collective-permute-start.3) | collective-permute-done | bytes 1048608 | tf_op jit(solution)/shard_map/ppermute | solution.py:430
  27.1 7.8 %collective-permute-start.6 = (bf16[4,144,256]{2,1,0:T(8,128)(2,1)S(1)}, bf16[4,144,256]{2,1,0:T(8,128)(2,1)S(1)}, u32[]{:S(2)}, u32[]{:S(2)}) collective-permute-start(bf16[4,144,256]{2,1,0:T(8,128)(2,1)S(1)} %pad_maximum_fusion.2.refs_6_), channel_id=1, source_target_pairs={{0,16},{2,18},{4,20},{6,22},{8,24},{10,26},{12,28},{14,30},{1,17},... | collective-permute-start | bytes 884744 | tf_op jit(solution)/shard_map/ppermute | solution.py:430
  36.3 1.4 pad_maximum_fusion.refs_0_
  39.9 2.4 %collective-permute-done.2.refs_4_ = bf16[2,256,1024]{2,1,0:T(8,128)(2,1)S(1)} collective-permute-done((bf16[2,256,1024]{2,1,0:T(8,128)(2,1)}, bf16[2,256,1024]{2,1,0:T(8,128)(2,1)S(1)}, u32[]{:S(2)}, u32[]{:S(2)}) %collective-permute-start.2) | collective-permute-done | bytes 1048608 | tf_op jit(solution)/shard_map/ppermute | solution.py:427
  42.5 3.9 %collective-permute-done.5.refs_7_ = bf16[4,144,256]{2,1,0:T(8,128)(2,1)S(1)} collective-permute-done((bf16[4,144,256]{2,1,0:T(8,128)(2,1)S(1)}, bf16[4,144,256]{2,1,0:T(8,128)(2,1)S(1)}, u32[]{:S(2)}, u32[]{:S(2)}) %collective-permute-start.5) | collective-permute-done | bytes 294944 | tf_op jit(solution)/shard_map/ppermute | solution.py:430
  46.5 1.5 %collective-permute-start.11 = (bf16[2,128,4096]{2,1,0:T(8,128)(2,1)S(1)}, bf16[2,128,4096]{2,1,0:T(8,128)(2,1)S(1)}, u32[]{:S(2)}, u32[]{:S(2)}) collective-permute-start(bf16[2,128,4096]{2,1,0:T(8,128)(2,1)S(1)} %pad_maximum_fusion.refs_0_), channel_id=1, source_target_pairs={{0,4},{2,6},{4,0},{6,2},{8,12},{10,14},{12,8},{14,10},{16,20},{18,... | collective-permute-start | bytes 6291464 | tf_op jit(solution)/shard_map/ppermute | solution.py:427
  49.4 16.1 %collective-permute-done.15.refs_6_ = bf16[4096,128]{1,0:T(8,128)(2,1)S(1)} collective-permute-done((bf16[4096,128]{1,0:T(8,128)(2,1)S(1)}, bf16[4096,128]{1,0:T(8,128)(2,1)S(1)}, u32[]{:S(2)}, u32[]{:S(2)}) %collective-permute-start.15) | collective-permute-done | bytes 1048608 | tf_op jit(solution)/shard_map/ppermute | solution.py:430
  67.7 28.6 %attention_both_ways.1 = (bf16[2,128,1024]{2,1,0:T(8,128)(2,1)S(1)}, bf16[2,128,1024]{2,1,0:T(8,128)(2,1)S(1)}, f32[512,256]{1,0:T(8,128)S(1)}, bf16[512,256]{1,0:T(8,128)(2,1)S(1)}, bf16[512,256]{1,0:T(8,128)(2,1)S(1)}) custom-call(s32[3]{0:T(128)S(1)} %copy-done.10, bf16[128,4096]{1,0:T(8,128)(2,1)S(1)} %copy-done.6, bf16[128,4096]{1,0:T(8,128)(2,1)S(1)} %copy-done.7, ...), custom_call_target="tpu_custom_call" | custom-call | flops 1342177280 | bytes 3145728 | tf_op jit(solution)/shard_map/attention_both_ways/pallas_call | solution.py:246
  102.0 3.0 %collective-permute-done.18.refs_3_ = bf16[2,128,4096]{2,1,0:T(8,128)(2,1)S(1)} collective-permute-done((bf16[2,128,4096]{2,1,0:T(8,128)(2,1)S(1)}, bf16[2,128,4096]{2,1,0:T(8,128)(2,1)S(1)}, u32[]{:S(2)}, u32[]{:S(2)}) %collective-permute-start.18) | collective-permute-done | bytes 2097184 | tf_op jit(solution)/shard_map/ppermute | solution.py:427
  105.0 6.2 %project_deltas.1.refs_2_.p_ref = f32[1024,512]{1,0:T(8,128)S(1)} custom-call(s32[3]{0:T(128)S(1)} %copy-done.10, bf16[2,128,4096]{2,1,0:T(8,128)(2,1)S(1)} %pad_maximum_fusion.refs_0_, bf16[2,128,4096]{2,1,0:T(8,128)(2,1)S(1)} %collective-permute-done.10.refs_1_, bf16[2,128,4096]{2,1,0:T(8,128)(2,1)S(1)} %collective-permute-done.11.refs_2_, ...), custom_call_target="tpu_custom_call" | custom-call | flops 4294967296 | bytes 12582912 | tf_op jit(solution)/shard_map/project_deltas/pallas_call | solution.py:362
  113.3 2.8 %join.1 = bf16[2,128,1024]{2,1,0:T(8,128)(2,1)} custom-call(bf16[2,128,1024]{2,1,0:T(8,128)(2,1)} %copy-done.3, bf16[2,128,1024]{2,1,0:T(8,128)(2,1)} %copy-done.13, f32[1024,512]{1,0:T(8,128)} %copy-done), custom_call_target="tpu_custom_call" | custom-call | tf_op jit(solution)/shard_map/join/pallas_call | solution.py:100
  117.7 2.9 %sum_key_value_gradients.1 = (bf16[2,128,256]{2,1,0:T(8,128)(2,1)}, bf16[2,128,256]{2,1,0:T(8,128)(2,1)}, bf16[512,128]{1,0:T(8,128)(2,1)}, bf16[512,128]{1,0:T(8,128)(2,1)}) custom-call(s32[3]{0:T(128)} %pad_add_fusion.place_ref.refs_0_, f32[512,256]{1,0:T(8,128)} %copy-done.8, bf16[512,256]{1,0:T(8,128)(2,1)} %collective-permute-done.20.refs_0_, ...), custom_call_target="tpu_custom_call" | custom-call | tf_op jit(solution)/shard_map/sum_key_value_gradients/pallas_call | solution.py:299
  121.7 1.6 %collective-permute-start.24 = (bf16[512,128]{1,0:T(8,128)(2,1)}, bf16[512,128]{1,0:T(8,128)(2,1)S(1)}, u32[]{:S(2)}, u32[]{:S(2)}) collective-permute-start(bf16[512,128]{1,0:T(8,128)(2,1)} %get-tuple-element.56), channel_id=1, source_target_pairs={{0,2},{2,0},{4,6},{6,4},{8,10},{10,8},{12,14},{14,12},{16,18},{18,... | collective-permute-start | bytes 393224 | tf_op jit(solution)/shard_map/ppermute | solution.py:427
  125.9 4.6 %collective-permute-done.25.g2 = bf16[512,128]{1,0:T(8,128)(2,1)S(1)} collective-permute-done((bf16[512,128]{1,0:T(8,128)(2,1)}, bf16[512,128]{1,0:T(8,128)(2,1)S(1)}, u32[]{:S(2)}, u32[]{:S(2)}) %collective-permute-start.25) | collective-permute-done | bytes 131104 | tf_op jit(solution)/shard_map/ppermute | solution.py:438
  131.5 1.6 %contract_scores.1 = f32[32,8,128]{2,1,0:T(8,128)} custom-call(s32[3]{0:T(128)S(1)} %copy-done.11, s32[2]{0:T(128)S(1)} %copy-done.12, f32[1024,512]{1,0:T(8,128)S(1)} %copy-done.1, bf16[512,128]{1,0:T(8,128)(2,1)S(1)} %copy-done.9, bf16[512,128]{1,0:T(8,128)(2,1)S(1)} %collective-permute-done.24.g1, bf16[512,128]{1,0:T(8,128)(2,1)S(1)} %collective-permute-done.25.g2, ...), custom_call_target="tpu_custom_call" | custom-call | tf_op jit(solution)/shard_map/contract_scores/pallas_call | solution.py:402
  133.0 6.2 %all-to-all-start = ((f32[32,8,128]{2,1,0:T(8,128)}), f32[32,8,128]{2,1,0:T(8,128)S(1)}, u32[]{:S(2)}, u32[]{:S(2)}) async-start(f32[32,8,128]{2,1,0:T(8,128)} %contract_scores.1), calls=%async_computation | async-start | bytes 262144 | tf_op jit(solution)/shard_map/all_to_all | solution.py:512
  139.3 2.8 %place_heads.1 = (bf16[128,4096]{1,0:T(8,128)(2,1)}, bf16[128,1024]{1,0:T(8,128)(2,1)}) custom-call(s32[3]{0:T(128)} %pad_add_fusion.place_ref.refs_0_, bf16[2,128,1024]{2,1,0:T(8,128)(2,1)} %copy-done.3, bf16[2,128,1024]{2,1,0:T(8,128)(2,1)} %copy-done.2, bf16[2,128,1024]{2,1,0:T(8,128)(2,1)} %copy-done.13, bf16[2,128,1024]{2,1,0:T(8,128)(2,1)} %copy-done.2, ...), custom_call_target="tpu_custom_call" | custom-call | tf_op jit(solution)/shard_map/place_heads/pallas_call | solution.py:322
  142.1 5.8 %all-to-all-done = f32[32,8,128]{2,1,0:T(8,128)S(1)} async-done(((f32[32,8,128]{2,1,0:T(8,128)}), f32[32,8,128]{2,1,0:T(8,128)S(1)}, u32[]{:S(2)}, u32[]{:S(2)}) %all-to-all-start) | async-done | bytes 131104 | tf_op jit(solution)/shard_map/all_to_all | solution.py:512
  (92 shorter events, 25.9 us)
Async XLA Ops:
  0.6 26.5 %collective-permute-start.3 = (bf16[4096,128]{1,0:T(8,128)(2,1)}, bf16[4096,128]{1,0:T(8,128)(2,1)S(1)}, u32[]{:S(2)}, u32[]{:S(2)}) collective-permute-start(bf16[4096,128]{1,0:T(8,128)(2,1)} %refs_4_.1), channel_id=1, source_target_pairs={{0,8},{2,10},{4,12},{6,14},{8,0},{10,2},{12,4},{14,6},{16,24},{18,... | collective-permute-start | bytes 3145736 | tf_op jit(solution)/shard_map/ppermute | solution.py:430
  3.7 23.4 %collective-permute-start.4 = (bf16[4096,128]{1,0:T(8,128)(2,1)}, bf16[4096,128]{1,0:T(8,128)(2,1)S(1)}, u32[]{:S(2)}, u32[]{:S(2)}) collective-permute-start(bf16[4096,128]{1,0:T(8,128)(2,1)} %refs_4_.1), channel_id=1, source_target_pairs={{8,16},{10,18},{12,20},{14,22},{16,8},{18,10},{20,12},{22,14},{9,1... | collective-permute-start | bytes 3145736 | tf_op jit(solution)/shard_map/ppermute | solution.py:430
  6.8 6.1 %collective-permute-start = (bf16[2,144,256]{2,1,0:T(8,128)(2,1)}, bf16[2,144,256]{2,1,0:T(8,128)(2,1)S(1)}, u32[]{:S(2)}, u32[]{:S(2)}) collective-permute-start(bf16[2,144,256]{2,1,0:T(8,128)(2,1)} %get-tuple-element.33), channel_id=1, source_target_pairs={{0,4},{2,6},{4,0},{6,2},{8,12},{10,14},{12,8},{14,10},{16,20},{18,... | collective-permute-start | bytes 442376 | tf_op jit(solution)/shard_map/ppermute | solution.py:427
  11.3 24.9 %collective-permute-start.9 = (bf16[128,4096]{1,0:T(8,128)(2,1)}, bf16[128,4096]{1,0:T(8,128)(2,1)}, u32[]{:S(2)}, u32[]{:S(2)}) collective-permute-start(bf16[128,4096]{1,0:T(8,128)(2,1)} %get-tuple-element.40), channel_id=1, source_target_pairs={{0,1},{1,0},{2,3},{3,2},{4,5},{5,4},{6,7},{7,6},{8,9},{9,8},{10,11... | collective-permute-start | bytes 3145736 | tf_op jit(solution)/shard_map/ppermute | solution.py:438
  16.6 25.7 %collective-permute-start.2 = (bf16[2,256,1024]{2,1,0:T(8,128)(2,1)}, bf16[2,256,1024]{2,1,0:T(8,128)(2,1)S(1)}, u32[]{:S(2)}, u32[]{:S(2)}) collective-permute-start(bf16[2,256,1024]{2,1,0:T(8,128)(2,1)} %get-tuple-element.34), channel_id=1, source_target_pairs={{0,4},{2,6},{4,0},{6,2},{8,12},{10,14},{12,8},{14,10},{16,20},{18,... | collective-permute-start | bytes 3145736 | tf_op jit(solution)/shard_map/ppermute | solution.py:427
  27.1 15.4 %collective-permute-start.6 = (bf16[4,144,256]{2,1,0:T(8,128)(2,1)S(1)}, bf16[4,144,256]{2,1,0:T(8,128)(2,1)S(1)}, u32[]{:S(2)}, u32[]{:S(2)}) collective-permute-start(bf16[4,144,256]{2,1,0:T(8,128)(2,1)S(1)} %pad_maximum_fusion.2.refs_6_), channel_id=1, source_target_pairs={{0,16},{2,18},{4,20},{6,22},{8,24},{10,26},{12,28},{14,30},{1,17},... | collective-permute-start | bytes 884744 | tf_op jit(solution)/shard_map/ppermute | solution.py:430
  34.9 11.5 %collective-permute-start.5 = (bf16[4,144,256]{2,1,0:T(8,128)(2,1)S(1)}, bf16[4,144,256]{2,1,0:T(8,128)(2,1)S(1)}, u32[]{:S(2)}, u32[]{:S(2)}) collective-permute-start(bf16[4,144,256]{2,1,0:T(8,128)(2,1)S(1)} %pad_maximum_fusion.2.refs_6_), channel_id=1, source_target_pairs={{0,8},{2,10},{4,12},{6,14},{8,16},{10,18},{12,20},{14,22},{16,24},... | collective-permute-start | bytes 884744 | tf_op jit(solution)/shard_map/ppermute | solution.py:430
  37.7 11.0 %collective-permute-start.16 = (bf16[4096,128]{1,0:T(8,128)(2,1)S(1)}, bf16[4096,128]{1,0:T(8,128)(2,1)S(1)}, u32[]{:S(2)}, u32[]{:S(2)}) collective-permute-start(bf16[4096,128]{1,0:T(8,128)(2,1)S(1)} %collective-permute-done.3.refs_5_), channel_id=1, source_target_pairs={{16,8},{18,10},{20,12},{22,14},{17,9},{19,11},{21,13},{23,15}} | collective-permute-start | bytes 3145736 | tf_op jit(solution)/shard_map/ppermute | solution.py:430
  38.6 27.0 %collective-permute-start.15 = (bf16[4096,128]{1,0:T(8,128)(2,1)S(1)}, bf16[4096,128]{1,0:T(8,128)(2,1)S(1)}, u32[]{:S(2)}, u32[]{:S(2)}) collective-permute-start(bf16[4096,128]{1,0:T(8,128)(2,1)S(1)} %collective-permute-done.4.refs_7_.refs_8_), channel_id=1, source_target_pairs={{8,0},{10,2},{12,4},{14,6},{9,1},{11,3},{13,5},{15,7}} | collective-permute-start | bytes 3145736 | tf_op jit(solution)/shard_map/ppermute | solution.py:430
  46.5 19.9 %collective-permute-start.7 = (bf16[2,256,1024]{2,1,0:T(8,128)(2,1)S(1)}, bf16[2,256,1024]{2,1,0:T(8,128)(2,1)S(1)}, u32[]{:S(2)}, u32[]{:S(2)}) collective-permute-start(bf16[2,256,1024]{2,1,0:T(8,128)(2,1)S(1)} %pad_maximum_fusion.1), channel_id=1, source_target_pairs={{0,2},{2,0},{4,6},{6,4},{8,10},{10,8},{12,14},{14,12},{16,18},{18,... | collective-permute-start | bytes 3145736 | tf_op jit(solution)/shard_map/ppermute | solution.py:427
  46.5 51.4 %collective-permute-start.11 = (bf16[2,128,4096]{2,1,0:T(8,128)(2,1)S(1)}, bf16[2,128,4096]{2,1,0:T(8,128)(2,1)S(1)}, u32[]{:S(2)}, u32[]{:S(2)}) collective-permute-start(bf16[2,128,4096]{2,1,0:T(8,128)(2,1)S(1)} %pad_maximum_fusion.refs_0_), channel_id=1, source_target_pairs={{0,4},{2,6},{4,0},{6,2},{8,12},{10,14},{12,8},{14,10},{16,20},{18,... | collective-permute-start | bytes 6291464 | tf_op jit(solution)/shard_map/ppermute | solution.py:427
  48.0 49.9 %collective-permute-start.14 = (bf16[4096,128]{1,0:T(8,128)(2,1)S(1)}, bf16[4096,128]{1,0:T(8,128)(2,1)S(1)}, u32[]{:S(2)}, u32[]{:S(2)}) collective-permute-start(bf16[4096,128]{1,0:T(8,128)(2,1)S(1)} %collective-permute-done.3.refs_5_), channel_id=1, source_target_pairs={{8,24},{10,26},{12,28},{14,30},{9,25},{11,27},{13,29},{15,31}} | collective-permute-start | bytes 3145736 | tf_op jit(solution)/shard_map/ppermute | solution.py:430
  48.7 49.1 %collective-permute-start.13 = (bf16[4096,128]{1,0:T(8,128)(2,1)S(1)}, bf16[4096,128]{1,0:T(8,128)(2,1)S(1)}, u32[]{:S(2)}, u32[]{:S(2)}) collective-permute-start(bf16[4096,128]{1,0:T(8,128)(2,1)S(1)} %collective-permute-done.3.refs_5_), channel_id=1, source_target_pairs={{8,16},{10,18},{12,20},{14,22},{9,17},{11,19},{13,21},{15,23}} | collective-permute-start | bytes 3145736 | tf_op jit(solution)/shard_map/ppermute | solution.py:430
  65.6 32.2 %collective-permute-start.12 = (bf16[4096,128]{1,0:T(8,128)(2,1)S(1)}, bf16[4096,128]{1,0:T(8,128)(2,1)S(1)}, u32[]{:S(2)}, u32[]{:S(2)}) collective-permute-start(bf16[4096,128]{1,0:T(8,128)(2,1)S(1)} %collective-permute-done.4.refs_7_.refs_8_), channel_id=1, source_target_pairs={{16,24},{18,26},{20,28},{22,30},{17,25},{19,27},{21,29},{23,31}} | collective-permute-start | bytes 3145736 | tf_op jit(solution)/shard_map/ppermute | solution.py:430
  66.3 31.5 %collective-permute-start.17 = (bf16[4096,128]{1,0:T(8,128)(2,1)S(1)}, bf16[4096,128]{1,0:T(8,128)(2,1)S(1)}, u32[]{:S(2)}, u32[]{:S(2)}) collective-permute-start(bf16[4096,128]{1,0:T(8,128)(2,1)S(1)} %collective-permute-done.3.refs_5_), channel_id=1, source_target_pairs={{16,0},{18,2},{20,4},{22,6},{17,1},{19,3},{21,5},{23,7}} | collective-permute-start | bytes 3145736 | tf_op jit(solution)/shard_map/ppermute | solution.py:430
  97.9 7.1 %collective-permute-start.18 = (bf16[2,128,4096]{2,1,0:T(8,128)(2,1)S(1)}, bf16[2,128,4096]{2,1,0:T(8,128)(2,1)S(1)}, u32[]{:S(2)}, u32[]{:S(2)}) collective-permute-start(bf16[2,128,4096]{2,1,0:T(8,128)(2,1)S(1)} %collective-permute-done.11.refs_2_), channel_id=1, source_target_pairs={{0,2},{2,0},{4,6},{6,4},{8,10},{10,8},{12,14},{14,12},{16,18},{18,... | collective-permute-start | bytes 6291464 | tf_op jit(solution)/shard_map/ppermute | solution.py:427
  98.4 14.1 %collective-permute-start.8 = (bf16[2,128,1024]{2,1,0:T(8,128)(2,1)S(1)}, bf16[2,128,1024]{2,1,0:T(8,128)(2,1)S(1)}, u32[]{:S(2)}, u32[]{:S(2)}) collective-permute-start(bf16[2,128,1024]{2,1,0:T(8,128)(2,1)S(1)} %get-tuple-element.38), channel_id=1, source_target_pairs={{0,4},{2,6},{4,0},{6,2},{8,12},{10,14},{12,8},{14,10},{16,20},{18,... | collective-permute-start | bytes 1572872 | tf_op jit(solution)/shard_map/ppermute | solution.py:427
  98.9 18.1 %collective-permute-start.21 = (bf16[512,256]{1,0:T(8,128)(2,1)S(1)}, bf16[512,256]{1,0:T(8,128)(2,1)S(1)}, u32[]{:S(2)}, u32[]{:S(2)}) collective-permute-start(bf16[512,256]{1,0:T(8,128)(2,1)S(1)} %get-tuple-element.50), channel_id=1, source_target_pairs={{16,0},{18,2},{20,4},{22,6},{24,8},{26,10},{28,12},{30,14},{17,1},... | collective-permute-start | bytes 786440 | tf_op jit(solution)/shard_map/ppermute | solution.py:430
  100.2 16.8 %collective-permute-start.20 = (bf16[512,256]{1,0:T(8,128)(2,1)S(1)}, bf16[512,256]{1,0:T(8,128)(2,1)}, u32[]{:S(2)}, u32[]{:S(2)}) collective-permute-start(bf16[512,256]{1,0:T(8,128)(2,1)S(1)} %get-tuple-element.48), channel_id=1, source_target_pairs={{8,0},{10,2},{12,4},{14,6},{16,8},{18,10},{20,12},{22,14},{24,16},... | collective-permute-start | bytes 786440 | tf_op jit(solution)/shard_map/ppermute | solution.py:430
  116.0 14.5 %collective-permute-start.19 = (bf16[2,128,1024]{2,1,0:T(8,128)(2,1)}, bf16[2,128,1024]{2,1,0:T(8,128)(2,1)S(1)}, u32[]{:S(2)}, u32[]{:S(2)}) collective-permute-start(bf16[2,128,1024]{2,1,0:T(8,128)(2,1)} %join.1), channel_id=1, source_target_pairs={{0,2},{2,0},{4,6},{6,4},{8,10},{10,8},{12,14},{14,12},{16,18},{18,... | collective-permute-start | bytes 1572872 | tf_op jit(solution)/shard_map/ppermute | solution.py:427
  121.7 8.8 %collective-permute-start.26 = (bf16[512,128]{1,0:T(8,128)(2,1)}, bf16[512,128]{1,0:T(8,128)(2,1)S(1)}, u32[]{:S(2)}, u32[]{:S(2)}) collective-permute-start(bf16[512,128]{1,0:T(8,128)(2,1)} %get-tuple-element.56), channel_id=1, source_target_pairs={{0,3},{1,2},{2,1},{3,0},{4,7},{5,6},{6,5},{7,4},{8,11},{9,10},{10,... | collective-permute-start | bytes 393224 | tf_op jit(solution)/shard_map/ppermute | solution.py:442
  121.7 8.8 %collective-permute-start.24 = (bf16[512,128]{1,0:T(8,128)(2,1)}, bf16[512,128]{1,0:T(8,128)(2,1)S(1)}, u32[]{:S(2)}, u32[]{:S(2)}) collective-permute-start(bf16[512,128]{1,0:T(8,128)(2,1)} %get-tuple-element.56), channel_id=1, source_target_pairs={{0,2},{2,0},{4,6},{6,4},{8,10},{10,8},{12,14},{14,12},{16,18},{18,... | collective-permute-start | bytes 393224 | tf_op jit(solution)/shard_map/ppermute | solution.py:427
  124.1 6.4 %collective-permute-start.25 = (bf16[512,128]{1,0:T(8,128)(2,1)}, bf16[512,128]{1,0:T(8,128)(2,1)S(1)}, u32[]{:S(2)}, u32[]{:S(2)}) collective-permute-start(bf16[512,128]{1,0:T(8,128)(2,1)} %get-tuple-element.55.g0), channel_id=1, source_target_pairs={{0,1},{1,0},{2,3},{3,2},{4,5},{5,4},{6,7},{7,6},{8,9},{9,8},{10,11... | collective-permute-start | bytes 393224 | tf_op jit(solution)/shard_map/ppermute | solution.py:438
  133.0 14.9 %all-to-all-start = ((f32[32,8,128]{2,1,0:T(8,128)}), f32[32,8,128]{2,1,0:T(8,128)S(1)}, u32[]{:S(2)}, u32[]{:S(2)}) async-start(f32[32,8,128]{2,1,0:T(8,128)} %contract_scores.1), calls=%async_computation | async-start | bytes 262144 | tf_op jit(solution)/shard_map/all_to_all | solution.py:512
  (22 other events, 277.2 us)
